TPU v7x, 32 devices: a whole 2x2x4 slice. The times are simulated.
32 devices in a mesh: dp: 4 (over z), rep: 2 (over x), sub: 4 (over y, core).
Axes of the slice: x: 2, y: 2, z: 4, core: 2. Of those that a mesh axis runs over, the one named last changes fastest.
Arguments:
- byte_ids: int32 [8192], P(('dp', 'rep', 'sub')), may hold values from 0 to 255
- hash_ids: int32 [8192, 6], P(('dp', 'rep', 'sub')), may hold values from 0 to 62527, as said below
- lengths: int32 [32, 64], P(('dp', 'rep', 'sub')), may hold values from 1 to 64, 256 in all within a row
- byte_table: bfloat16 [256, 1024], replicated, may hold values from -2.390625 to 2.390625
- hash_table: bfloat16 [62528, 1024], P(('dp', 'rep', 'sub')), may hold values from -2.390625 to 2.390625
- norm_attn: float32 [1024], replicated, may hold values from 0.1 to 1.9
- norm_ffn: float32 [1024], replicated, may hold values from 0.1 to 1.9
- norm_cross: float32 [1024], replicated, may hold values from 0.1 to 1.9
- w_query: bfloat16 [1024, 1024], P('dp'), may hold values from -0.1875 to 0.1875
- w_key: bfloat16 [1024, 1024], P('dp'), may hold values from -0.1875 to 0.1875
- w_value: bfloat16 [1024, 1024], P('dp'), may hold values from -0.1875 to 0.1875
- w_out: bfloat16 [1024, 1024], P('dp'), may hold values from -1 to 1
- w_gate: bfloat16 [1024, 2816], P('dp'), may hold values from -0.1875 to 0.1875
- w_up: bfloat16 [1024, 2816], P('dp'), may hold values from -0.1875 to 0.1875
- w_down: bfloat16 [2816, 1024], P('dp'), may hold values from -0.109375 to 0.109375
- c_query: bfloat16 [1024, 1024], P('dp'), may hold values from -0.1875 to 0.1875
- c_key: bfloat16 [1024, 1024], P('dp'), may hold values from -0.1875 to 0.1875
- c_value: bfloat16 [1024, 1024], P('dp'), may hold values from -0.1875 to 0.1875
- c_out: bfloat16 [1024, 1024], P('dp'), may hold values from -0.375 to 0.375
- cot_bytes: bfloat16 [8192, 1024], P(('dp', 'rep', 'sub')), may hold values from -6 to 6
- cot_patches: bfloat16 [2048, 1024], P(('dp', 'rep', 'sub')), may hold values from -6 to 6
Outputs:
- byte_states: bfloat16 [8192, 1024], P(('dp', 'rep', 'sub'))
- patch_states: bfloat16 [2048, 1024], P(('dp', 'rep', 'sub'))
- embed_grad: bfloat16 [8192, 1024], P(('dp', 'rep', 'sub'))
- byte_table_grad: float32 [256, 1024], P(('dp', 'rep', 'sub'))
- hash_table_grad: float32 [62528, 1024], P(('dp', 'rep', 'sub'))
- row_counts: int32 [62528], P(('dp', 'rep', 'sub'))
- norm_attn_grad: float32 [1024], P(('dp', 'rep', 'sub'))
- norm_ffn_grad: float32 [1024], P(('dp', 'rep', 'sub'))
- norm_cross_grad: float32 [1024], P(('dp', 'rep', 'sub'))
- w_query_grad: float32 [1024, 1024], P(('dp', 'rep', 'sub'))
- w_key_grad: float32 [1024, 1024], P(('dp', 'rep', 'sub'))
- w_value_grad: float32 [1024, 1024], P(('dp', 'rep', 'sub'))
- w_out_grad: float32 [1024, 1024], P(('dp', 'rep', 'sub'))
- w_gate_grad: float32 [1024, 2816], P(('dp', 'rep', 'sub'))
- w_up_grad: float32 [1024, 2816], P(('dp', 'rep', 'sub'))
- w_down_grad: float32 [2816, 1024], P(('dp', 'rep', 'sub'))
- c_query_grad: float32 [1024, 1024], P(('dp', 'rep', 'sub'))
- c_key_grad: float32 [1024, 1024], P(('dp', 'rep', 'sub'))
- c_value_grad: float32 [1024, 1024], P(('dp', 'rep', 'sub'))
- c_out_grad: float32 [1024, 1024], P(('dp', 'rep', 'sub'))
Inputs may be any that keep to these rules, and one draw needn't show every extreme that they name: `hash_ids`: of the 1536 ids of one device's bytes, at most 96 fall in the 1954 rows held by any one device (rows d * 1954 onward for device d in the order dp, rep, sub), and in every draw some device's rows receive exactly 96 from every device. Row b holds the lengths of the 64 patches of bytes b * 256 to (b + 1) * 256 - 1, in order; each row sums to 256 and its largest is 64.
All inputs are finite; a program needn't handle non-finite values.
Results may differ from a plain program's by a relative error of at most 0.02.
Values may be sent and summed in bfloat16 or wider, within the bound.
A program may use at most 384 MiB of HBM per device.

v0:
```python
import jax
import jax.numpy as jnp
from jax import lax
from jax.sharding import PartitionSpec as P

HD = 64
WIN = 512
BYTE_VALUES = 256


PRECISE = lax.Precision.HIGHEST
NEG_BIG = -1e30
EPSILON = 1e-06
SCORE_SCALE = 0.125


def passed_along(x, axis, by):
    devices = lax.axis_size(axis)
    pairs = [(i, i + by) for i in range(devices) if 0 <= i + by < devices]
    return lax.ppermute(x, axis, pairs)


def matmul(matrix_a, matrix_b):
    return jnp.dot(matrix_a, matrix_b, preferred_element_type=jnp.float32)


def times_t(matrix_a, matrix_b):
    return lax.dot_general(
        matrix_a, matrix_b, (((1,), (1,)), ((), ())), preferred_element_type=jnp.float32
    )


def t_times(matrix_a, matrix_b):
    return lax.dot_general(
        matrix_a, matrix_b, (((0,), (0,)), ((), ())), preferred_element_type=jnp.float32
    )


def normalize(values, gains):
    inv_rms = lax.rsqrt(jnp.mean(values * values, axis=-1, keepdims=True) + EPSILON)
    normed = values * inv_rms
    return ((normed * gains).astype(jnp.bfloat16), normed, inv_rms)


def norm_back(grad_out, normed, inv_rms, gains):
    grad_gain = jnp.sum(grad_out * normed, axis=0)
    scaled_grad = grad_out * gains
    grad_in = inv_rms * (
        scaled_grad - normed * jnp.mean(scaled_grad * normed, axis=-1, keepdims=True)
    )
    return (grad_in, grad_gain)


def soft_forward(scores, allowed):
    masked = jnp.where(allowed, scores, NEG_BIG)
    row_max = jnp.max(masked, axis=-1, keepdims=True)
    exps = jnp.exp(masked - row_max)
    row_sum = jnp.sum(exps, axis=-1, keepdims=True)
    return (exps / row_sum, row_max + jnp.log(row_sum))


def soft_again(scores, allowed, log_total):
    return jnp.where(allowed, jnp.exp(scores - log_total), 0.0)


def soft_back(probs_full, grad_probs):
    row_total = jnp.sum(probs_full * grad_probs, axis=-1, keepdims=True)
    return (probs_full * (grad_probs - row_total)).astype(jnp.bfloat16)


def window_mask(first_query, first_key, row_count, col_count):
    query_pos = first_query + jnp.arange(row_count, dtype=jnp.int32)
    key_pos = first_key + jnp.arange(col_count, dtype=jnp.int32)
    near = (
        (key_pos[None, :] <= query_pos[:, None])
        & (key_pos[None, :] > query_pos[:, None] - WIN)
        & (key_pos[None, :] >= 0)
    )
    return near[None]


def body(
    byte_ids,
    hash_ids,
    lengths,
    byte_table,
    hash_table,
    norm_attn,
    norm_ffn,
    norm_cross,
    w_query,
    w_key,
    w_value,
    w_out,
    w_gate,
    w_up,
    w_down,
    c_query,
    c_key,
    c_value,
    c_out,
    cot_bytes,
    cot_patches,
):
    dp_count = lax.axis_size("dp")
    rs_count = lax.axis_size(("rep", "sub"))
    all_count = dp_count * rs_count
    rank_seq = lax.axis_index(("rep", "sub"))
    rank_table = lax.axis_index("dp") * rs_count + rank_seq
    tokens, gram_count = hash_ids.shape
    rows_dev, model_width = hash_table.shape
    head_count = model_width // HD
    request_count = tokens * gram_count
    slot_count = 2 * request_count // all_count
    flat_ids = hash_ids.reshape(request_count)
    owners = flat_ids // rows_dev
    ordering = jnp.argsort(owners, stable=True)
    owners_sorted = owners[ordering]
    per_owner = jnp.sum(
        (owners[:, None] == jnp.arange(all_count, dtype=jnp.int32)[None, :]).astype(jnp.int32),
        axis=0,
    )
    first_slot = jnp.cumsum(per_owner) - per_owner
    place_sorted = (
        owners_sorted * slot_count
        + jnp.arange(request_count, dtype=jnp.int32)
        - first_slot[owners_sorted]
    )
    placement = jnp.zeros((request_count,), jnp.int32).at[ordering].set(place_sorted)
    requests = jnp.full((all_count * slot_count,), -1, jnp.int32).at[placement].set(flat_ids)
    requests = requests.reshape(dp_count, rs_count, slot_count)
    incoming = lax.all_to_all(
        lax.all_to_all(requests, "dp", split_axis=0, concat_axis=0, tiled=True),
        ("rep", "sub"),
        split_axis=1,
        concat_axis=1,
        tiled=True,
    )
    present = incoming >= 0
    safe_rows = jnp.where(present, incoming - rank_table * rows_dev, 0)
    served = jnp.where(present[..., None], hash_table[safe_rows], jnp.zeros((), jnp.bfloat16))
    returned = lax.all_to_all(
        lax.all_to_all(served, "dp", split_axis=0, concat_axis=0, tiled=True),
        ("rep", "sub"),
        split_axis=1,
        concat_axis=1,
        tiled=True,
    )
    fetched = returned.reshape(all_count * slot_count, model_width)[placement]
    fetched = fetched.astype(jnp.float32).reshape(tokens, gram_count, model_width)
    one_hot = byte_ids[:, None] == jnp.arange(BYTE_VALUES, dtype=jnp.int32)[None, :]
    embedded = matmul(one_hot.astype(jnp.bfloat16), byte_table) + jnp.sum(fetched, axis=1)
    row_counts = (
        jnp.zeros((rows_dev,), jnp.int32)
        .at[safe_rows.reshape(-1)]
        .add(present.reshape(-1).astype(jnp.int32))
    )
    weight_list = (
        w_query,
        w_key,
        w_value,
        w_out,
        w_gate,
        w_up,
        w_down,
        c_query,
        c_key,
        c_value,
        c_out,
    )
    gathered = (
        lax.all_gather(weight_list[0], "dp", axis=0, tiled=True),
        lax.all_gather(weight_list[1], "dp", axis=0, tiled=True),
        lax.all_gather(weight_list[2], "dp", axis=0, tiled=True),
        lax.all_gather(weight_list[3], "dp", axis=0, tiled=True),
        lax.all_gather(weight_list[4], "dp", axis=0, tiled=True),
        lax.all_gather(weight_list[5], "dp", axis=0, tiled=True),
        lax.all_gather(weight_list[6], "dp", axis=0, tiled=True),
        lax.all_gather(weight_list[7], "dp", axis=0, tiled=True),
        lax.all_gather(weight_list[8], "dp", axis=0, tiled=True),
        lax.all_gather(weight_list[9], "dp", axis=0, tiled=True),
        lax.all_gather(weight_list[10], "dp", axis=0, tiled=True),
    )
    (
        full_query,
        full_key,
        full_value,
        full_out,
        full_gate,
        full_up,
        full_down,
        full_cquery,
        full_ckey,
        full_cvalue,
        full_cout,
    ) = gathered
    x_attn, normed_attn, scale_attn = normalize(embedded, norm_attn)
    queries = matmul(x_attn, full_query).astype(jnp.bfloat16).reshape(tokens, head_count, HD)
    key_rows = matmul(x_attn, full_key).astype(jnp.bfloat16).reshape(tokens, head_count, HD)
    value_rows = matmul(x_attn, full_value).astype(jnp.bfloat16).reshape(tokens, head_count, HD)
    behind = (WIN - 2) // tokens + 1
    key_parts = []
    value_parts = []
    for offset_back in range(behind, 0, -1):
        far_keys, far_values = passed_along((key_rows, value_rows), ("rep", "sub"), offset_back)
        key_parts.append(far_keys)
        value_parts.append(far_values)
    all_keys = jnp.concatenate(key_parts + [key_rows], axis=0)
    all_values = jnp.concatenate(value_parts + [value_rows], axis=0)
    q_rows = min(tokens, 512)
    key_span = (WIN - 1 + q_rows - 1) // q_rows * q_rows
    base_key = (rank_seq - behind) * tokens
    block_index = 0
    q_start = block_index * q_rows
    k_start = behind * tokens + q_start - key_span
    allowed = window_mask(
        rank_seq * tokens + q_start, base_key + k_start, q_rows, q_rows + key_span
    )
    scores = (
        jnp.einsum("qhd,khd->hqk", queries, all_keys, preferred_element_type=jnp.float32)
        * SCORE_SCALE
    )
    prob_block, log_total = soft_forward(scores, allowed)
    attended_parts = jnp.einsum(
        "hqk,khd->qhd",
        prob_block.astype(jnp.bfloat16),
        all_values,
        preferred_element_type=jnp.float32,
    )
    lse_parts = [log_total]
    attended = attended_parts.astype(jnp.bfloat16).reshape(tokens, model_width)
    h_mid = embedded + matmul(attended, full_out)
    x_ffn, normed_ffn, scale_ffn = normalize(h_mid, norm_ffn)
    gate_pre = matmul(x_ffn, full_gate)
    up_pre = matmul(x_ffn, full_up)
    gate_sig = jax.nn.sigmoid(gate_pre)
    silu_val = gate_pre * gate_sig
    hidden = (silu_val * up_pre).astype(jnp.bfloat16)
    h_out = h_mid + matmul(hidden, full_down)
    byte_states = h_out.astype(jnp.bfloat16)
    x_cross, normed_cross, scale_cross = normalize(h_out, norm_cross)
    patch_len = lengths[0]
    patch_count = patch_len.shape[0]
    patch_end = jnp.cumsum(patch_len)
    patch_start = patch_end - patch_len
    byte_pos = jnp.arange(tokens, dtype=jnp.int32)
    member = (byte_pos[None, :] >= patch_start[:, None]) & (byte_pos[None, :] < patch_end[:, None])
    length_f = patch_len.astype(jnp.float32)[:, None]
    pooled = matmul(member.astype(jnp.bfloat16), x_cross) / length_f
    pooled_low = pooled.astype(jnp.bfloat16)
    p_query = (
        matmul(pooled_low, full_cquery).astype(jnp.bfloat16).reshape(patch_count, head_count, HD)
    )
    p_key = matmul(x_cross, full_ckey).astype(jnp.bfloat16).reshape(tokens, head_count, HD)
    p_value = matmul(x_cross, full_cvalue).astype(jnp.bfloat16).reshape(tokens, head_count, HD)
    cross_scores = (
        jnp.einsum("phd,thd->hpt", p_query, p_key, preferred_element_type=jnp.float32) * SCORE_SCALE
    )
    cross_prob, cross_lse = soft_forward(cross_scores, member[None])
    p_attended = (
        jnp.einsum(
            "hpt,thd->phd",
            cross_prob.astype(jnp.bfloat16),
            p_value,
            preferred_element_type=jnp.float32,
        )
        .astype(jnp.bfloat16)
        .reshape(patch_count, model_width)
    )
    patch_states = (pooled + matmul(p_attended, full_cout)).astype(jnp.bfloat16)
    grad_c_out = t_times(p_attended, cot_patches)
    grad_patt = (
        times_t(cot_patches, full_cout).astype(jnp.bfloat16).reshape(patch_count, head_count, HD)
    )
    cross_again = (
        jnp.einsum("phd,thd->hpt", p_query, p_key, preferred_element_type=jnp.float32) * SCORE_SCALE
    )
    cross_full = soft_again(cross_again, member[None], cross_lse)
    grad_cprob = jnp.einsum("phd,thd->hpt", grad_patt, p_value, preferred_element_type=jnp.float32)
    grad_cscore = soft_back(cross_full, grad_cprob)
    grad_pquery = (
        (
            jnp.einsum("hpt,thd->phd", grad_cscore, p_key, preferred_element_type=jnp.float32)
            * SCORE_SCALE
        )
        .astype(jnp.bfloat16)
        .reshape(patch_count, model_width)
    )
    grad_pkey = (
        (
            jnp.einsum("hpt,phd->thd", grad_cscore, p_query, preferred_element_type=jnp.float32)
            * SCORE_SCALE
        )
        .astype(jnp.bfloat16)
        .reshape(tokens, model_width)
    )
    grad_pvalue = (
        jnp.einsum(
            "hpt,phd->thd",
            cross_full.astype(jnp.bfloat16),
            grad_patt,
            preferred_element_type=jnp.float32,
        )
        .astype(jnp.bfloat16)
        .reshape(tokens, model_width)
    )
    grad_c_query = t_times(pooled_low, grad_pquery)
    grad_c_key = t_times(x_cross, grad_pkey)
    grad_c_value = t_times(x_cross, grad_pvalue)
    grad_pooled = cot_patches.astype(jnp.float32) + times_t(grad_pquery, full_cquery).astype(
        jnp.bfloat16
    ).astype(jnp.float32)
    to_bytes = lax.dot_general(
        member.astype(jnp.float32),
        grad_pooled / length_f,
        (((0,), (0,)), ((), ())),
        precision=PRECISE,
    )
    grad_xcross = (
        times_t(grad_pkey, full_ckey) + times_t(grad_pvalue, full_cvalue) + to_bytes
    ).astype(jnp.bfloat16)
    grad_hout_norm, grad_norm_cross = norm_back(
        grad_xcross.astype(jnp.float32), normed_cross, scale_cross, norm_cross
    )
    grad_hout = cot_bytes.astype(jnp.float32) + grad_hout_norm
    grad_branch_f = grad_hout.astype(jnp.bfloat16)
    grad_w_down = t_times(hidden, grad_branch_f)
    grad_hidden = times_t(grad_branch_f, full_down).astype(jnp.bfloat16).astype(jnp.float32)
    grad_gate = (grad_hidden * up_pre * gate_sig * (1.0 + gate_pre * (1.0 - gate_sig))).astype(
        jnp.bfloat16
    )
    grad_up = (grad_hidden * silu_val).astype(jnp.bfloat16)
    grad_w_gate = t_times(x_ffn, grad_gate)
    grad_w_up = t_times(x_ffn, grad_up)
    grad_xffn = (times_t(grad_gate, full_gate) + times_t(grad_up, full_up)).astype(jnp.bfloat16)
    grad_hmid_norm, grad_norm_ffn = norm_back(
        grad_xffn.astype(jnp.float32), normed_ffn, scale_ffn, norm_ffn
    )
    grad_hmid = grad_hout + grad_hmid_norm
    grad_branch_a = grad_hmid.astype(jnp.bfloat16)
    grad_w_out = t_times(attended, grad_branch_a)
    grad_att = times_t(grad_branch_a, full_out).astype(jnp.bfloat16).reshape(tokens, head_count, HD)
    grad_keys_all = jnp.zeros(((behind + 1) * tokens, head_count, HD), jnp.float32)
    grad_values_all = jnp.zeros(((behind + 1) * tokens, head_count, HD), jnp.float32)
    block_index = 0
    q_start = block_index * q_rows
    k_start = behind * tokens + q_start - key_span
    k_stop = k_start + q_rows + key_span
    allowed = window_mask(
        rank_seq * tokens + q_start, base_key + k_start, q_rows, q_rows + key_span
    )
    scores = (
        jnp.einsum("qhd,khd->hqk", queries, all_keys, preferred_element_type=jnp.float32)
        * SCORE_SCALE
    )
    prob_block = soft_again(scores, allowed, lse_parts[block_index])
    grad_prob = jnp.einsum("qhd,khd->hqk", grad_att, all_values, preferred_element_type=jnp.float32)
    grad_score = soft_back(prob_block, grad_prob)
    grad_q_parts = (
        jnp.einsum("hqk,khd->qhd", grad_score, all_keys, preferred_element_type=jnp.float32)
        * SCORE_SCALE
    )
    grad_keys_all = grad_keys_all.at[k_start:k_stop].add(
        jnp.einsum("hqk,qhd->khd", grad_score, queries, preferred_element_type=jnp.float32)
        * SCORE_SCALE
    )
    grad_values_all = grad_values_all.at[k_start:k_stop].add(
        jnp.einsum(
            "hqk,qhd->khd",
            prob_block.astype(jnp.bfloat16),
            grad_att,
            preferred_element_type=jnp.float32,
        )
    )
    grad_keys = grad_keys_all[behind * tokens :]
    grad_values = grad_values_all[behind * tokens :]
    for offset_back in range(behind, 0, -1):
        part_index = behind - offset_back
        far_grad_k, far_grad_v = (
            passed_along(
                grad_keys_all[part_index * tokens : (part_index + 1) * tokens].astype(jnp.bfloat16),
                ("rep", "sub"),
                -offset_back,
            ).astype(jnp.float32),
            passed_along(
                grad_values_all[part_index * tokens : (part_index + 1) * tokens].astype(
                    jnp.bfloat16
                ),
                ("rep", "sub"),
                -offset_back,
            ).astype(jnp.float32),
        )
        grad_keys = grad_keys + far_grad_k
        grad_values = grad_values + far_grad_v
    grad_queries = grad_q_parts.astype(jnp.bfloat16).reshape(tokens, model_width)
    grad_keys_low = grad_keys.astype(jnp.bfloat16).reshape(tokens, model_width)
    grad_values_low = grad_values.astype(jnp.bfloat16).reshape(tokens, model_width)
    grad_w_query = t_times(x_attn, grad_queries)
    grad_w_key = t_times(x_attn, grad_keys_low)
    grad_w_value = t_times(x_attn, grad_values_low)
    grad_xattn = (
        times_t(grad_queries, full_query)
        + times_t(grad_keys_low, full_key)
        + times_t(grad_values_low, full_value)
    ).astype(jnp.bfloat16)
    grad_embed_norm, grad_norm_attn = norm_back(
        grad_xattn.astype(jnp.float32), normed_attn, scale_attn, norm_attn
    )
    grad_embed = grad_hmid + grad_embed_norm
    embed_grad = grad_embed.astype(jnp.bfloat16)
    grad_byte_table = lax.dot_general(
        one_hot.astype(jnp.float32), grad_embed, (((0,), (0,)), ((), ())), precision=PRECISE
    )
    per_request = jnp.broadcast_to(
        grad_embed[:, None, :], (tokens, gram_count, model_width)
    ).reshape(request_count, model_width)
    outgoing = (
        jnp.zeros((all_count * slot_count, model_width), jnp.float32).at[placement].set(per_request)
    )
    outgoing = outgoing.reshape(dp_count, rs_count, slot_count, model_width)
    arrived = lax.all_to_all(
        lax.all_to_all(
            outgoing.astype(jnp.bfloat16), "dp", split_axis=0, concat_axis=0, tiled=True
        ),
        ("rep", "sub"),
        split_axis=1,
        concat_axis=1,
        tiled=True,
    ).astype(outgoing.dtype)
    hash_table_grad = (
        jnp.zeros((rows_dev, model_width), jnp.float32)
        .at[safe_rows.reshape(-1)]
        .add(jnp.where(present[..., None], arrived, 0.0).reshape(-1, model_width))
    )
    summed_all = (
        lax.psum_scatter(grad_norm_attn, ("dp", "rep", "sub"), scatter_dimension=0, tiled=True),
        lax.psum_scatter(grad_norm_ffn, ("dp", "rep", "sub"), scatter_dimension=0, tiled=True),
        lax.psum_scatter(grad_norm_cross, ("dp", "rep", "sub"), scatter_dimension=0, tiled=True),
        lax.psum_scatter(grad_w_query, ("dp", "rep", "sub"), scatter_dimension=0, tiled=True),
        lax.psum_scatter(grad_w_key, ("dp", "rep", "sub"), scatter_dimension=0, tiled=True),
        lax.psum_scatter(grad_w_value, ("dp", "rep", "sub"), scatter_dimension=0, tiled=True),
        lax.psum_scatter(grad_w_out, ("dp", "rep", "sub"), scatter_dimension=0, tiled=True),
        lax.psum_scatter(grad_w_gate, ("dp", "rep", "sub"), scatter_dimension=0, tiled=True),
        lax.psum_scatter(grad_w_up, ("dp", "rep", "sub"), scatter_dimension=0, tiled=True),
        lax.psum_scatter(grad_w_down, ("dp", "rep", "sub"), scatter_dimension=0, tiled=True),
        lax.psum_scatter(grad_c_query, ("dp", "rep", "sub"), scatter_dimension=0, tiled=True),
        lax.psum_scatter(grad_c_key, ("dp", "rep", "sub"), scatter_dimension=0, tiled=True),
        lax.psum_scatter(grad_c_value, ("dp", "rep", "sub"), scatter_dimension=0, tiled=True),
        lax.psum_scatter(grad_c_out, ("dp", "rep", "sub"), scatter_dimension=0, tiled=True),
        lax.psum_scatter(grad_byte_table, ("dp", "rep", "sub"), scatter_dimension=0, tiled=True),
    )
    (
        out_norm_attn,
        out_norm_ffn,
        out_norm_cross,
        out_query,
        out_key,
        out_value,
        out_proj,
        out_gate,
        out_up,
        out_down,
        out_cquery,
        out_ckey,
        out_cvalue,
        out_cout,
        out_bytes,
    ) = summed_all
    return (
        byte_states,
        patch_states,
        embed_grad,
        out_bytes,
        hash_table_grad,
        row_counts,
        out_norm_attn,
        out_norm_ffn,
        out_norm_cross,
        out_query,
        out_key,
        out_value,
        out_proj,
        out_gate,
        out_up,
        out_down,
        out_cquery,
        out_ckey,
        out_cvalue,
        out_cout,
    )


def solution(mesh):
    return jax.shard_map(
        body,
        mesh=mesh,
        in_specs=(
            P(("dp", "rep", "sub")),
            P(("dp", "rep", "sub"), None),
            P(("dp", "rep", "sub"), None),
            P(),
            P(("dp", "rep", "sub"), None),
            P(),
            P(),
            P(),
            P("dp", None),
            P("dp", None),
            P("dp", None),
            P("dp", None),
            P("dp", None),
            P("dp", None),
            P("dp", None),
            P("dp", None),
            P("dp", None),
            P("dp", None),
            P("dp", None),
            P(("dp", "rep", "sub"), None),
            P(("dp", "rep", "sub"), None),
        ),
        out_specs=(
            P(("dp", "rep", "sub"), None),
            P(("dp", "rep", "sub"), None),
            P(("dp", "rep", "sub"), None),
            P(("dp", "rep", "sub"), None),
            P(("dp", "rep", "sub"), None),
            P(("dp", "rep", "sub")),
            P(("dp", "rep", "sub")),
            P(("dp", "rep", "sub")),
            P(("dp", "rep", "sub")),
            P(("dp", "rep", "sub"), None),
            P(("dp", "rep", "sub"), None),
            P(("dp", "rep", "sub"), None),
            P(("dp", "rep", "sub"), None),
            P(("dp", "rep", "sub"), None),
            P(("dp", "rep", "sub"), None),
            P(("dp", "rep", "sub"), None),
            P(("dp", "rep", "sub"), None),
            P(("dp", "rep", "sub"), None),
            P(("dp", "rep", "sub"), None),
            P(("dp", "rep", "sub"), None),
        ),
        check_vma=False,
    )
```

profile of v0, /device:TPU:0, one launch (start us, length us, event | category | flops | bytes accessed | tf_op | source)
XLA Modules:
  0.0 2657.3 jit_solution(17379161900394877637)
XLA Ops:
  19.8 8.4 gather_fusion
  33.2 16.0 select_subtract_fusion
  61.7 12.0 all_to_all.30
  84.0 18.5 gather_fusion.1
  115.1 221.9 %all-to-all-done.2 = bf16[4,8,96,1024]{3,2,1,0:T(8,128)(2,1)} async-done(((bf16[4,8,96,1024]{3,2,1,0:T(8,128)(2,1)}), bf16[4,8,96,1024]{3,2,1,0:T(8,128)(2,1)}, u32[]{:S(2)}, u32[]{:S(2)}) %all-to-all-start.2) | async-done | bytes 6291488 | tf_op jit(solution)/shard_map/all_to_all | solution.py:143
  354.6 64.6 %all-to-all-done.3 = bf16[4,8,96,1024]{3,2,0,1:T(8,128)(2,1)} async-done(((bf16[4,8,96,1024]{3,2,0,1:T(8,128)(2,1)}), bf16[4,8,96,1024]{3,2,0,1:T(8,128)(2,1)}, u32[]{:S(2)}, u32[]{:S(2)}) %all-to-all-start.3) | async-done | bytes 6291488 | tf_op jit(solution)/shard_map/all_to_all | solution.py:142
  425.8 11.4 gather_fusion.2
  496.5 70.3 %all-gather.22.cloned.1.call-done = bf16[1024,2816]{1,0:T(8,128)(2,1)} async-done(((bf16[256,2816]{1,0:T(8,128)(2,1)}), bf16[1024,2816]{1,0:T(8,128)(2,1)}) %all-gather.22.cloned.1.call-update) | async-done | bytes 5767184 | tf_op jit(solution)/shard_map/all_gather | solution.py:177
  574.0 99.4 %all-gather.24.cloned.1.call-done = bf16[2816,1024]{1,0:T(8,128)(2,1)} async-done(((bf16[704,1024]{1,0:T(8,128)(2,1)}), bf16[2816,1024]{1,0:T(8,128)(2,1)}) %all-gather.24.cloned.1.call-update) | async-done | bytes 5767184 | tf_op jit(solution)/shard_map/all_gather | solution.py:178
  679.7 39.5 %all-gather.28.cloned.1.call-done = bf16[1024,1024]{1,0:T(8,128)(2,1)} async-done(((bf16[256,1024]{1,0:T(8,128)(2,1)}), bf16[1024,1024]{1,0:T(8,128)(2,1)}) %all-gather.28.cloned.1.call-update) | async-done | bytes 2097168 | tf_op jit(solution)/shard_map/all_gather | solution.py:179
  722.2 43.2 %all-gather.30.cloned.1.call-done = bf16[1024,1024]{1,0:T(8,128)(2,1)} async-done(((bf16[256,1024]{1,0:T(8,128)(2,1)}), bf16[1024,1024]{1,0:T(8,128)(2,1)}) %all-gather.30.cloned.1.call-update) | async-done | bytes 2097168 | tf_op jit(solution)/shard_map/all_gather | solution.py:180
  769.7 41.9 %all-gather.26.cloned.1.call-done = bf16[1024,1024]{1,0:T(8,128)(2,1)} async-done(((bf16[256,1024]{1,0:T(8,128)(2,1)}), bf16[1024,1024]{1,0:T(8,128)(2,1)}) %all-gather.26.cloned.1.call-update) | async-done | bytes 2097168 | tf_op jit(solution)/shard_map/all_gather | solution.py:181
  852.3 10.4 multiply_reduce_fusion
  878.2 11.0 collective-permute-done.4
  955.9 8.3 reshape.601
  964.2 13.2 scatter_custom_fusion.2
  977.4 8.3 convert_element_type.268
  985.7 158.0 %all_to_all.31 = bf16[4,8,96,1024]{3,2,1,0:T(8,128)(2,1)S(1)} all-to-all(bf16[4,8,96,1024]{3,2,1,0:T(8,128)(2,1)} %bitcast.160), channel_id=1, replica_groups=mesh['dp'=4,'rep'=2,'sub'=4] {'dp'}, dimensions={0} | all-to-all | bytes 12582912 | tf_op jit(solution)/shard_map/all_to_all | solution.py:422
  1152.3 17.3 scatter_custom_fusion.4
  1170.7 103.2 %all-reduce.3 = (f32[1024]{0:T(1024)S(1)}, f32[1024]{0:T(1024)S(1)}, f32[1024]{0:T(1024)S(1)}) all-reduce(f32[1024]{0:T(1024)S(1)} %get-tuple-element.66, f32[1024]{0:T(1024)S(1)} %copy-done.77, f32[1024]{0:T(1024)S(1)} %get-tuple-element.62), channel_id=3, replica_groups=mesh['dp'=4,'rep'=2,'sub'=4] {'dp','rep','sub'}, use_global_device_ids=true, to_apply=%region_24.25.clone | all-reduce | flops 3072 | bytes 24576
  1275.7 7.7 convert_select_fusion
  1283.4 31.4 %scatter_custom_fusion.3 = f32[1954,1024]{1,0:T(8,128)} fusion(s32[3072]{0:T(1024)S(1)} %bitcast.200, f32[3072,1024]{1,0:T(8,128)} %bitcast.162, f32[]{:T(128)} %constant.143.clone.1), kind=kCustom, calls=%fused_computation.26 | custom fusion | flops 3145728 | bytes 8004096 | tf_op jit(solution)/shard_map/scatter-add | solution.py:433
  1314.8 30.9 %reduce-scatter.29.cloned.1.call-done = f32[32,1024]{1,0:T(8,128)} async-done(((f32[1024,1024]{1,0:T(8,128)}), f32[32,1024]{1,0:T(8,128)}) %reduce-scatter.29.cloned.1.call-update) | async-done | bytes 131088 | tf_op jit(solution)/shard_map/reduce_scatter | solution.py:446
  1345.7 139.9 %reduce-scatter.33.cloned.1.call-done = f32[32,1024]{1,0:T(8,128)} async-done(((f32[1024,1024]{1,0:T(8,128)}), f32[32,1024]{1,0:T(8,128)}) %reduce-scatter.33.cloned.1.call-update) | async-done | bytes 131088 | tf_op jit(solution)/shard_map/reduce_scatter | solution.py:448
  1485.5 139.7 %reduce-scatter.31.cloned.1.call-done = f32[32,1024]{1,0:T(8,128)} async-done(((f32[1024,1024]{1,0:T(8,128)}), f32[32,1024]{1,0:T(8,128)}) %reduce-scatter.31.cloned.1.call-update) | async-done | bytes 131088 | tf_op jit(solution)/shard_map/reduce_scatter | solution.py:447
  1625.3 139.8 %reduce-scatter.35.cloned.1.call-done = f32[32,1024]{1,0:T(8,128)} async-done(((f32[1024,1024]{1,0:T(8,128)}), f32[32,1024]{1,0:T(8,128)}) %reduce-scatter.35.cloned.1.call-update) | async-done | bytes 131088 | tf_op jit(solution)/shard_map/reduce_scatter | solution.py:449
  1765.1 139.7 %reduce-scatter.15.cloned.1.call-done = f32[32,1024]{1,0:T(8,128)} async-done(((f32[1024,1024]{1,0:T(8,128)}), f32[32,1024]{1,0:T(8,128)}) %reduce-scatter.15.cloned.1.call-update) | async-done | bytes 131088 | tf_op jit(solution)/shard_map/reduce_scatter | solution.py:439
  1904.8 140.4 %reduce-scatter.19.cloned.1.call-done = f32[32,1024]{1,0:T(8,128)} async-done(((f32[1024,1024]{1,0:T(8,128)}), f32[32,1024]{1,0:T(8,128)}) %reduce-scatter.19.cloned.1.call-update) | async-done | bytes 131088 | tf_op jit(solution)/shard_map/reduce_scatter | solution.py:441
  2045.2 139.8 %reduce-scatter.17.cloned.1.call-done = f32[32,1024]{1,0:T(8,128)} async-done(((f32[1024,1024]{1,0:T(8,128)}), f32[32,1024]{1,0:T(8,128)}) %reduce-scatter.17.cloned.1.call-update) | async-done | bytes 131088 | tf_op jit(solution)/shard_map/reduce_scatter | solution.py:440
  2185.1 153.7 %reduce-scatter.27.cloned.1.call-done = f32[88,1024]{1,0:T(8,128)} async-done(((f32[2816,1024]{1,0:T(8,128)}), f32[88,1024]{1,0:T(8,128)}) %reduce-scatter.27.cloned.1.call-update) | async-done | bytes 360464 | tf_op jit(solution)/shard_map/reduce_scatter | solution.py:445
  2338.8 155.9 %reduce-scatter.25.cloned.1.call-done = f32[32,2816]{1,0:T(8,128)} async-done(((f32[1024,2816]{1,0:T(8,128)}), f32[32,2816]{1,0:T(8,128)}) %reduce-scatter.25.cloned.1.call-update) | async-done | bytes 360464 | tf_op jit(solution)/shard_map/reduce_scatter | solution.py:444
  2494.6 155.9 %reduce-scatter.23.cloned.1.call-done = f32[32,2816]{1,0:T(8,128)} async-done(((f32[1024,2816]{1,0:T(8,128)}), f32[32,2816]{1,0:T(8,128)}) %reduce-scatter.23.cloned.1.call-update) | async-done | bytes 360464 | tf_op jit(solution)/shard_map/reduce_scatter | solution.py:443
  (394 shorter events, 290.2 us)
Async XLA Ops:
  7.2 344.2 %all-gather.32.cloned.1.call-start = ((), (), s32[]{:S(2)}) async-start(), calls=%async_computation.28 | async-start | bytes 2621440 | tf_op jit(solution)/shard_map/all_gather | solution.py:182
  8.0 442.5 %all-gather.16.cloned.1.call-start = ((), (), s32[]{:S(2)}) async-start(), calls=%async_computation.20 | async-start | bytes 2621440 | tf_op jit(solution)/shard_map/all_gather | solution.py:173
  8.7 450.4 %all-gather.12.cloned.1.call-start = ((), (), s32[]{:S(2)}) async-start(), calls=%async_computation.18 | async-start | bytes 2621440 | tf_op jit(solution)/shard_map/all_gather | solution.py:174
  9.4 458.3 %all-gather.14.cloned.1.call-start = ((), (), s32[]{:S(2)}) async-start(), calls=%async_computation.19 | async-start | bytes 2621440 | tf_op jit(solution)/shard_map/all_gather | solution.py:172
  10.0 477.4 %all-gather.18.cloned.1.call-start = ((), (), s32[]{:S(2)}) async-start(), calls=%async_computation.21 | async-start | bytes 2621440 | tf_op jit(solution)/shard_map/all_gather | solution.py:175
  10.6 479.6 %all-gather.20.cloned.1.call-start = ((), (), s32[]{:S(2)}) async-start(), calls=%async_computation.22 | async-start | bytes 7208960 | tf_op jit(solution)/shard_map/all_gather | solution.py:176
  11.2 555.6 %all-gather.22.cloned.1.call-start = ((), (), s32[]{:S(2)}) async-start(), calls=%async_computation.23 | async-start | bytes 7208960 | tf_op jit(solution)/shard_map/all_gather | solution.py:177
  11.9 661.5 %all-gather.24.cloned.1.call-start = ((), (), s32[]{:S(2)}) async-start(), calls=%async_computation.24 | async-start | bytes 7208960 | tf_op jit(solution)/shard_map/all_gather | solution.py:178
  109.1 227.9 %all-to-all-start.2 = ((bf16[4,8,96,1024]{3,2,1,0:T(8,128)(2,1)}), bf16[4,8,96,1024]{3,2,1,0:T(8,128)(2,1)}, u32[]{:S(2)}, u32[]{:S(2)}) async-start(bf16[4,8,96,1024]{3,2,1,0:T(8,128)(2,1)} %broadcast_select_fusion), calls=%async_computation.2 | async-start | bytes 12582912 | tf_op jit(solution)/shard_map/all_to_all | solution.py:143
  114.4 604.9 %all-gather.28.cloned.1.call-start = ((), (), s32[]{:S(2)}) async-start(), calls=%async_computation.26 | async-start | bytes 2621440 | tf_op jit(solution)/shard_map/all_gather | solution.py:179
  343.7 75.5 %all-to-all-start.3 = ((bf16[4,8,96,1024]{3,2,0,1:T(8,128)(2,1)}), bf16[4,8,96,1024]{3,2,0,1:T(8,128)(2,1)}, u32[]{:S(2)}, u32[]{:S(2)}) async-start(bf16[4,8,96,1024]{3,2,0,1:T(8,128)(2,1)} %copy.116), calls=%async_computation.3 | async-start | bytes 12582912 | tf_op jit(solution)/shard_map/all_to_all | solution.py:142
  348.5 416.8 %all-gather.30.cloned.1.call-start = ((), (), s32[]{:S(2)}) async-start(), calls=%async_computation.27 | async-start | bytes 2621440 | tf_op jit(solution)/shard_map/all_gather | solution.py:180
  349.1 462.5 %all-gather.26.cloned.1.call-start = ((), (), s32[]{:S(2)}) async-start(), calls=%async_computation.25 | async-start | bytes 2621440 | tf_op jit(solution)/shard_map/all_gather | solution.py:181
  349.9 964.9 %reduce-scatter.13.cloned.1.call-start = ((), (), s32[]{:S(2)}) async-start(), calls=%async_computation.29 | async-start | bytes 1081344 | tf_op jit(solution)/shard_map/reduce_scatter | solution.py:450
  453.0 19.4 collective-permute-start.3
  455.3 17.1 collective-permute-start.2
  461.6 17.9 collective-permute-start.1
  849.4 40.9 %collective-permute-start.6 = (bf16[256,16,64]{0,2,1:T(8,128)(2,1)}, bf16[256,16,64]{0,2,1:T(8,128)(2,1)}, u32[]{:S(2)}, u32[]{:S(2)}) collective-permute-start(bf16[256,16,64]{0,2,1:T(8,128)(2,1)} %get-tuple-element.106), channel_id=1, source_target_pairs={{2,0},{3,1},{4,2},{5,3},{6,4},{7,5},{10,8},{11,9},{12,10},{13,11},... | collective-permute-start | bytes 1572872 | tf_op jit(solution)/shard_map/ppermute | solution.py:20
  850.7 39.6 %collective-permute-start.7 = (bf16[256,16,64]{0,2,1:T(8,128)(2,1)}, bf16[256,16,64]{0,2,1:T(8,128)(2,1)}, u32[]{:S(2)}, u32[]{:S(2)}) collective-permute-start(bf16[256,16,64]{0,2,1:T(8,128)(2,1)} %get-tuple-element.107), channel_id=1, source_target_pairs={{1,0},{2,1},{3,2},{4,3},{5,4},{6,5},{7,6},{9,8},{10,9},{11,10},{12... | collective-permute-start | bytes 1572872 | tf_op jit(solution)/shard_map/ppermute | solution.py:20
  871.4 17.8 collective-permute-start.4
  897.1 417.6 %reduce-scatter.21.cloned.1.call-start = ((), (), s32[]{:S(2)}) async-start(), calls=%async_computation.33 | async-start | bytes 4325376 | tf_op jit(solution)/shard_map/reduce_scatter | solution.py:442
  900.9 444.7 %reduce-scatter.29.cloned.1.call-start = ((), (), s32[]{:S(2)}) async-start(), calls=%async_computation.37 | async-start | bytes 4325376 | tf_op jit(solution)/shard_map/reduce_scatter | solution.py:446
  904.7 580.8 %reduce-scatter.33.cloned.1.call-start = ((), (), s32[]{:S(2)}) async-start(), calls=%async_computation.39 | async-start | bytes 4325376 | tf_op jit(solution)/shard_map/reduce_scatter | solution.py:448
  908.5 716.8 %reduce-scatter.31.cloned.1.call-start = ((), (), s32[]{:S(2)}) async-start(), calls=%async_computation.38 | async-start | bytes 4325376 | tf_op jit(solution)/shard_map/reduce_scatter | solution.py:447
  912.3 852.8 %reduce-scatter.35.cloned.1.call-start = ((), (), s32[]{:S(2)}) async-start(), calls=%async_computation.40 | async-start | bytes 4325376 | tf_op jit(solution)/shard_map/reduce_scatter | solution.py:449
  916.6 988.3 %reduce-scatter.15.cloned.1.call-start = ((), (), s32[]{:S(2)}) async-start(), calls=%async_computation.30 | async-start | bytes 4325376 | tf_op jit(solution)/shard_map/reduce_scatter | solution.py:439
  920.4 1124.9 %reduce-scatter.19.cloned.1.call-start = ((), (), s32[]{:S(2)}) async-start(), calls=%async_computation.32 | async-start | bytes 4325376 | tf_op jit(solution)/shard_map/reduce_scatter | solution.py:441
  924.3 1260.8 %reduce-scatter.17.cloned.1.call-start = ((), (), s32[]{:S(2)}) async-start(), calls=%async_computation.31 | async-start | bytes 4325376 | tf_op jit(solution)/shard_map/reduce_scatter | solution.py:440
  928.1 1410.7 %reduce-scatter.27.cloned.1.call-start = ((), (), s32[]{:S(2)}) async-start(), calls=%async_computation.36 | async-start | bytes 11894784 | tf_op jit(solution)/shard_map/reduce_scatter | solution.py:445
  935.6 1559.0 %reduce-scatter.25.cloned.1.call-start = ((), (), s32[]{:S(2)}) async-start(), calls=%async_computation.35 | async-start | bytes 11894784 | tf_op jit(solution)/shard_map/reduce_scatter | solution.py:444
  943.2 1707.3 %reduce-scatter.23.cloned.1.call-start = ((), (), s32[]{:S(2)}) async-start(), calls=%async_computation.34 | async-start | bytes 11894784 | tf_op jit(solution)/shard_map/reduce_scatter | solution.py:443
  1147.1 128.6 %all-to-all-start.5 = ((bf16[4,8,96,1024]{3,2,0,1:T(8,128)(2,1)}), bf16[4,8,96,1024]{3,2,0,1:T(8,128)(2,1)}, u32[]{:S(2)}, u32[]{:S(2)}) async-start(bf16[4,8,96,1024]{3,2,0,1:T(8,128)(2,1)} %copy.130), calls=%async_computation.6 | async-start | bytes 12582912 | tf_op jit(solution)/shard_map/all_to_all | solution.py:421
  (95 other events, 3988.5 us)
Sparse Core Ops, SparseCore 0:
  9.6 49.3 all-gather.31
  60.6 45.3 all-gather.15
  107.6 95.0 all-gather.11
  204.1 93.9 all-gather.13
  299.5 55.1 all-gather.17
  356.1 103.9 all-gather.19
  461.7 104.9 all-gather.21
  568.3 104.9 all-gather.23
  675.0 44.2 all-gather.27
  720.7 44.6 all-gather.29
  766.9 44.6 all-gather.25
  897.3 140.9 reduce-scatter.12
  1041.2 159.9 reduce-scatter.20
  1204.0 141.5 reduce-scatter.28
  1348.5 137.0 reduce-scatter.32
  1488.3 136.8 reduce-scatter.30
  1628.1 136.9 reduce-scatter.34
  1767.9 136.8 reduce-scatter.14
  1907.8 137.4 reduce-scatter.18
  2048.0 137.0 reduce-scatter.16
  2188.1 150.6 reduce-scatter.26
  2341.8 152.8 reduce-scatter.24
  2497.6 152.8 reduce-scatter.22
where the time goes:
time: 2670 us; the launch traced here: 2660 us
  waiting for transfers between devices  1940 us (73%)
  blocking collectives  273 us (10%)
  matrix products  136 us (5%)
  local copies, waits for them, and re-layouts  130 us (5%)
  other arithmetic  122 us (5%)
  starting transfers between devices  38.2 us (1%)
    all_to_all x1, waiting for transfers between devices, body(): lax.all_to_all(served, 'dp', split_axis=0, concat_axis=0, tiled=True)  222 us
    all_to_all x1, blocking collectives, body(): lax.all_to_all(outgoing.astype(jnp.bfloat16), 'dp', split_axis=0, concat_...  158 us
    reduce_scatter x1, waiting for transfers between devices, body(): lax.psum_scatter(grad_w_gate, ('dp', 'rep', 'sub'), scatter_dimension=0,...  156 us
    reduce_scatter x1, waiting for transfers between devices, body(): lax.psum_scatter(grad_w_up, ('dp', 'rep', 'sub'), scatter_dimension=0, ti...  156 us
    reduce_scatter x1, waiting for transfers between devices, body(): lax.psum_scatter(grad_w_down, ('dp', 'rep', 'sub'), scatter_dimension=0,...  154 us
    reduce_scatter x1, waiting for transfers between devices, body(): lax.psum_scatter(grad_w_value, ('dp', 'rep', 'sub'), scatter_dimension=0,...  140 us
    reduce_scatter x1, waiting for transfers between devices, body(): lax.psum_scatter(grad_c_value, ('dp', 'rep', 'sub'), scatter_dimension=0,...  140 us
    reduce_scatter x1, waiting for transfers between devices, body(): lax.psum_scatter(grad_w_key, ('dp', 'rep', 'sub'), scatter_dimension=0, t...  140 us
  transfers between devices with their start and end apart: 35, of which 20 were waited for; matrix products, arithmetic and copies ran while one was open for 12% of the time, Pallas kernels for 0%

commit v1 on v0

--- a/solution.py
+++ b/solution.py
@@ -1,6 +1,10 @@
+import functools
+
 import jax
 import jax.numpy as jnp
 from jax import lax
+from jax.experimental import pallas as pl
+from jax.experimental.pallas import tpu as pltpu
 from jax.sharding import PartitionSpec as P
 
 HD = 64
@@ -77,6 +81,748 @@
         & (key_pos[None, :] >= 0)
     )
     return near[None]
+
+
+MESH_ID = pl.DeviceIdType.MESH
+SLOTS = 96
+VMEM_CAP = 60 * 1024 * 1024
+
+
+class Place:
+    def __init__(self, dp_count):
+        self.n = dp_count
+        self.z = lax.axis_index("dp")
+        self.x = lax.axis_index("rep")
+        sub = lax.axis_index("sub")
+        self.y = sub // 2
+        self.c = sub % 2
+        self.started = []
+
+    def at(self, dz=0, dx=0, dy=0, dc=0):
+        z = lax.rem(self.z + dz, self.n) if dz else self.z
+        x = 1 - self.x if dx else self.x
+        y = 1 - self.y if dy else self.y
+        c = 1 - self.c if dc else self.c
+        return (z, x, y * 2 + c)
+
+    def greet(self):
+        barrier = pltpu.get_barrier_semaphore()
+        peers = [self.at(dx=1), self.at(dy=1), self.at(dc=1)]
+        peers += [self.at(dz=j) for j in range(1, self.n)]
+        for peer in peers:
+            pl.semaphore_signal(barrier, inc=1, device_id=peer, device_id_type=MESH_ID)
+        pl.semaphore_wait(barrier, len(peers))
+
+    def send(self, src, dst, send_sem, recv_sem, peer):
+        copy = pltpu.make_async_remote_copy(
+            src_ref=src,
+            dst_ref=dst,
+            send_sem=send_sem,
+            recv_sem=recv_sem,
+            device_id=peer,
+            device_id_type=MESH_ID,
+        )
+        copy.start()
+        self.started.append(copy)
+        return copy
+
+    def expect(self, dst, recv_sem):
+        pltpu.make_async_remote_copy(
+            src_ref=dst,
+            dst_ref=dst,
+            send_sem=recv_sem,
+            recv_sem=recv_sem,
+            device_id=self.at(dc=1),
+            device_id_type=MESH_ID,
+        ).wait_recv()
+
+    def sent(self, copy):
+        copy.wait_send()
+        self.started = [other for other in self.started if other is not copy]
+
+    def finish(self):
+        for copy in self.started:
+            copy.wait_send()
+        self.started = []
+
+
+def add_into(dst, src, blocks, width):
+    def step(i, carry):
+        total = dst(i)[...].astype(jnp.float32) + src(i)[...].astype(jnp.float32)
+        dst(i)[...] = total.astype(jnp.bfloat16)
+        return carry
+
+    lax.fori_loop(0, blocks, step, 0)
+
+
+class Reduction:
+    def __init__(self, here, p0, r1a, r1b, r2a, r2b, sems, index):
+        self.here, self.p0 = here, p0
+        self.r1a, self.r1b, self.r2a, self.r2b = r1a, r1b, r2a, r2b
+        self.sems, self.i = sems, index
+        self.planes, _, _, self.rows, cols = p0.shape
+        self.half = cols // 2
+        self.left = pl.ds(0, self.half)
+        self.right = pl.ds(self.half, self.half)
+
+    def sem(self, k):
+        return self.sems.at[self.i, k, 0], self.sems.at[self.i, k, 1]
+
+    def first(self):
+        h = self.here
+        self.s1a = h.send(
+            self.p0.at[:, 1 - h.x, :, :, self.left], self.r1a, *self.sem(0), h.at(dx=1)
+        )
+        self.s1b = h.send(
+            self.p0.at[:, :, 1 - h.y, :, self.right], self.r1b, *self.sem(1), h.at(dy=1)
+        )
+
+    def second(self):
+        h = self.here
+        self.s1a.wait_recv()
+        add_into(
+            lambda i: self.p0.at[i // 2, h.x, i % 2, :, self.left],
+            lambda i: self.r1a.at[i // 2, i % 2],
+            2 * self.planes,
+            self.half,
+        )
+        self.s2a = h.send(
+            self.p0.at[:, h.x, 1 - h.y, :, self.left], self.r2a, *self.sem(2), h.at(dy=1)
+        )
+        self.s1b.wait_recv()
+        add_into(
+            lambda i: self.p0.at[i // 2, i % 2, h.y, :, self.right],
+            lambda i: self.r1b.at[i // 2, i % 2],
+            2 * self.planes,
+            self.half,
+        )
+        self.s2b = h.send(
+            self.p0.at[:, 1 - h.x, h.y, :, self.right], self.r2b, *self.sem(3), h.at(dx=1)
+        )
+
+    def third(self):
+        h = self.here
+        self.s2a.wait_recv()
+        add_into(
+            lambda i: self.p0.at[i, h.x, h.y, :, self.left],
+            lambda i: self.r2a.at[i],
+            self.planes,
+            self.half,
+        )
+        self.s2b.wait_recv()
+        add_into(
+            lambda i: self.p0.at[i, h.x, h.y, :, self.right],
+            lambda i: self.r2b.at[i],
+            self.planes,
+            self.half,
+        )
+        return self.p0.at[:, h.x, h.y]
+
+
+def fetch_kernel(dp_count, weight_count, gram_tokens, *refs):
+    shards = refs[:weight_count]
+    lists, table = refs[weight_count : weight_count + 2]
+    fulls = refs[weight_count + 2 : 2 * weight_count + 2]
+    (
+        summed,
+        send0,
+        p0,
+        r1a,
+        r1b,
+        r2a,
+        r2b,
+        r3,
+        g_rows,
+        core_sems,
+        stage_sems,
+        z_sems,
+        local_sems,
+        w_send,
+        w_recv,
+    ) = refs[2 * weight_count + 2 :]
+    here = Place(dp_count)
+    n = dp_count
+    z, x, y, c = here.z, here.x, here.y, here.c
+    tokens = gram_tokens
+
+    class Weight:
+        def __init__(self, i):
+            self.i = i
+            self.shard, self.full = shards[i], fulls[i]
+            self.kind = i % 2
+            rows, cols = self.shard.shape
+            self.by_cols = rows % 128 != 0
+            self.step = (cols if self.by_cols else rows) // 8
+            near, far = (x, y) if self.kind == 0 else (y, x)
+            self.q = (c * 2 + far) * 2 + near
+
+        def cut(self, ref, start, count):
+            span = pl.ds(start * self.step, count * self.step)
+            if self.by_cols:
+                return ref.at[:, span]
+            return ref.at[span, :]
+
+        def local(self):
+            self.copy = pltpu.make_async_copy(
+                self.shard, self.full.at[z], local_sems.at[self.i]
+            )
+            self.copy.start()
+
+        def stage(self, k, j, start, count, src_ref, plane, peer):
+            here.send(
+                self.cut(src_ref, start, count),
+                self.cut(self.full.at[plane], start, count),
+                w_send.at[self.i, k, j - 1],
+                w_recv.at[self.i, k, j - 1],
+                peer,
+            )
+
+        def came(self, k, j, start, count):
+            plane = lax.rem(z + n - j, n)
+            here.expect(
+                self.cut(self.full.at[plane], start, count), w_recv.at[self.i, k, j - 1]
+            )
+            return plane
+
+        def along_z(self):
+            for j in range(1, n):
+                self.stage(0, j, self.q, 1, self.shard, z, here.at(dz=j))
+
+        def near(self):
+            for j in range(1, n):
+                plane = self.came(0, j, self.q, 1)
+                peer = here.at(dx=1) if self.kind == 0 else here.at(dy=1)
+                self.stage(1, j, self.q, 1, self.full.at[plane], plane, peer)
+
+        def far(self):
+            other = self.q + 1 - 2 * (self.q % 2)
+            for j in range(1, n):
+                plane = self.came(1, j, other, 1)
+                peer = here.at(dy=1) if self.kind == 0 else here.at(dx=1)
+                self.stage(2, j, self.q // 2 * 2, 2, self.full.at[plane], plane, peer)
+
+        def across(self):
+            pair = self.q // 2
+            other = pair + 1 - 2 * (pair % 2)
+            for j in range(1, n):
+                plane = self.came(2, j, other * 2, 2)
+                self.stage(3, j, c * 4, 4, self.full.at[plane], plane, here.at(dc=1))
+
+        def done(self):
+            for j in range(1, n):
+                self.came(3, j, (1 - c) * 4, 4)
+            self.copy.wait()
+
+    weights = [Weight(i) for i in range(weight_count)]
+
+    row_iota = lax.broadcasted_iota(jnp.int32, (SLOTS, table.shape[0]), 1)
+    byte_iota = lax.broadcasted_iota(jnp.int32, (SLOTS, tokens), 1)
+
+    def partial_sums(plane, core, write):
+        for place in range(4):
+            source = plane * 8 + place * 2 + core
+            entry = lists[source]
+            pick = (jnp.right_shift(entry, 8) == row_iota).astype(jnp.bfloat16)
+            g_rows[place * SLOTS : (place + 1) * SLOTS, :] = matmul(pick, table[...]).astype(
+                jnp.bfloat16
+            )
+        for place in range(4):
+            source = plane * 8 + place * 2 + core
+            entry = lists[source]
+            to_byte = (jnp.bitwise_and(entry, 255) == byte_iota).astype(jnp.bfloat16)
+            sums = t_times(to_byte, g_rows[place * SLOTS : (place + 1) * SLOTS, :])
+            write(place, sums)
+
+    units = []
+    for u in range(n):
+        units.append(
+            Reduction(
+                here,
+                p0.at[pl.ds(u, 1)],
+                r1a.at[pl.ds(u, 1)],
+                r1b.at[pl.ds(u, 1)],
+                r2a.at[pl.ds(u, 1)],
+                r2b.at[pl.ds(u, 1)],
+                stage_sems,
+                u,
+            )
+        )
+    core_copies = [None] * n
+    z_copies = [None] * n
+
+    def plane_of(u):
+        return lax.rem(z + u + 1, n)
+
+    def hash_a(u):
+        slot = u % 2
+        if u >= 2:
+            here.sent(core_copies[u - 2])
+
+        def write(place, sums):
+            send0[slot, place // 2, place % 2] = sums.astype(jnp.bfloat16)
+
+        partial_sums(plane_of(u), 1 - c, write)
+        core_copies[u] = here.send(
+            send0.at[slot], p0.at[u], core_sems.at[u, 0], core_sems.at[u, 1], here.at(dc=1)
+        )
+
+    def hash_b(u):
+        core_copies[u].wait_recv()
+
+        def write(place, sums):
+            total = sums + p0[u, place // 2, place % 2].astype(jnp.float32)
+            p0[u, place // 2, place % 2] = total.astype(jnp.bfloat16)
+
+        partial_sums(plane_of(u), c, write)
+        units[u].first()
+
+    def hash_c(u):
+        units[u].second()
+
+    def hash_d(u):
+        mine = units[u].third()
+        if u < n - 1:
+            z_copies[u] = here.send(
+                mine.at[0], r3.at[u], z_sems.at[u, 0], z_sems.at[u, 1], here.at(dz=u + 1)
+            )
+
+    def hash_e():
+        for u in range(n - 1):
+            z_copies[u].wait_recv()
+        total = p0[n - 1, x, y].astype(jnp.float32)
+        for u in range(n - 1):
+            total = total + r3[u].astype(jnp.float32)
+        summed[...] = total
+
+    here.greet()
+    for w in weights:
+        w.local()
+    for w in weights[:2]:
+        w.along_z()
+    steps = []
+    hash_steps = []
+    for t in range(n + 3):
+        group = []
+        for u, stage in ((t, hash_a), (t - 1, hash_b), (t - 2, hash_c), (t - 3, hash_d)):
+            if 0 <= u < n:
+                group.append(lambda u=u, stage=stage: stage(u))
+        hash_steps.append(group)
+    hash_steps.append([hash_e])
+    for t in range(max(weight_count + 3, len(hash_steps))):
+        if t + 2 < weight_count:
+            weights[t + 2].along_z()
+        if t < len(hash_steps):
+            for run in hash_steps[t]:
+                run()
+        if t < weight_count:
+            weights[t].near()
+        if 0 <= t - 1 < weight_count:
+            weights[t - 1].far()
+        if 0 <= t - 2 < weight_count:
+            weights[t - 2].across()
+        if 0 <= t - 3 < weight_count:
+            weights[t - 3].done()
+    here.finish()
+
+
+def fetch(lists, table, shards, dp_count, tokens):
+    width = table.shape[1]
+    count = len(shards)
+    hbm = pl.BlockSpec(memory_space=pl.ANY)
+    vmem = pl.BlockSpec(memory_space=pltpu.VMEM)
+    n, half = dp_count, width // 2
+    low = jnp.bfloat16
+    dma = pltpu.SemaphoreType.DMA
+    results = pl.pallas_call(
+        functools.partial(fetch_kernel, dp_count, count, tokens),
+        out_shape=[jax.ShapeDtypeStruct((n, *w.shape), w.dtype) for w in shards]
+        + [jax.ShapeDtypeStruct((tokens, width), jnp.float32)],
+        in_specs=[hbm] * count + [vmem, vmem],
+        out_specs=[hbm] * count + [vmem],
+        scratch_shapes=[
+            pltpu.VMEM((2, 2, 2, tokens, width), low),
+            pltpu.VMEM((n, 2, 2, tokens, width), low),
+            pltpu.VMEM((n, 2, tokens, half), low),
+            pltpu.VMEM((n, 2, tokens, half), low),
+            pltpu.VMEM((n, tokens, half), low),
+            pltpu.VMEM((n, tokens, half), low),
+            pltpu.VMEM((n - 1, tokens, width), low),
+            pltpu.VMEM((4 * SLOTS, width), low),
+            dma((n, 2)),
+            dma((n, 4, 2)),
+            dma((n - 1, 2)),
+            dma((count,)),
+            dma((count, 4, n - 1)),
+            dma((count, 4, n - 1)),
+        ],
+        compiler_params=pltpu.CompilerParams(
+            collective_id=0, has_side_effects=True, vmem_limit_bytes=VMEM_CAP
+        ),
+        name="fetch",
+    )(*shards, lists, table)
+    fulls = [w.reshape(n * w.shape[1], w.shape[2]) for w in results[:count]]
+    return fulls, results[count]
+
+
+def grads_kernel(dp_count, units, left_count, right_count, slots_of, *refs):
+    n = dp_count
+    count = len(units)
+    refs = list(refs)
+
+    def take(number):
+        taken = refs[:number]
+        del refs[:number]
+        return taken
+
+    lefts_in, rights_in = take(left_count), take(right_count)
+    embed_in, gains_in = take(2)
+    outs = take(count)
+    gathered, gains_out = take(2)
+    lefts, rights = take(left_count), take(right_count)
+    pools = take(len(slots_of))
+    r1a, r1b, r2a, r2b, r3 = (take(count) for _ in range(5))
+    gain_send, gain_recv = take(2)
+    (
+        left_sems,
+        right_sems,
+        stage_sems,
+        z_sems,
+        gain_sems,
+        own_sem,
+        near_sems,
+        plane_sems,
+    ) = refs
+    here = Place(n)
+    z, x, y, c = here.z, here.x, here.y, here.c
+
+    here.greet()
+
+    def bring(source, target, sems, i, split):
+        mine = source.at[c] if split else source
+        theirs = source.at[1 - c] if split else source
+        local = pltpu.make_async_copy(mine, target.at[0], sems.at[i, 0])
+        local.start()
+        remote = here.send(
+            theirs, target.at[1], sems.at[i, 1], sems.at[i, 2], here.at(dc=1)
+        )
+        return [local, remote]
+
+    left_copies, right_copies = {}, {}
+
+    def need(i):
+        left, right = units[i][0], units[i][1]
+        if left not in left_copies:
+            left_copies[left] = bring(lefts_in[left], lefts[left], left_sems, left, True)
+        if right not in right_copies:
+            right_copies[right] = bring(rights_in[right], rights[right], right_sems, right, False)
+
+    def have(i):
+        for copies in (left_copies[units[i][0]], right_copies[units[i][1]]):
+            if copies:
+                copies[0].wait()
+                copies[1].wait_recv()
+                copies.clear()
+
+    own = pltpu.make_async_copy(embed_in, gathered.at[z, x, y, c], own_sem)
+    own.start()
+    for j in range(1, n):
+        here.send(
+            embed_in,
+            gathered.at[z, x, y, c],
+            plane_sems.at[j - 1, 0],
+            plane_sems.at[j - 1, 1],
+            here.at(dz=j),
+        )
+    width = embed_in.shape[1]
+    left_half, right_half = pl.ds(0, width // 2), pl.ds(width // 2, width // 2)
+
+    def embed_near(j):
+        plane = lax.rem(z + n - j, n)
+        if j:
+            here.expect(gathered.at[plane, x, y, c], plane_sems.at[j - 1, 1])
+        else:
+            own.wait()
+        a = gathered.at[plane, x, y, c, :, left_half]
+        b = gathered.at[plane, x, y, c, :, right_half]
+        here.send(a, a, near_sems.at[j, 0, 0], near_sems.at[j, 0, 1], here.at(dx=1))
+        here.send(b, b, near_sems.at[j, 1, 0], near_sems.at[j, 1, 1], here.at(dy=1))
+
+    def embed_far(j):
+        plane = lax.rem(z + n - j, n)
+        here.expect(gathered.at[plane, 1 - x, y, c, :, left_half], near_sems.at[j, 0, 1])
+        here.expect(gathered.at[plane, x, 1 - y, c, :, right_half], near_sems.at[j, 1, 1])
+        a = gathered.at[plane, :, y, c, :, left_half]
+        b = gathered.at[plane, x, :, c, :, right_half]
+        here.send(a, a, near_sems.at[j, 2, 0], near_sems.at[j, 2, 1], here.at(dy=1))
+        here.send(b, b, near_sems.at[j, 3, 0], near_sems.at[j, 3, 1], here.at(dx=1))
+
+    def embed_across(j):
+        plane = lax.rem(z + n - j, n)
+        here.expect(gathered.at[plane, :, 1 - y, c, :, left_half], near_sems.at[j, 2, 1])
+        here.expect(gathered.at[plane, 1 - x, :, c, :, right_half], near_sems.at[j, 3, 1])
+        a = gathered.at[plane, :, :, c]
+        here.send(a, a, near_sems.at[j, 4, 0], near_sems.at[j, 4, 1], here.at(dc=1))
+
+    def embed_done(j):
+        plane = lax.rem(z + n - j, n)
+        here.expect(gathered.at[plane, :, :, 1 - c], near_sems.at[j, 4, 1])
+
+    def gains(stage):
+        if stage == 0:
+            gain_send[0] = gains_in[...]
+        elif stage <= 3:
+            here.expect(gain_recv.at[stage - 1], gain_sems.at[stage - 1, 1])
+            gain_send[stage] = gain_send[stage - 1] + gain_recv[stage - 1]
+        if stage < 3:
+            peer = (here.at(dc=1), here.at(dx=1), here.at(dy=1))[stage]
+            here.send(
+                gain_send.at[stage],
+                gain_recv.at[stage],
+                gain_sems.at[stage, 0],
+                gain_sems.at[stage, 1],
+                peer,
+            )
+        elif stage == 3:
+            for j in range(1, n):
+                here.send(
+                    gain_send.at[3],
+                    gain_recv.at[2 + j],
+                    gain_sems.at[2 + j, 0],
+                    gain_sems.at[2 + j, 1],
+                    here.at(dz=j),
+                )
+        else:
+            total = gain_send[3]
+            for j in range(1, n):
+                here.expect(gain_recv.at[2 + j], gain_sems.at[2 + j, 1])
+                total = total + gain_recv[2 + j]
+            gains_out[...] = total
+
+    sums = [None] * count
+    using = {}
+    mine_of = [None] * count
+    sent_of = [None] * count
+
+    def product(i):
+        left, right, pool, slot = units[i]
+        have(i)
+        if (pool, slot) in using:
+            for copy in using[(pool, slot)]:
+                here.sent(copy)
+        p0 = pools[pool].at[slot]
+        xt, g = lefts[left], rights[right]
+        k, depth = xt.shape[2], xt.shape[3]
+        cols = g.shape[2]
+        chunks = 1 if k <= 32 else n
+        planes = n // chunks
+        tile = 256
+
+        def columns(t, carry):
+            span = pl.ds(pl.multiple_of(t * tile, tile), tile)
+            for chunk in range(chunks):
+                total = None
+                for who in range(2):
+                    rows = xt[who, chunk * planes * 4 : (chunk + 1) * planes * 4]
+                    part = matmul(rows.reshape(planes * 4 * k, depth), g[who, :, span])
+                    total = part if total is None else total + part
+                p0[chunk * planes : (chunk + 1) * planes, :, :, :, span] = total.astype(
+                    jnp.bfloat16
+                ).reshape(planes, 2, 2, k, tile)
+            return carry
+
+        lax.fori_loop(0, cols // tile, columns, 0)
+        sums[i] = Reduction(here, p0, r1a[i], r1b[i], r2a[i], r2b[i], stage_sems, i)
+        sums[i].first()
+        using[(pool, slot)] = [sums[i].s1a, sums[i].s1b]
+
+    def second(i):
+        sums[i].second()
+        using[units[i][2:]] += [sums[i].s2a, sums[i].s2b]
+
+    def third(i):
+        mine = sums[i].third()
+        sent_of[i] = []
+        for j in range(1, n):
+            sent_of[i].append(
+                here.send(
+                    mine.at[lax.rem(z + j, n)],
+                    r3[i].at[j - 1],
+                    z_sems.at[i, j - 1, 0],
+                    z_sems.at[i, j - 1, 1],
+                    here.at(dz=j),
+                )
+            )
+        using[units[i][2:]] += sent_of[i]
+        mine_of[i] = mine
+
+    def final(i):
+        total = mine_of[i][z].astype(jnp.float32)
+        for j in range(1, n):
+            sent_of[i][j - 1].wait_recv()
+            total = total + r3[i][j - 1].astype(jnp.float32)
+        outs[i][...] = total
+
+    ahead = 2
+    for i in range(ahead):
+        need(i)
+    for t in range(count + 4):
+        if t + ahead < count:
+            need(t + ahead)
+        if t < 5:
+            gains(t)
+        if 0 <= t - 4 < count:
+            final(t - 4)
+        if t < count:
+            product(t)
+        if t < n:
+            embed_near(t)
+        if 0 <= t - 1 < n:
+            embed_far(t - 1)
+        if 0 <= t - 2 < n:
+            embed_across(t - 2)
+        if 0 <= t - 3 < n:
+            embed_done(t - 3)
+        if 0 <= t - 1 < count:
+            second(t - 1)
+        if 0 <= t - 3 < count:
+            third(t - 3)
+    here.finish()
+
+
+def reduce_grads(pairs, lefts, rights, embed_low, gains, dp_count):
+    n = dp_count
+    low = jnp.bfloat16
+    dma = pltpu.SemaphoreType.DMA
+    hbm = pl.BlockSpec(memory_space=pl.ANY)
+    vmem = pl.BlockSpec(memory_space=pltpu.VMEM)
+    shapes, units, pools = [], [], []
+    seen = {}
+    for left, right in pairs:
+        shape = (lefts[left].shape[2], rights[right].shape[1])
+        number = seen.get(shape, 0)
+        seen[shape] = number + 1
+        shapes.append(shape)
+    classes = list(seen)
+    slots = [min(seen[s], 5) for s in classes]
+    used = {s: 0 for s in classes}
+    for (left, right), shape in zip(pairs, shapes):
+        pool = classes.index(shape)
+        units.append((left, right, pool, used[shape] % slots[pool]))
+        used[shape] += 1
+    count = len(pairs)
+    tokens, width = embed_low.shape
+    scratch = [pltpu.VMEM(a.shape, low) for a in lefts]
+    scratch += [pltpu.VMEM((2, *a.shape), low) for a in rights]
+    scratch += [pltpu.VMEM((s, n, 2, 2, *shape), low) for s, shape in zip(slots, classes)]
+    halves = [(k, cols // 2) for k, cols in shapes]
+    for _ in range(2):
+        scratch += [pltpu.VMEM((n, 2, *half), low) for half in halves]
+    for _ in range(2):
+        scratch += [pltpu.VMEM((n, *half), low) for half in halves]
+    scratch += [pltpu.VMEM((n - 1, *shape), low) for shape in shapes]
+    scratch += [
+        pltpu.VMEM((4, 8, width), jnp.float32),
+        pltpu.VMEM((2 + n, 8, width), jnp.float32),
+        dma((len(lefts), 3)),
+        dma((len(rights), 3)),
+        dma((count, 4, 2)),
+        dma((count, n - 1, 2)),
+        dma((2 + n, 2)),
+        dma,
+        dma((n, 5, 2)),
+        dma((n - 1, 2)),
+    ]
+    results = pl.pallas_call(
+        functools.partial(grads_kernel, n, units, len(lefts), len(rights), slots),
+        out_shape=[jax.ShapeDtypeStruct(shape, jnp.float32) for shape in shapes]
+        + [
+            jax.ShapeDtypeStruct((n, 2, 2, 2, tokens, width), low),
+            jax.ShapeDtypeStruct((8, width), jnp.float32),
+        ],
+        in_specs=[hbm] * (len(lefts) + len(rights) + 1) + [vmem],
+        out_specs=[vmem] * count + [hbm, vmem],
+        scratch_shapes=scratch,
+        compiler_params=pltpu.CompilerParams(
+            collective_id=1, has_side_effects=True, vmem_limit_bytes=VMEM_CAP
+        ),
+        name="reduce_grads",
+    )(*lefts, *rights, embed_low, gains)
+    return results[:count], results[count], results[count + 1]
+
+
+def spread_kernel(lists, rows_of, grads, out, counts, stacked):
+    step = pl.program_id(0)
+    group, tokens = grads.shape[0], grads.shape[1]
+
+    @pl.when(step == 0)
+    def _():
+        out[...] = jnp.zeros_like(out)
+        counts[...] = jnp.zeros_like(counts)
+
+    byte_iota = lax.broadcasted_iota(jnp.int32, (SLOTS, tokens), 1)
+    for s in range(group):
+        pick = (jnp.bitwise_and(lists[s], 255) == byte_iota).astype(jnp.bfloat16)
+        stacked[s * SLOTS : (s + 1) * SLOTS, :] = matmul(pick, grads[s]).astype(jnp.bfloat16)
+    row_iota = lax.broadcasted_iota(jnp.int32, (out.shape[0], group * SLOTS), 0)
+    onto = (rows_of[0] == row_iota).astype(jnp.float32)
+    counts[...] += jnp.sum(onto, axis=1, keepdims=True)
+    out[...] += matmul(onto.astype(jnp.bfloat16), stacked[...])
+
+
+def spread(entries, gathered, rows_dev):
+    sources, tokens, width = gathered.shape
+    group = 8
+    steps = sources // group
+    rows_of = jnp.right_shift(entries, 8).reshape(steps, 1, group * SLOTS)
+    out, counts = pl.pallas_call(
+        spread_kernel,
+        grid=(steps,),
+        out_shape=[
+            jax.ShapeDtypeStruct((rows_dev, width), jnp.float32),
+            jax.ShapeDtypeStruct((rows_dev, 1), jnp.float32),
+        ],
+        in_specs=[
+            pl.BlockSpec((group, SLOTS, 1), lambda i: (i, 0, 0)),
+            pl.BlockSpec((1, 1, group * SLOTS), lambda i: (i, 0, 0)),
+            pl.BlockSpec((group, tokens, width), lambda i: (i, 0, 0)),
+        ],
+        out_specs=[
+            pl.BlockSpec((rows_dev, width), lambda i: (0, 0)),
+            pl.BlockSpec((rows_dev, 1), lambda i: (0, 0)),
+        ],
+        scratch_shapes=[pltpu.VMEM((group * SLOTS, width), jnp.bfloat16)],
+        compiler_params=pltpu.CompilerParams(vmem_limit_bytes=VMEM_CAP),
+        name="spread",
+    )(entries[:, :, None], rows_of, gathered)
+    return out, counts[:, 0].astype(jnp.int32)
+
+
+def asked_rows(all_ids, first_row, rows_dev, gram_count):
+    requests = all_ids.shape[1]
+    local = all_ids - first_row
+    inside = (local >= 0) & (local < rows_dev)
+    index = jnp.arange(requests, dtype=jnp.int32)
+    earlier = (index[:, None] < index[None, :]).astype(jnp.bfloat16)
+    place = matmul(inside.astype(jnp.bfloat16), earlier).astype(jnp.int32)
+    place = jnp.where(inside, place, -1)
+    entry = local * 256 + (index // gram_count)[None, :] + 1
+    slots = jnp.arange(SLOTS, dtype=jnp.int32)
+    chosen = place[:, None, :] == slots[None, :, None]
+    return jnp.sum(jnp.where(chosen, entry[:, None, :], 0), axis=2) - 1
+
+
+def by_rows(a, dp_count):
+    depth, total = a.shape
+    pairs = dp_count * 4
+    both = total // pairs
+    a = a.T.reshape(pairs, both, depth)
+    rows = -(-(both // 2) // 16) * 16
+    return jnp.stack([a[:, :rows], a[:, both - rows :]])
+
+
+def own_rows(block, rows):
+    core = lax.axis_index("sub") % 2
+    return jnp.where(core == 0, block[:rows], block[block.shape[0] - rows :])
 
 
 def body(
@@ -490,9 +1236,373 @@
     )
 
 
+def fast_body(
+    byte_ids,
+    hash_ids,
+    lengths,
+    byte_table,
+    hash_table,
+    norm_attn,
+    norm_ffn,
+    norm_cross,
+    w_query,
+    w_key,
+    w_value,
+    w_out,
+    w_gate,
+    w_up,
+    w_down,
+    c_query,
+    c_key,
+    c_value,
+    c_out,
+    cot_bytes,
+    cot_patches,
+):
+    dp_count = lax.axis_size("dp")
+    rs_count = lax.axis_size(("rep", "sub"))
+    all_count = dp_count * rs_count
+    rank_seq = lax.axis_index(("rep", "sub"))
+    rank_table = lax.axis_index("dp") * rs_count + rank_seq
+    tokens, gram_count = hash_ids.shape
+    rows_dev, model_width = hash_table.shape
+    head_count = model_width // HD
+    request_count = tokens * gram_count
+    all_ids = lax.all_gather(hash_ids.reshape(1, request_count), ("dp", "rep", "sub"), tiled=True)
+    entries = asked_rows(all_ids, rank_table * rows_dev, rows_dev, gram_count)
+    weight_list = (
+        w_query,
+        w_key,
+        w_value,
+        w_out,
+        w_gate,
+        w_up,
+        w_down,
+        c_query,
+        c_key,
+        c_value,
+        c_out,
+    )
+    order = (0, 1, 2, 3, 4, 5, 7, 8, 9, 6, 10)
+    got, hash_sum = fetch(
+        entries[:, :, None], hash_table, [weight_list[i] for i in order], dp_count, tokens
+    )
+    gathered = [got[order.index(i)] for i in range(len(order))]
+    one_hot = byte_ids[:, None] == jnp.arange(BYTE_VALUES, dtype=jnp.int32)[None, :]
+    embedded = matmul(one_hot.astype(jnp.bfloat16), byte_table) + hash_sum
+    (
+        full_query,
+        full_key,
+        full_value,
+        full_out,
+        full_gate,
+        full_up,
+        full_down,
+        full_cquery,
+        full_ckey,
+        full_cvalue,
+        full_cout,
+    ) = gathered
+    x_attn, normed_attn, scale_attn = normalize(embedded, norm_attn)
+    queries = matmul(x_attn, full_query).astype(jnp.bfloat16).reshape(tokens, head_count, HD)
+    key_rows = matmul(x_attn, full_key).astype(jnp.bfloat16).reshape(tokens, head_count, HD)
+    value_rows = matmul(x_attn, full_value).astype(jnp.bfloat16).reshape(tokens, head_count, HD)
+    behind = (WIN - 2) // tokens + 1
+    key_parts = []
+    value_parts = []
+    for offset_back in range(behind, 0, -1):
+        far_keys, far_values = passed_along((key_rows, value_rows), ("rep", "sub"), offset_back)
+        key_parts.append(far_keys)
+        value_parts.append(far_values)
+    all_keys = jnp.concatenate(key_parts + [key_rows], axis=0)
+    all_values = jnp.concatenate(value_parts + [value_rows], axis=0)
+    q_rows = min(tokens, 512)
+    key_span = (WIN - 1 + q_rows - 1) // q_rows * q_rows
+    base_key = (rank_seq - behind) * tokens
+    block_index = 0
+    q_start = block_index * q_rows
+    k_start = behind * tokens + q_start - key_span
+    allowed = window_mask(
+        rank_seq * tokens + q_start, base_key + k_start, q_rows, q_rows + key_span
+    )
+    scores = (
+        jnp.einsum("qhd,khd->hqk", queries, all_keys, preferred_element_type=jnp.float32)
+        * SCORE_SCALE
+    )
+    prob_block, log_total = soft_forward(scores, allowed)
+    attended_parts = jnp.einsum(
+        "hqk,khd->qhd",
+        prob_block.astype(jnp.bfloat16),
+        all_values,
+        preferred_element_type=jnp.float32,
+    )
+    lse_parts = [log_total]
+    attended = attended_parts.astype(jnp.bfloat16).reshape(tokens, model_width)
+    h_mid = embedded + matmul(attended, full_out)
+    x_ffn, normed_ffn, scale_ffn = normalize(h_mid, norm_ffn)
+    gate_pre = matmul(x_ffn, full_gate)
+    up_pre = matmul(x_ffn, full_up)
+    gate_sig = jax.nn.sigmoid(gate_pre)
+    silu_val = gate_pre * gate_sig
+    hidden = (silu_val * up_pre).astype(jnp.bfloat16)
+    h_out = h_mid + matmul(hidden, full_down)
+    byte_states = h_out.astype(jnp.bfloat16)
+    x_cross, normed_cross, scale_cross = normalize(h_out, norm_cross)
+    patch_len = lengths[0]
+    patch_count = patch_len.shape[0]
+    patch_end = jnp.cumsum(patch_len)
+    patch_start = patch_end - patch_len
+    byte_pos = jnp.arange(tokens, dtype=jnp.int32)
+    member = (byte_pos[None, :] >= patch_start[:, None]) & (byte_pos[None, :] < patch_end[:, None])
+    length_f = patch_len.astype(jnp.float32)[:, None]
+    pooled = matmul(member.astype(jnp.bfloat16), x_cross) / length_f
+    pooled_low = pooled.astype(jnp.bfloat16)
+    p_query = (
+        matmul(pooled_low, full_cquery).astype(jnp.bfloat16).reshape(patch_count, head_count, HD)
+    )
+    p_key = matmul(x_cross, full_ckey).astype(jnp.bfloat16).reshape(tokens, head_count, HD)
+    p_value = matmul(x_cross, full_cvalue).astype(jnp.bfloat16).reshape(tokens, head_count, HD)
+    cross_scores = (
+        jnp.einsum("phd,thd->hpt", p_query, p_key, preferred_element_type=jnp.float32) * SCORE_SCALE
+    )
+    cross_prob, cross_lse = soft_forward(cross_scores, member[None])
+    p_attended = (
+        jnp.einsum(
+            "hpt,thd->phd",
+            cross_prob.astype(jnp.bfloat16),
+            p_value,
+            preferred_element_type=jnp.float32,
+        )
+        .astype(jnp.bfloat16)
+        .reshape(patch_count, model_width)
+    )
+    patch_states = (pooled + matmul(p_attended, full_cout)).astype(jnp.bfloat16)
+    grad_patt = (
+        times_t(cot_patches, full_cout).astype(jnp.bfloat16).reshape(patch_count, head_count, HD)
+    )
+    cross_again = (
+        jnp.einsum("phd,thd->hpt", p_query, p_key, preferred_element_type=jnp.float32) * SCORE_SCALE
+    )
+    cross_full = soft_again(cross_again, member[None], cross_lse)
+    grad_cprob = jnp.einsum("phd,thd->hpt", grad_patt, p_value, preferred_element_type=jnp.float32)
+    grad_cscore = soft_back(cross_full, grad_cprob)
+    grad_pquery = (
+        (
+            jnp.einsum("hpt,thd->phd", grad_cscore, p_key, preferred_element_type=jnp.float32)
+            * SCORE_SCALE
+        )
+        .astype(jnp.bfloat16)
+        .reshape(patch_count, model_width)
+    )
+    grad_pkey = (
+        (
+            jnp.einsum("hpt,phd->thd", grad_cscore, p_query, preferred_element_type=jnp.float32)
+            * SCORE_SCALE
+        )
+        .astype(jnp.bfloat16)
+        .reshape(tokens, model_width)
+    )
+    grad_pvalue = (
+        jnp.einsum(
+            "hpt,phd->thd",
+            cross_full.astype(jnp.bfloat16),
+            grad_patt,
+            preferred_element_type=jnp.float32,
+        )
+        .astype(jnp.bfloat16)
+        .reshape(tokens, model_width)
+    )
+    grad_pooled = cot_patches.astype(jnp.float32) + times_t(grad_pquery, full_cquery).astype(
+        jnp.bfloat16
+    ).astype(jnp.float32)
+    to_bytes = lax.dot_general(
+        member.astype(jnp.float32),
+        grad_pooled / length_f,
+        (((0,), (0,)), ((), ())),
+        precision=PRECISE,
+    )
+    grad_xcross = (
+        times_t(grad_pkey, full_ckey) + times_t(grad_pvalue, full_cvalue) + to_bytes
+    ).astype(jnp.bfloat16)
+    grad_hout_norm, grad_norm_cross = norm_back(
+        grad_xcross.astype(jnp.float32), normed_cross, scale_cross, norm_cross
+    )
+    grad_hout = cot_bytes.astype(jnp.float32) + grad_hout_norm
+    grad_branch_f = grad_hout.astype(jnp.bfloat16)
+    grad_hidden = times_t(grad_branch_f, full_down).astype(jnp.bfloat16).astype(jnp.float32)
+    grad_gate = (grad_hidden * up_pre * gate_sig * (1.0 + gate_pre * (1.0 - gate_sig))).astype(
+        jnp.bfloat16
+    )
+    grad_up = (grad_hidden * silu_val).astype(jnp.bfloat16)
+    grad_xffn = (times_t(grad_gate, full_gate) + times_t(grad_up, full_up)).astype(jnp.bfloat16)
+    grad_hmid_norm, grad_norm_ffn = norm_back(
+        grad_xffn.astype(jnp.float32), normed_ffn, scale_ffn, norm_ffn
+    )
+    grad_hmid = grad_hout + grad_hmid_norm
+    grad_branch_a = grad_hmid.astype(jnp.bfloat16)
+    grad_att = times_t(grad_branch_a, full_out).astype(jnp.bfloat16).reshape(tokens, head_count, HD)
+    grad_keys_all = jnp.zeros(((behind + 1) * tokens, head_count, HD), jnp.float32)
+    grad_values_all = jnp.zeros(((behind + 1) * tokens, head_count, HD), jnp.float32)
+    block_index = 0
+    q_start = block_index * q_rows
+    k_start = behind * tokens + q_start - key_span
+    k_stop = k_start + q_rows + key_span
+    allowed = window_mask(
+        rank_seq * tokens + q_start, base_key + k_start, q_rows, q_rows + key_span
+    )
+    scores = (
+        jnp.einsum("qhd,khd->hqk", queries, all_keys, preferred_element_type=jnp.float32)
+        * SCORE_SCALE
+    )
+    prob_block = soft_again(scores, allowed, lse_parts[block_index])
+    grad_prob = jnp.einsum("qhd,khd->hqk", grad_att, all_values, preferred_element_type=jnp.float32)
+    grad_score = soft_back(prob_block, grad_prob)
+    grad_q_parts = (
+        jnp.einsum("hqk,khd->qhd", grad_score, all_keys, preferred_element_type=jnp.float32)
+        * SCORE_SCALE
+    )
+    grad_keys_all = grad_keys_all.at[k_start:k_stop].add(
+        jnp.einsum("hqk,qhd->khd", grad_score, queries, preferred_element_type=jnp.float32)
+        * SCORE_SCALE
+    )
+    grad_values_all = grad_values_all.at[k_start:k_stop].add(
+        jnp.einsum(
+            "hqk,qhd->khd",
+            prob_block.astype(jnp.bfloat16),
+            grad_att,
+            preferred_element_type=jnp.float32,
+        )
+    )
+    grad_keys = grad_keys_all[behind * tokens :]
+    grad_values = grad_values_all[behind * tokens :]
+    for offset_back in range(behind, 0, -1):
+        part_index = behind - offset_back
+        far_grad_k, far_grad_v = (
+            passed_along(
+                grad_keys_all[part_index * tokens : (part_index + 1) * tokens].astype(jnp.bfloat16),
+                ("rep", "sub"),
+                -offset_back,
+            ).astype(jnp.float32),
+            passed_along(
+                grad_values_all[part_index * tokens : (part_index + 1) * tokens].astype(
+                    jnp.bfloat16
+                ),
+                ("rep", "sub"),
+                -offset_back,
+            ).astype(jnp.float32),
+        )
+        grad_keys = grad_keys + far_grad_k
+        grad_values = grad_values + far_grad_v
+    grad_queries = grad_q_parts.astype(jnp.bfloat16).reshape(tokens, model_width)
+    grad_keys_low = grad_keys.astype(jnp.bfloat16).reshape(tokens, model_width)
+    grad_values_low = grad_values.astype(jnp.bfloat16).reshape(tokens, model_width)
+    grad_xattn = (
+        times_t(grad_queries, full_query)
+        + times_t(grad_keys_low, full_key)
+        + times_t(grad_values_low, full_value)
+    ).astype(jnp.bfloat16)
+    grad_embed_norm, grad_norm_attn = norm_back(
+        grad_xattn.astype(jnp.float32), normed_attn, scale_attn, norm_attn
+    )
+    grad_embed = grad_hmid + grad_embed_norm
+    embed_grad = grad_embed.astype(jnp.bfloat16)
+    lefts = [
+        by_rows(a, dp_count)
+        for a in (
+            x_attn,
+            attended,
+            x_ffn,
+            hidden,
+            pooled_low,
+            x_cross,
+            p_attended,
+            one_hot.astype(jnp.bfloat16),
+        )
+    ]
+    rights = [
+        grad_queries,
+        grad_keys_low,
+        grad_values_low,
+        grad_branch_a,
+        grad_gate,
+        grad_up,
+        grad_branch_f,
+        grad_pquery,
+        grad_pkey,
+        grad_pvalue,
+        cot_patches,
+        embed_grad,
+    ]
+    pairs = [
+        (5, 8),
+        (2, 4),
+        (5, 9),
+        (2, 5),
+        (6, 10),
+        (3, 6),
+        (4, 7),
+        (1, 3),
+        (0, 0),
+        (0, 1),
+        (0, 2),
+        (7, 11),
+    ]
+    gain_rows = jnp.concatenate(
+        [grad_norm_attn[None], grad_norm_ffn[None], grad_norm_cross[None]]
+        + [jnp.zeros((5, model_width), jnp.float32)]
+    )
+    sums, all_embed, gain_sums = reduce_grads(pairs, lefts, rights, embed_grad, gain_rows, dp_count)
+    (
+        out_ckey,
+        out_gate,
+        out_cvalue,
+        out_up,
+        out_cout,
+        down_rows,
+        out_cquery,
+        out_proj,
+        out_query,
+        out_key,
+        out_value,
+        byte_rows,
+    ) = sums
+    out_down = own_rows(down_rows, hidden.shape[1] // all_count)
+    out_bytes = own_rows(byte_rows, BYTE_VALUES // all_count)
+    hash_table_grad, row_counts = spread(
+        entries, all_embed.reshape(all_count, tokens, model_width), rows_dev
+    )
+    own_gains = lax.dynamic_slice_in_dim(
+        gain_sums, rank_table * (model_width // all_count), model_width // all_count, 1
+    )
+    out_norm_attn, out_norm_ffn, out_norm_cross = own_gains[0], own_gains[1], own_gains[2]
+    return (
+        byte_states,
+        patch_states,
+        embed_grad,
+        out_bytes,
+        hash_table_grad,
+        row_counts,
+        out_norm_attn,
+        out_norm_ffn,
+        out_norm_cross,
+        out_query,
+        out_key,
+        out_value,
+        out_proj,
+        out_gate,
+        out_up,
+        out_down,
+        out_cquery,
+        out_ckey,
+        out_cvalue,
+        out_cout,
+    )
+
+
 def solution(mesh):
+    fits = mesh.shape["rep"] == 2 and mesh.shape["sub"] == 4 and mesh.shape["dp"] <= 4
     return jax.shard_map(
-        body,
+        fast_body if fits else body,
         mesh=mesh,
         in_specs=(
             P(("dp", "rep", "sub")),

time: 2670 us -> 810 us (0.30)
  waiting for transfers between devices: 1940 us -> 0.02 us
  Pallas kernels: 0 us -> 563 us
  blocking collectives: 273 us -> 43.8 us
  local copies, waits for them, and re-layouts: 130 us -> 41.9 us
  other arithmetic: 122 us -> 35.8 us
  matrix products: 136 us -> 95.7 us
    reduce_scatter x12 -> x0, waiting for transfers between devices: 1340 us -> none  [the longest x1 156 us: body(): lax.psum_scatter(grad_w_gate, ('dp', 'rep', 'sub'), scatter_dimension=0,...]
    pallas_call x0 -> x3, Pallas kernels: none -> 563 us  [the longest x1 273 us: reduce_grads(): pl.pallas_call(functools.partial(grads_kernel, n, units, len(lefts), len(...]
    all_gather x11 -> x0, waiting for transfers between devices: 294 us -> none  [the longest x1 99.4 us: body(): lax.all_gather(weight_list[6], 'dp', axis=0, tiled=True)]
    all_to_all x4 -> x0, waiting for transfers between devices: 291 us -> none  [the longest x1 222 us: body(): lax.all_to_all(served, 'dp', split_axis=0, concat_axis=0, tiled=True)]
    all_to_all x2 -> x0, blocking collectives: 170 us -> none  [the longest x1 158 us: body(): lax.all_to_all(outgoing.astype(jnp.bfloat16), 'dp', split_axis=0, concat_...]
    unnamed x1 -> x0, blocking collectives: 103 us -> none
    scatter-add x2 -> x0, other arithmetic: 48.7 us -> none  [the longest x1 31.4 us: body(): hash_table_grad = jnp.zeros((rows_dev, model_width), jnp.float32).at[safe...]
    all_gather x0 -> x1, blocking collectives: none -> 43.8 us  [fast_body(): lax.all_gather(hash_ids.reshape(1, request_count), ('dp', 'rep', 'sub'),...]
  transfers between devices with their start and end apart: 35 -> 8, of which waited for: 20 -> 0; matrix products, arithmetic and copies ran while one was open for 12% -> 9% of each run, Pallas kernels for 0% -> 0%
where the time goes in v1:
time: 810 us; the launch traced here: 800 us
  Pallas kernels  563 us (70%)
  matrix products  95.7 us (12%)
  blocking collectives  43.8 us (5%)
  local copies, waits for them, and re-layouts  41.9 us (5%)
  other arithmetic  35.8 us (4%)
  starting transfers between devices  17.8 us (2%)
    pallas_call x1, Pallas kernels, reduce_grads(): pl.pallas_call(functools.partial(grads_kernel, n, units, len(lefts), len(...  273 us
    pallas_call x1, Pallas kernels, fetch(): pl.pallas_call(functools.partial(fetch_kernel, dp_count, count, tokens),...  266 us
    all_gather x1, blocking collectives, fast_body(): lax.all_gather(hash_ids.reshape(1, request_count), ('dp', 'rep', 'sub'),...  43.8 us
    dot_general x11, matrix products, times_t(): lax.dot_general(matrix_a, matrix_b, (((1,), (1,)), ((), ())), preferred_e...  27.7 us
    dot_general x14, matrix products, matmul(): return jnp.dot(matrix_a, matrix_b, preferred_element_type=jnp.float32)  26.3 us
    pallas_call x1, Pallas kernels, spread(): pl.pallas_call(spread_kernel, grid=(steps,), out_shape=[jax.ShapeDtypeStr...  23.7 us
    ppermute x8, starting transfers between devices, passed_along(): return lax.ppermute(x, axis, pairs)  17.8 us
  transfers between devices with their start and end apart: 8, of which 0 were waited for; matrix products, arithmetic and copies ran while one was open for 9% of the time, Pallas kernels for 0%

profile of v1, /device:TPU:0, one launch (start us, length us, event | category | flops | bytes accessed | tf_op | source)
XLA Modules:
  0.0 800.3 jit_solution(2142547001661854086)
XLA Ops:
  1.7 43.8 %all-gather = s32[32,1,1536]{2,1,0:T(1,128)S(1)} all-gather(s32[1,1,1536]{2,1,0:T(1,128)S(1)} %reshape.537), channel_id=1, replica_groups=mesh['dp'=4,'rep'=2,'sub'=4] {'dp','rep','sub'}, dimensions={0}, use_global_device_ids=true | all-gather | bytes 202752 | tf_op jit(solution)/shard_map/all_gather | solution.py:1271
  46.2 2.6 select_reduce_fusion
  50.4 266.2 %fetch.1 = (bf16[4,256,1024]{2,1,0:T(8,128)(2,1)}, bf16[4,256,1024]{2,1,0:T(8,128)(2,1)}, bf16[4,256,1024]{2,1,0:T(8,128)(2,1)}, bf16[4,256,1024]{2,1,0:T(8,128)...) custom-call(bf16[256,1024]{1,0:T(8,128)(2,1)} %refs_0_.1, ...), custom_call_target="tpu_custom_call" | custom-call | tf_op jit(solution)/shard_map/fetch/pallas_call | solution.py:436
  320.4 4.4 collective-permute-start.2
  324.8 2.5 collective-permute-start.3
  327.3 2.3 convolution_convert_fusion.7
  330.6 3.0 collective-permute-start
  333.6 2.5 collective-permute-start.1
  336.3 2.3 convolution_convert_fusion.6
  339.2 2.3 fusion.40
  345.4 3.7 select_reduce_fusion.1
  349.1 3.2 fusion
  352.4 3.1 copy-done.2
  355.5 5.6 fusion.28
  364.5 3.0 fusion.11
  372.3 3.3 convolution_convert_fusion.3
  379.0 2.7 convolution_convert_fusion.11
  393.6 3.5 fusion.105
  400.4 2.8 convolution_add_fusion.4
  404.6 5.8 multiply_convert_fusion.1
  412.5 2.4 fusion.52
  417.7 8.2 %fusion.103 = (bf16[768,16,64]{0,2,1:T(8,128)(2,1)S(1)}, f32[768,16,64]{0,2,1:T(8,128)}) fusion(bf16[256,16,64]{0,2,1:T(8,128)(2,1)S(1)} %bitcast.213, f32[16,256,768]{2,1,0:T(8,128)} %copy-done.2, f32[16,256]{1,0:T(8,128)S(1)} %log_add_fusion, pred[256,768]{1,0:T(8,128)(4,1)S(1)} %and_and_fusion), kind=kOutput, calls=%fused_computation.218 | convolution fusion | flops 416022528 | bytes 18038784 | tf_op jit(solution)/shard_map/hqk,qhd->khd/dot_general | solution.py:1469
  429.8 10.2 %multiply_reduce_fusion = (f32[16,256]{1,0:T(8,128)S(1)}, f32[16,256,768]{2,1,0:T(8,128)}) fusion(f32[16,256,768]{2,1,0:T(8,128)} %copy-done.2, f32[16,256]{1,0:T(8,128)S(1)} %log_add_fusion, pred[256,768]{1,0:T(8,128)(4,1)S(1)} %and_and_fusion, bf16[256,16,64]{0,2,1:T(8,128)(2,1)S(1)} %bitcast.214, bf16[256,16,64]{0,2,1:T(8,128)(2,1)} %bitcast.4, ...), kind=kOutput, calls=%fused_computation.3 | convolution fusion | flops 423096320 | bytes 27492352 | tf_op jit(solution)/shard_map/qhd,khd->hqk/dot_general | solution.py:1458
  440.1 7.3 multiply_convert_fusion
  447.4 3.5 fusion.102
  461.4 2.9 fusion.36
  468.4 5.4 fusion.24
  481.5 2.6 convolution_add_fusion.3
  486.9 2.6 fusion.53
  491.4 272.9 %reduce_grads.1 = (f32[32,1024]{1,0:T(8,128)}, f32[32,2816]{1,0:T(8,128)}, f32[32,1024]{1,0:T(8,128)}, f32[32,2816]{1,0:T(8,128)}, f32[32,1024]{1,0:T(8,128)}, /...) custom-call(bf16[2,16,32,256]{3,2,1,0:T(8,128)(2,1)} %pad_maximum_fu, ...), custom_call_target="tpu_custom_call" | custom-call | tf_op jit(solution)/shard_map/reduce_grads/pallas_call | solution.py:735
  764.4 23.7 %spread.1 = (f32[1954,1024]{1,0:T(8,128)}, f32[1954,1]{1,0:T(8,128)}) custom-call(s32[32,96,1]{2,1,0:T(8,128)} %copy.129.refs_11_.lists, s32[4,1,768]{2,1,0:T(1,128)} %shift_right_arithmetic.18.rows_of, bf16[32,256,1024]{2,1,0:T(8,128)(2,1)} %bitcast.197), custom_call_target="tpu_custom_call" | custom-call | tf_op jit(solution)/shard_map/spread/pallas_call | solution.py:777
  788.1 2.3 convert_reduce_fusion
  (305 shorter events, 85.1 us)
Async XLA Ops:
  0.7 316.0 %copy-start = (bf16[256,1024]{1,0:T(8,128)(2,1)S(1)}, bf16[256,1024]{1,0:T(8,128)(2,1)}, u32[]{:S(2)}) copy-start(bf16[256,1024]{1,0:T(8,128)(2,1)} %param.32) | copy-start | bytes 1572868
  50.4 266.3 %copy-start.63 = (s32[256]{0:T(256)S(1)}, s32[256]{0:T(256)}, u32[]{:S(2)}) copy-start(s32[256]{0:T(256)} %param.29) | copy-start | bytes 3076
  50.4 268.1 %copy-start.54 = (f32[1024]{0:T(1024)S(1)}, f32[1024]{0:T(1024)}, u32[]{:S(2)}) copy-start(f32[1024]{0:T(1024)} %param.34) | copy-start | bytes 12292
  320.4 24.9 %collective-permute-start.2 = (bf16[256,16,64]{0,2,1:T(8,128)(2,1)}, bf16[256,16,64]{0,2,1:T(8,128)(2,1)}, u32[]{:S(2)}, u32[]{:S(2)}) collective-permute-start(bf16[256,16,64]{0,2,1:T(8,128)(2,1)} %bitcast.8), channel_id=1, source_target_pairs={{0,2},{1,3},{2,4},{3,5},{4,6},{5,7},{8,10},{9,11},{10,12},{11,13},... | collective-permute-start | bytes 1572872 | tf_op jit(solution)/shard_map/ppermute | solution.py:24
  324.8 20.6 %collective-permute-start.3 = (bf16[256,16,64]{0,2,1:T(8,128)(2,1)}, bf16[256,16,64]{0,2,1:T(8,128)(2,1)}, u32[]{:S(2)}, u32[]{:S(2)}) collective-permute-start(bf16[256,16,64]{0,2,1:T(8,128)(2,1)} %bitcast.8), channel_id=1, source_target_pairs={{0,1},{1,2},{2,3},{3,4},{4,5},{5,6},{6,7},{8,9},{9,10},{10,11},{11... | collective-permute-start | bytes 1572872 | tf_op jit(solution)/shard_map/ppermute | solution.py:24
  330.6 21.8 %collective-permute-start = (bf16[256,16,64]{0,2,1:T(8,128)(2,1)}, bf16[256,16,64]{0,2,1:T(8,128)(2,1)}, u32[]{:S(2)}, u32[]{:S(2)}) collective-permute-start(bf16[256,16,64]{0,2,1:T(8,128)(2,1)} %bitcast.4), channel_id=1, source_target_pairs={{0,2},{1,3},{2,4},{3,5},{4,6},{5,7},{8,10},{9,11},{10,12},{11,13},... | collective-permute-start | bytes 1572872 | tf_op jit(solution)/shard_map/ppermute | solution.py:24
  333.6 18.8 %collective-permute-start.1 = (bf16[256,16,64]{0,2,1:T(8,128)(2,1)}, bf16[256,16,64]{0,2,1:T(8,128)(2,1)}, u32[]{:S(2)}, u32[]{:S(2)}) collective-permute-start(bf16[256,16,64]{0,2,1:T(8,128)(2,1)} %bitcast.4), channel_id=1, source_target_pairs={{0,1},{1,2},{2,3},{3,4},{4,5},{5,6},{6,7},{8,9},{9,10},{10,11},{11... | collective-permute-start | bytes 1572872 | tf_op jit(solution)/shard_map/ppermute | solution.py:24
  338.9 37.9 %copy-start.69 = (f32[64]{0:T(128)}, f32[64]{0:T(128)S(1)}, u32[]{:S(2)}) copy-start(f32[64]{0:T(128)S(1)} %bitcast_convert_fusion) | copy-start | bytes 772
  339.2 37.6 %copy-start.61 = (s32[64]{0:T(128)}, s32[64]{0:T(128)S(1)}, u32[]{:S(2)}) copy-start(s32[64]{0:T(128)S(1)} %reduce.4) | copy-start | bytes 772
  339.2 37.6 %copy-start.65 = (s32[64]{0:T(128)}, s32[64]{0:T(128)S(1)}, u32[]{:S(2)}) copy-start(s32[64]{0:T(128)S(1)} %bitcast_subtract_fusion) | copy-start | bytes 772
  349.1 12.9 %slice-start.7 = ((s8[5767168]{0:T(1024)(128)(4,1)}), s8[4194304]{0:T(1024)(128)(4,1)S(1)}, s32[]{:S(2)}) async-start(s8[5767168]{0:T(1024)(128)(4,1)} %bitcast.255), calls=%async_computation.7 | async-start | bytes 8388608
  352.4 9.7 %slice-start.8 = ((s8[5767168]{0:T(1024)(128)(4,1)}), s8[1572864]{0:T(1024)(128)(4,1)S(1)}, s32[]{:S(2)}) async-start(s8[5767168]{0:T(1024)(128)(4,1)} %bitcast.255), calls=%async_computation.8 | async-start | bytes 3145728
  362.0 27.5 %copy-start.59 = (f32[256]{0:T(256)}, f32[256]{0:T(256)S(1)}, u32[]{:S(2)}) copy-start(f32[256]{0:T(256)S(1)} %add_rsqrt_fusion.1) | copy-start | bytes 3076
  403.2 9.1 %slice-start.5 = ((s8[5767168]{0:T(1024)(128)(4,1)}), s8[4194304]{0:T(1024)(128)(4,1)S(1)}, s32[]{:S(2)}) async-start(s8[5767168]{0:T(1024)(128)(4,1)} %bitcast.252), calls=%async_computation.5 | async-start | bytes 8388608
  416.7 9.2 %copy-start.15 = (bf16[256,1024]{1,0:T(8,128)(2,1)}, bf16[256,1024]{1,0:T(8,128)(2,1)S(1)}, u32[]{:S(2)}) copy-start(bf16[256,1024]{1,0:T(8,128)(2,1)S(1)} %get-tuple-element.122.refs_11_) | copy-start | bytes 1572868
  417.6 22.4 %slice-start = ((s8[12582912]{0:T(1024)(128)(4,1)}), s8[4194304]{0:T(1024)(128)(4,1)S(1)}, s32[]{:S(2)}) async-start(s8[12582912]{0:T(1024)(128)(4,1)} %bitcast.195), calls=%async_computation | async-start | bytes 8388608
  417.7 22.4 %slice-start.1 = ((s8[12582912]{0:T(1024)(128)(4,1)}), s8[4194304]{0:T(1024)(128)(4,1)S(1)}, s32[]{:S(2)}) async-start(s8[12582912]{0:T(1024)(128)(4,1)} %bitcast.195), calls=%async_computation.1 | async-start | bytes 8388608
  427.0 57.1 %collective-permute-start.6 = (bf16[256,16,64]{0,2,1:T(8,128)(2,1)}, bf16[256,16,64]{0,2,1:T(8,128)(2,1)}, u32[]{:S(2)}, u32[]{:S(2)}) collective-permute-start(bf16[256,16,64]{0,2,1:T(8,128)(2,1)} %get-tuple-element.126), channel_id=1, source_target_pairs={{2,0},{3,1},{4,2},{5,3},{6,4},{7,5},{10,8},{11,9},{12,10},{13,11},... | collective-permute-start | bytes 1572872 | tf_op jit(solution)/shard_map/ppermute | solution.py:24
  428.3 11.8 %slice-start.2 = ((s8[12582912]{0:T(1024)(128)(4,1)}), s8[4194304]{0:T(1024)(128)(4,1)S(1)}, s32[]{:S(2)}) async-start(s8[12582912]{0:T(1024)(128)(4,1)} %bitcast.195), calls=%async_computation.2 | async-start | bytes 8388608
  428.3 55.8 %collective-permute-start.7 = (bf16[256,16,64]{0,2,1:T(8,128)(2,1)}, bf16[256,16,64]{0,2,1:T(8,128)(2,1)}, u32[]{:S(2)}, u32[]{:S(2)}) collective-permute-start(bf16[256,16,64]{0,2,1:T(8,128)(2,1)} %get-tuple-element.127), channel_id=1, source_target_pairs={{1,0},{2,1},{3,2},{4,3},{5,4},{6,5},{7,6},{9,8},{10,9},{11,10},{12... | collective-permute-start | bytes 1572872 | tf_op jit(solution)/shard_map/ppermute | solution.py:24
  452.2 26.5 %collective-permute-start.4 = (bf16[256,16,64]{0,2,1:T(8,128)(2,1)}, bf16[256,16,64]{0,2,1:T(8,128)(2,1)}, u32[]{:S(2)}, u32[]{:S(2)}) collective-permute-start(bf16[256,16,64]{0,2,1:T(8,128)(2,1)} %get-tuple-element.128), channel_id=1, source_target_pairs={{2,0},{3,1},{4,2},{5,3},{6,4},{7,5},{10,8},{11,9},{12,10},{13,11},... | collective-permute-start | bytes 1572872 | tf_op jit(solution)/shard_map/ppermute | solution.py:24
  453.5 25.3 %collective-permute-start.5 = (bf16[256,16,64]{0,2,1:T(8,128)(2,1)}, bf16[256,16,64]{0,2,1:T(8,128)(2,1)}, u32[]{:S(2)}, u32[]{:S(2)}) collective-permute-start(bf16[256,16,64]{0,2,1:T(8,128)(2,1)} %get-tuple-element.129), channel_id=1, source_target_pairs={{1,0},{2,1},{3,2},{4,3},{5,4},{6,5},{7,6},{9,8},{10,9},{11,10},{12... | collective-permute-start | bytes 1572872 | tf_op jit(solution)/shard_map/ppermute | solution.py:24
  764.3 26.1 %copy-start.31 = (f32[96,1024]{1,0:T(8,128)S(1)}, f32[96,1024]{1,0:T(8,128)}, u32[]{:S(2)}) copy-start(f32[96,1024]{1,0:T(8,128)} %get-tuple-element.111) | copy-start | bytes 1179652
  764.3 26.9 %copy-start.57 = (f32[16,1024]{1,0:T(8,128)S(1)}, f32[16,1024]{1,0:T(8,128)}, u32[]{:S(2)}) copy-start(f32[16,1024]{1,0:T(8,128)} %get-tuple-element.100) | copy-start | bytes 196612
  764.3 28.7 %copy-start.52 = (f32[32,1024]{1,0:T(8,128)S(1)}, f32[32,1024]{1,0:T(8,128)}, u32[]{:S(2)}) copy-start(f32[32,1024]{1,0:T(8,128)} %get-tuple-element.204) | copy-start | bytes 393220
  764.4 29.4 %copy-start.51 = (f32[32,1024]{1,0:T(8,128)S(1)}, f32[32,1024]{1,0:T(8,128)}, u32[]{:S(2)}) copy-start(f32[32,1024]{1,0:T(8,128)} %get-tuple-element.205) | copy-start | bytes 393220
  764.4 30.0 %copy-start.50 = (f32[32,1024]{1,0:T(8,128)S(1)}, f32[32,1024]{1,0:T(8,128)}, u32[]{:S(2)}) copy-start(f32[32,1024]{1,0:T(8,128)} %get-tuple-element.206) | copy-start | bytes 393220
  788.1 9.1 %copy-start.48 = (f32[32,1024]{1,0:T(8,128)S(1)}, f32[32,1024]{1,0:T(8,128)}, u32[]{:S(2)}) copy-start(f32[32,1024]{1,0:T(8,128)} %get-tuple-element.211) | copy-start | bytes 393220
  788.1 9.8 %copy-start.47 = (f32[32,1024]{1,0:T(8,128)S(1)}, f32[32,1024]{1,0:T(8,128)}, u32[]{:S(2)}) copy-start(f32[32,1024]{1,0:T(8,128)} %get-tuple-element.212) | copy-start | bytes 393220
  788.1 10.4 %copy-start.46 = (f32[32,1024]{1,0:T(8,128)S(1)}, f32[32,1024]{1,0:T(8,128)}, u32[]{:S(2)}) copy-start(f32[32,1024]{1,0:T(8,128)} %get-tuple-element.213) | copy-start | bytes 393220
  788.1 11.1 %copy-start.45 = (f32[32,1024]{1,0:T(8,128)S(1)}, f32[32,1024]{1,0:T(8,128)}, u32[]{:S(2)}) copy-start(f32[32,1024]{1,0:T(8,128)} %get-tuple-element.214) | copy-start | bytes 393220
  788.1 11.7 %copy-start.1 = (bf16[256,1024]{1,0:T(8,128)(2,1)S(1)}, bf16[256,1024]{1,0:T(8,128)(2,1)}, u32[]{:S(2)}) copy-start(bf16[256,1024]{1,0:T(8,128)(2,1)} %param.32) | copy-start | bytes 1572868
  (64 other events, 271.0 us)

commit v2 on v0

--- a/solution.py
+++ b/solution.py
@@ -1,8 +1,16 @@
+import functools
+import typing
+
 import jax
 import jax.numpy as jnp
 from jax import lax
+from jax.experimental import pallas as pl
+from jax.experimental.pallas import tpu as pltpu
 from jax.sharding import PartitionSpec as P
 
+DP, REP, SUB = "dp", "rep", "sub"
+SEQ = (REP, SUB)
+ALL = (DP, REP, SUB)
 HD = 64
 WIN = 512
 BYTE_VALUES = 256
@@ -77,6 +85,1654 @@
         & (key_pos[None, :] >= 0)
     )
     return near[None]
+
+
+MESH_ID = pl.DeviceIdType.MESH
+SLOTS = 96
+GATHER_LAGS = (1, 1, 2, 3)
+
+
+HASH, GATHER, FORWARD = range(3)
+
+
+SCHEDULE = (
+    (HASH, 0),
+    (GATHER, 0),
+    (HASH, 1),
+    (GATHER, 1),
+    (HASH, 2),
+    (GATHER, 2),
+    (HASH, 3),
+    (GATHER, 3),
+    (HASH, 4),
+    (GATHER, 4),
+    (HASH, 5),
+    (GATHER, 5),
+    (HASH, 6),
+    (GATHER, 6),
+    (HASH, 7),
+    (GATHER, 7),
+    (FORWARD, 1),
+    (GATHER, 8),
+    (FORWARD, 1),
+    (GATHER, 9),
+    (FORWARD, 1),
+    (GATHER, 10),
+    (FORWARD, 1),
+    (GATHER, 11),
+    (FORWARD, 1),
+    (GATHER, 12),
+    (FORWARD, 1),
+    (GATHER, 13),
+    (FORWARD, 5),
+)
+VMEM_CAP = 60 * 1024 * 1024
+
+
+class Place:
+    def __init__(self, dp_count):
+        self.n = dp_count
+        self.z = lax.axis_index(DP)
+        self.x = lax.axis_index(REP)
+        sub = lax.axis_index(SUB)
+        self.y = sub // 2
+        self.c = sub % 2
+        self.started, self.maybe = [], []
+
+    def at(self, dz=0, dx=0, dy=0, dc=0):
+        z = lax.rem(self.z + dz, self.n) if dz else self.z
+        x = 1 - self.x if dx else self.x
+        y = 1 - self.y if dy else self.y
+        c = 1 - self.c if dc else self.c
+        return (z, x, y * 2 + c)
+
+    def greet(self):
+        barrier = pltpu.get_barrier_semaphore()
+        peers = [
+            self.at(dx=dx, dy=dy, dc=dc)
+            for dx in range(2)
+            for dy in range(2)
+            for dc in range(2)
+            if dx + dy + dc > 0
+        ]
+        peers += [self.at(dz=j) for j in range(1, self.n)]
+        for peer in peers:
+            pl.semaphore_signal(barrier, inc=1, device_id=peer, device_id_type=MESH_ID)
+        pl.semaphore_wait(barrier, len(peers))
+
+    def send_if(self, there, src, dst, send_sem, recv_sem, peer):
+        copy = pltpu.make_async_remote_copy(
+            src_ref=src,
+            dst_ref=dst,
+            send_sem=send_sem,
+            recv_sem=recv_sem,
+            device_id=peer,
+            device_id_type=MESH_ID,
+        )
+        pl.when(there)(copy.start)
+        self.maybe.append((there, copy))
+
+    def send(self, src, dst, send_sem, recv_sem, peer):
+        copy = pltpu.make_async_remote_copy(
+            src_ref=src,
+            dst_ref=dst,
+            send_sem=send_sem,
+            recv_sem=recv_sem,
+            device_id=peer,
+            device_id_type=MESH_ID,
+        )
+        copy.start()
+        self.started.append(copy)
+        return copy
+
+    def expect(self, dst, recv_sem):
+        pltpu.make_async_remote_copy(
+            src_ref=dst,
+            dst_ref=dst,
+            send_sem=recv_sem,
+            recv_sem=recv_sem,
+            device_id=self.at(dc=1),
+            device_id_type=MESH_ID,
+        ).wait_recv()
+
+    def sent(self, copy):
+        copy.wait_send()
+        self.started = [other for other in self.started if other is not copy]
+
+    def finish(self):
+        for copy in self.started:
+            copy.wait_send()
+        for there, copy in self.maybe:
+            pl.when(there)(copy.wait_send)
+        self.started, self.maybe = [], []
+
+
+def add_into(dst, src, blocks, width):
+    def step(i, carry):
+        total = dst(i)[...].astype(jnp.float32) + src(i)[...].astype(jnp.float32)
+        dst(i)[...] = total.astype(jnp.bfloat16)
+        return carry
+
+    lax.fori_loop(0, blocks, step, 0)
+
+
+class Reduction:
+    def __init__(self, here, p0, r1a, r1b, r2a, r2b, sems, index):
+        self.here, self.p0 = here, p0
+        self.r1a, self.r1b, self.r2a, self.r2b = r1a, r1b, r2a, r2b
+        self.sems, self.i = sems, index
+        self.planes, _, _, self.rows, cols = p0.shape
+        self.half = cols // 2
+        self.left = pl.ds(0, self.half)
+        self.right = pl.ds(self.half, self.half)
+
+    def sem(self, k):
+        return self.sems.at[self.i, k, 0], self.sems.at[self.i, k, 1]
+
+    def first(self):
+        h = self.here
+        self.s1a = h.send(
+            self.p0.at[:, 1 - h.x, :, :, self.left], self.r1a, *self.sem(0), h.at(dx=1)
+        )
+        self.s1b = h.send(
+            self.p0.at[:, :, 1 - h.y, :, self.right], self.r1b, *self.sem(1), h.at(dy=1)
+        )
+
+    def second(self):
+        h = self.here
+        self.s1a.wait_recv()
+        add_into(
+            lambda i: self.p0.at[i // 2, h.x, i % 2, :, self.left],
+            lambda i: self.r1a.at[i // 2, i % 2],
+            2 * self.planes,
+            self.half,
+        )
+        self.s2a = h.send(
+            self.p0.at[:, h.x, 1 - h.y, :, self.left], self.r2a, *self.sem(2), h.at(dy=1)
+        )
+        self.s1b.wait_recv()
+        add_into(
+            lambda i: self.p0.at[i // 2, i % 2, h.y, :, self.right],
+            lambda i: self.r1b.at[i // 2, i % 2],
+            2 * self.planes,
+            self.half,
+        )
+        self.s2b = h.send(
+            self.p0.at[:, 1 - h.x, h.y, :, self.right], self.r2b, *self.sem(3), h.at(dx=1)
+        )
+
+    def third(self):
+        h = self.here
+        self.s2a.wait_recv()
+        add_into(
+            lambda i: self.p0.at[i, h.x, h.y, :, self.left],
+            lambda i: self.r2a.at[i],
+            self.planes,
+            self.half,
+        )
+        self.s2b.wait_recv()
+        add_into(
+            lambda i: self.p0.at[i, h.x, h.y, :, self.right],
+            lambda i: self.r2b.at[i],
+            self.planes,
+            self.half,
+        )
+        return self.p0.at[:, h.x, h.y]
+
+
+EXTRA_IN = 5
+F32, LOW = jnp.float32, jnp.bfloat16
+class Kept(typing.NamedTuple):
+    x_attn: typing.Any
+    queries: typing.Any
+    key_values: typing.Any
+    lse: typing.Any
+    attended: typing.Any
+    h_mid: typing.Any
+    x_ffn: typing.Any
+    gate_pre: typing.Any
+    up_pre: typing.Any
+    hidden: typing.Any
+    h_out: typing.Any
+    byte_states: typing.Any
+    x_cross: typing.Any
+    pooled: typing.Any
+    p_query: typing.Any
+    p_key: typing.Any
+    p_value: typing.Any
+    cross_lse: typing.Any
+    p_attended: typing.Any
+    patch_states: typing.Any
+
+
+def kept_shapes(t, w, f, p):
+    one = jax.ShapeDtypeStruct
+    return Kept(
+        x_attn=one((t, w), LOW),
+        queries=one((t, w), LOW),
+        key_values=one((2, 3 * t, w), LOW),
+        lse=one((t, 128), F32),
+        attended=one((t, w), LOW),
+        h_mid=one((t, w), F32),
+        x_ffn=one((t, w), LOW),
+        gate_pre=one((t, f), F32),
+        up_pre=one((t, f), F32),
+        hidden=one((t, f), LOW),
+        h_out=one((t, w), F32),
+        byte_states=one((t, w), LOW),
+        x_cross=one((t, w), LOW),
+        pooled=one((p, w), LOW),
+        p_query=one((p, w), LOW),
+        p_key=one((t, w), LOW),
+        p_value=one((t, w), LOW),
+        cross_lse=one((p, 128), F32),
+        p_attended=one((p, w), LOW),
+        patch_states=one((p, w), LOW),
+    )
+
+
+def forward_steps(here, fulls, embedded, extra_in, extra_out, slots, scratch):
+    byte_ids, byte_table, gains, starts, ends = extra_in
+    out = Kept(*extra_out)
+    gate_w, up_w, load_sems, halo_sems = scratch
+    tokens, width = embedded.shape
+    heads = width // HD
+    n = here.n
+    z, x, y, c = here.z, here.x, here.y, here.c
+    rank = (x * 2 + y) * 2 + c
+    loads = {}
+    kv = out.key_values
+
+    def load(i, *targets):
+        copies = []
+        for b, target in enumerate(targets):
+            rows = target.shape[0]
+            copy = pltpu.make_async_copy(
+                fulls[i].at[pl.ds(b * rows, rows)], target, load_sems.at[i, b]
+            )
+            copy.start()
+            copies.append(copy)
+        loads[i] = copies
+
+    def load_slot(i, slot):
+        for b in range(4):
+            copy = pltpu.make_async_copy(
+                fulls[i].at[pl.ds(b * (width // 4), width // 4)],
+                slots[slot].at[b // 2, b % 2],
+                load_sems.at[i, b],
+            )
+            copy.start()
+            loads.setdefault(i, []).append(copy)
+
+    def wait(*weights):
+        for i in weights:
+            for copy in loads[i]:
+                copy.wait()
+
+    def through(a, slot):
+        total = None
+        for b in range(4):
+            part = matmul(
+                a[:, b * (width // 4) : (b + 1) * (width // 4)], slots[slot][b // 2, b % 2]
+            )
+            total = part if total is None else total + part
+        return total
+
+    def embed():
+        load_slot(0, 0)
+        load_slot(1, 1)
+        load_slot(2, 2)
+        ids = lax.broadcasted_iota(jnp.int32, (tokens, BYTE_VALUES), 1)
+        pick = jnp.where(byte_ids[...] == ids, 1.0, 0.0).astype(LOW)
+        embedded[...] = embedded[...] + matmul(pick, byte_table[...])
+        out.x_attn[...] = normalize(embedded[...], gains[0:1])[0]
+
+    def project():
+        wait(0, 1, 2)
+        a = out.x_attn[...]
+        kv[0, 2 * tokens :] = through(a, 1).astype(LOW)
+        kv[1, 2 * tokens :] = through(a, 2).astype(LOW)
+        for back in (1, 2):
+            target = rank + back
+            here.send_if(
+                target < 8,
+                kv.at[:, pl.ds(2 * tokens, tokens)],
+                kv.at[:, pl.ds((2 - back) * tokens, tokens)],
+                halo_sems.at[back - 1, 0],
+                halo_sems.at[back - 1, 1],
+                (z, target // 4, lax.rem(target, 4)),
+            )
+        out.queries[...] = through(a, 0).astype(LOW)
+        for back in (1, 2):
+            part = kv.at[:, pl.ds((2 - back) * tokens, tokens)]
+
+            @pl.when(rank >= back)
+            def _():
+                here.expect(part, halo_sems.at[back - 1, 1])
+
+            @pl.when(rank < back)
+            def _():
+                part[...] = jnp.zeros_like(part)
+
+    lane = lax.broadcasted_iota(jnp.int32, (1, 128), 1)
+    sides = [jnp.where(lane < HD, 1.0, 0.0).astype(LOW), jnp.where(lane < HD, 0.0, 1.0).astype(LOW)]
+
+    def attend(first):
+        row = lax.broadcasted_iota(jnp.int32, (tokens, tokens), 0)
+        col = lax.broadcasted_iota(jnp.int32, (tokens, tokens), 1)
+        mine = col <= row
+        far_bias = jnp.where(rank >= 2, 0.0, NEG_BIG)
+        near_bias = jnp.where(rank >= 1, 0.0, NEG_BIG)
+        if first == 0:
+            out.lse[...] = jnp.zeros_like(out.lse)
+        else:
+            load_slot(3, 3)
+
+        def heads_pair(pair, carry):
+            span = pl.ds(pl.multiple_of(pair * 128, 128), 128)
+            q2 = out.queries[:, span]
+            k2, v2 = kv[0, :, span], kv[1, :, span]
+            halves = []
+            for side in range(2):
+                scores = times_t(q2 * sides[side], k2) * SCORE_SCALE
+                edge = jnp.where(mine, scores[:, 2 * tokens :], scores[:, :tokens] + far_bias)
+                middle = scores[:, tokens : 2 * tokens] + near_bias
+                top = jnp.maximum(
+                    jnp.max(edge, axis=1, keepdims=True), jnp.max(middle, axis=1, keepdims=True)
+                )
+                edge, middle = jnp.exp(edge - top), jnp.exp(middle - top)
+                total = jnp.sum(edge, axis=1, keepdims=True) + jnp.sum(
+                    middle, axis=1, keepdims=True
+                )
+                inverse = 1.0 / total
+                edge, middle = edge * inverse, middle * inverse
+                probs = jnp.concatenate(
+                    [
+                        jnp.where(mine, 0.0, edge).astype(LOW),
+                        middle.astype(LOW),
+                        jnp.where(mine, edge, 0.0).astype(LOW),
+                    ],
+                    axis=1,
+                )
+                halves.append(matmul(probs, v2))
+                where = lane == pair * 2 + side
+                out.lse[...] = jnp.where(where, top + jnp.log(total), out.lse[...])
+            out.attended[:, span] = jnp.where(lane < HD, halves[0], halves[1]).astype(LOW)
+            return carry
+
+        lax.fori_loop(first * heads // 4, (first + 1) * heads // 4, heads_pair, 0)
+
+    def attention_out():
+        wait(3)
+        h_mid = embedded[...] + through(out.attended[...], 3)
+        out.h_mid[...] = h_mid
+        out.x_ffn[...] = normalize(h_mid, gains[1:2])[0]
+
+    def down_block(t):
+        return slots[t // 4].at[t // 2 % 2, t % 2]
+
+    tile = 256
+    tiles = gate_w.shape[1] // tile
+
+    def feed_forward():
+        for t in range(tiles):
+            copy = pltpu.make_async_copy(
+                fulls[6].at[pl.ds(t * tile, tile)], down_block(t), down_sems.at[t]
+            )
+            copy.start()
+            loads.setdefault(6, []).append(copy)
+        wait(4, 5)
+        a = out.x_ffn[...]
+
+        def columns(t, carry):
+            span = pl.ds(pl.multiple_of(t * tile, tile), tile)
+            gate = matmul(a, gate_w[:, span])
+            up = matmul(a, up_w[:, span])
+            out.gate_pre[:, span] = gate
+            out.up_pre[:, span] = up
+            out.hidden[:, span] = (gate * jax.nn.sigmoid(gate) * up).astype(LOW)
+            return carry
+
+        lax.fori_loop(0, tiles, columns, 0)
+
+    def feed_out():
+        wait(6)
+        total = out.h_mid[...]
+        for t in range(tiles):
+            total = total + matmul(
+                out.hidden[:, t * tile : (t + 1) * tile], down_block(t)[...]
+            )
+        out.h_out[...] = total
+        out.byte_states[...] = total.astype(LOW)
+        out.x_cross[...] = normalize(total, gains[2:3])[0]
+
+    byte_pos = lax.broadcasted_iota(jnp.int32, (starts.shape[0], tokens), 1)
+
+    def member():
+        return (byte_pos >= starts[...]) & (byte_pos < ends[...])
+
+    pooled_f = []
+
+    def cross_keys():
+        load_slot(8, 4)
+        load_slot(9, 5)
+        inside = jnp.where(member(), 1.0, 0.0).astype(LOW)
+        length = (ends[...] - starts[...]).astype(F32)
+        pooled = matmul(inside, out.x_cross[...]) / length
+        pooled_f.append(pooled)
+        out.pooled[...] = pooled.astype(LOW)
+        wait(8, 9)
+        a = out.x_cross[...]
+        out.p_key[...] = through(a, 4).astype(LOW)
+        out.p_value[...] = through(a, 5).astype(LOW)
+
+    def cross_query():
+        load_slot(7, 3)
+        load_slot(10, 0)
+        wait(7)
+        out.p_query[...] = through(out.pooled[...], 3).astype(LOW)
+        allowed = member()
+        out.cross_lse[...] = jnp.zeros_like(out.cross_lse)
+
+        def heads_pair(pair, carry):
+            span = pl.ds(pl.multiple_of(pair * 128, 128), 128)
+            q2, k2, v2 = out.p_query[:, span], out.p_key[:, span], out.p_value[:, span]
+            halves = []
+            for side in range(2):
+                scores = times_t(q2 * sides[side], k2) * SCORE_SCALE
+                masked = jnp.where(allowed, scores, NEG_BIG)
+                top = jnp.max(masked, axis=1, keepdims=True)
+                exps = jnp.exp(masked - top)
+                total = jnp.sum(exps, axis=1, keepdims=True)
+                halves.append(matmul((exps / total).astype(LOW), v2))
+                where = lane == pair * 2 + side
+                out.cross_lse[...] = jnp.where(
+                    where, top + jnp.log(total), out.cross_lse[...]
+                )
+            out.p_attended[:, span] = jnp.where(lane < HD, halves[0], halves[1]).astype(LOW)
+            return carry
+
+        lax.fori_loop(0, heads // 2, heads_pair, 0)
+
+    def cross_out():
+        wait(10)
+        states = pooled_f[0] + through(out.p_attended[...], 0)
+        out.patch_states[...] = states.astype(LOW)
+
+    down_sems = load_sems.at[6]
+    return [
+        ((0, 1, 2), embed),
+        ((), project),
+        ((), lambda: attend(0)),
+        ((3,), lambda: attend(1)),
+        ((), attention_out),
+        ((4, 5), lambda: (load(4, gate_w), load(5, up_w))),
+        ((6,), feed_forward),
+        ((), feed_out),
+        ((8, 9), cross_keys),
+        ((7, 10), cross_query),
+        ((), cross_out),
+    ]
+
+
+def fetch_kernel(dp_count, weight_count, steps_of, tokens, gram_count, used_lines, *refs):
+    shards = refs[:weight_count]
+    refs = list(refs[weight_count:])
+
+    def take(number):
+        taken = refs[:number]
+        del refs[:number]
+        return taken
+
+    ids, table = take(2)
+    extra_in = take(EXTRA_IN)
+    fulls = take(weight_count)
+    embedded, lists = take(2)
+    extra_out = take(len(Kept._fields))
+    (
+        all_ids,
+        send0,
+        p0,
+        r1a,
+        r1b,
+        r2a,
+        r2b,
+        r3,
+        g_rows,
+        core_sems,
+        stage_sems,
+        z_sems,
+        local_sems,
+        w_send,
+        w_recv,
+        id_sems,
+        places,
+        entries,
+        *extra_scratch,
+    ) = refs
+    here = Place(dp_count)
+    n = dp_count
+    z, x, y, c = here.z, here.x, here.y, here.c
+
+    class Weight:
+        def __init__(self, number, i, part, parts, kind):
+            self.i = number
+            self.kind = kind
+            rows, cols = shards[i].shape
+            self.by_cols = rows // 8 % 16 != 0
+            self.all_rows, self.count = rows, rows // parts
+            self.first = part * self.count
+            self.shard = shards[i].at[pl.ds(self.first, self.count)]
+            self.full = fulls[i]
+            self.step = (cols if self.by_cols else rows // parts) // 8
+            near, far = (x, y) if kind == 0 else (y, x)
+            self.q = (c * 2 + far) * 2 + near
+
+        def on(self, plane):
+            return self.full.at[pl.ds(plane * self.all_rows + self.first, self.count)]
+
+        def cut(self, ref, start, count):
+            span = pl.ds(start * self.step, count * self.step)
+            if self.by_cols:
+                return ref.at[:, span]
+            return ref.at[span, :]
+
+        def local(self):
+            here.send(
+                self.shard,
+                self.on(z),
+                local_sems.at[self.i, 0],
+                local_sems.at[self.i, 1],
+                here.at(dc=1),
+            )
+
+        def stage(self, k, j, start, count, src_ref, plane, peer):
+            here.send(
+                self.cut(src_ref, start, count),
+                self.cut(self.on(plane), start, count),
+                w_send.at[self.i, k, j - 1],
+                w_recv.at[self.i, k, j - 1],
+                peer,
+            )
+
+        def came(self, k, j, start, count):
+            plane = lax.rem(z + n - j, n)
+            here.expect(
+                self.cut(self.on(plane), start, count), w_recv.at[self.i, k, j - 1]
+            )
+            return plane
+
+        def along_z(self):
+            for j in range(1, n):
+                self.stage(0, j, self.q, 1, self.shard, z, here.at(dz=j))
+
+        def near(self):
+            for j in range(1, n):
+                plane = self.came(0, j, self.q, 1)
+                peer = here.at(dx=1) if self.kind == 0 else here.at(dy=1)
+                self.stage(1, j, self.q, 1, self.on(plane), plane, peer)
+
+        def far(self):
+            other = self.q + 1 - 2 * (self.q % 2)
+            for j in range(1, n):
+                plane = self.came(1, j, other, 1)
+                peer = here.at(dy=1) if self.kind == 0 else here.at(dx=1)
+                self.stage(2, j, self.q // 2 * 2, 2, self.on(plane), plane, peer)
+
+        def across(self):
+            pair = self.q // 2
+            other = pair + 1 - 2 * (pair % 2)
+            for j in range(1, n):
+                plane = self.came(2, j, other * 2, 2)
+                self.stage(3, j, c * 4, 4, self.on(plane), plane, here.at(dc=1))
+
+        def done(self):
+            for j in range(1, n):
+                self.came(3, j, (1 - c) * 4, 4)
+            here.expect(self.on(z), local_sems.at[self.i, 1])
+
+    weights = []
+    for first, second in steps_of:
+        pair = []
+        for kind, (i, part, parts) in enumerate((first, second)):
+            pair.append(Weight(2 * len(weights) + kind, i, part, parts, kind))
+        weights.append(pair)
+
+    def each(t, name):
+        if 0 <= t < len(weights):
+            for w in weights[t]:
+                name(w)
+
+    def gather_ids():
+        all_ids[z, x, y, c] = ids[...]
+        mine = all_ids.at[z, x, y, c]
+        here.send(mine, mine, id_sems.at[0, 0], id_sems.at[0, 1], here.at(dc=1))
+        here.expect(all_ids.at[z, x, y, 1 - c], id_sems.at[0, 1])
+        pair = all_ids.at[z, x, y]
+        here.send(pair, pair, id_sems.at[1, 0], id_sems.at[1, 1], here.at(dx=1))
+        here.expect(all_ids.at[z, 1 - x, y], id_sems.at[1, 1])
+        four = all_ids.at[z, :, y]
+        here.send(four, four, id_sems.at[2, 0], id_sems.at[2, 1], here.at(dy=1))
+        here.expect(all_ids.at[z, :, 1 - y], id_sems.at[2, 1])
+        plane = all_ids.at[z]
+        for j in range(1, n):
+            here.send(plane, plane, id_sems.at[2 + j, 0], id_sems.at[2 + j, 1], here.at(dz=j))
+        for j in range(1, n):
+            here.expect(all_ids.at[lax.rem(z + n - j, n)], id_sems.at[2 + j, 1])
+
+    def list_rows():
+        lines, lanes = ids.shape
+        sources = n * 8
+        total = sources * lines
+        rows_dev = table.shape[0]
+        local = all_ids[...].reshape(total, lanes) - ((z * 2 + x) * 4 + y * 2 + c) * rows_dev
+        inside = (local >= 0) & (local < rows_dev)
+        flags = jnp.where(inside, 1.0, 0.0).astype(jnp.bfloat16)
+        row = lax.broadcasted_iota(jnp.int32, (lanes, lanes), 0)
+        col = lax.broadcasted_iota(jnp.int32, (lanes, lanes), 1)
+        place = matmul(flags, jnp.where(row < col, 1.0, 0.0).astype(jnp.bfloat16))
+        held = matmul(flags, jnp.ones((lanes, lanes), jnp.bfloat16)).astype(jnp.bfloat16)
+        row = lax.broadcasted_iota(jnp.int32, (total, total), 0)
+        col = lax.broadcasted_iota(jnp.int32, (total, total), 1)
+        before = (row // lines == col // lines) & (col < row)
+        place = place + matmul(jnp.where(before, 1.0, 0.0).astype(jnp.bfloat16), held)
+        places[...] = jnp.where(inside, place.astype(jnp.int32), -1)
+        line = lax.broadcasted_iota(jnp.int32, (total, lanes), 0)
+        lane = lax.broadcasted_iota(jnp.int32, (total, lanes), 1)
+        index = lax.rem(line, lines) * lanes + lane
+        entries[...] = local * 256 + index // gram_count + 1
+        slot = lax.broadcasted_iota(jnp.int32, (SLOTS, lanes), 0)
+
+        def source(s, carry):
+            span = pl.ds(pl.multiple_of(s * lines, lines), lines)
+            where, what = places[span], entries[span]
+            found = jnp.zeros((SLOTS, lanes), jnp.int32)
+            for line in range(used_lines):
+                hit = where[line : line + 1] == slot
+                found = found + jnp.where(hit, what[line : line + 1], 0)
+            lists[s] = jnp.sum(found, axis=1, keepdims=True) - 1
+            return carry
+
+        lax.fori_loop(0, sources, source, 0)
+
+    row_iota = lax.broadcasted_iota(jnp.int32, (SLOTS, table.shape[0]), 1)
+    byte_iota = lax.broadcasted_iota(jnp.int32, (SLOTS, tokens), 1)
+
+    def partial_sums(plane, core, write):
+        for place in range(4):
+            source = plane * 8 + place * 2 + core
+            entry = lists[source]
+            pick = (jnp.right_shift(entry, 8) == row_iota).astype(jnp.bfloat16)
+            g_rows[place * SLOTS : (place + 1) * SLOTS, :] = matmul(pick, table[...]).astype(
+                jnp.bfloat16
+            )
+        for place in range(4):
+            source = plane * 8 + place * 2 + core
+            entry = lists[source]
+            to_byte = (jnp.bitwise_and(entry, 255) == byte_iota).astype(jnp.bfloat16)
+            sums = t_times(to_byte, g_rows[place * SLOTS : (place + 1) * SLOTS, :])
+            write(place, sums)
+
+    units = []
+    for u in range(n):
+        units.append(
+            Reduction(
+                here,
+                p0.at[pl.ds(u, 1)],
+                r1a.at[pl.ds(u, 1)],
+                r1b.at[pl.ds(u, 1)],
+                r2a.at[pl.ds(u, 1)],
+                r2b.at[pl.ds(u, 1)],
+                stage_sems,
+                u,
+            )
+        )
+    core_copies = [None] * n
+    z_copies = [None] * n
+
+    def plane_of(u):
+        return lax.rem(z + u + 1, n)
+
+    def hash_a(u):
+        slot = u % 2
+        if u >= 2:
+            here.sent(core_copies[u - 2])
+
+        def write(place, sums):
+            send0[slot, place // 2, place % 2] = sums.astype(jnp.bfloat16)
+
+        partial_sums(plane_of(u), 1 - c, write)
+        core_copies[u] = here.send(
+            send0.at[slot], p0.at[u], core_sems.at[u, 0], core_sems.at[u, 1], here.at(dc=1)
+        )
+
+    def hash_b(u):
+        core_copies[u].wait_recv()
+
+        def write(place, sums):
+            total = sums + p0[u, place // 2, place % 2].astype(jnp.float32)
+            p0[u, place // 2, place % 2] = total.astype(jnp.bfloat16)
+
+        partial_sums(plane_of(u), c, write)
+        units[u].first()
+
+    def hash_c(u):
+        units[u].second()
+
+    def hash_d(u):
+        mine = units[u].third()
+        if u < n - 1:
+            z_copies[u] = here.send(
+                mine.at[0], r3.at[u], z_sems.at[u, 0], z_sems.at[u, 1], here.at(dz=u + 1)
+            )
+
+    def hash_e():
+        for u in range(n - 1):
+            z_copies[u].wait_recv()
+        total = p0[n - 1, x, y].astype(jnp.float32)
+        for u in range(n - 1):
+            total = total + r3[u].astype(jnp.float32)
+        embedded[...] = total
+        for copy in core_copies[-2:] + z_copies[:-1]:
+            here.sent(copy)
+        for unit in units:
+            for copy in (unit.s1a, unit.s1b, unit.s2a, unit.s2b):
+                here.sent(copy)
+
+    here.greet()
+    for t in range(len(weights)):
+        each(t, Weight.local)
+    lead, lag1, lag2, lag3 = GATHER_LAGS
+    for t in range(lead):
+        each(t, Weight.along_z)
+    gather_ids()
+    list_rows()
+    hash_steps = []
+    for t in range(n + 3):
+        group = []
+        for u, stage in ((t, hash_a), (t - 1, hash_b), (t - 2, hash_c), (t - 3, hash_d)):
+            if 0 <= u < n:
+                group.append(lambda u=u, stage=stage: stage(u))
+        hash_steps.append(group)
+    hash_steps.append([hash_e])
+    layer = forward_steps(
+        here,
+        fulls,
+        embedded,
+        extra_in,
+        extra_out,
+        [p0.at[u] for u in range(n)] + [send0.at[u] for u in range(2)],
+        extra_scratch,
+    )
+    gather_done, runs = set(), iter(layer)
+    for what, number in SCHEDULE:
+        if what == HASH:
+            for run in hash_steps[number]:
+                run()
+        elif what == GATHER:
+            each(number + lead, Weight.along_z)
+            each(number, Weight.near)
+            each(number - lag1, Weight.far)
+            each(number - lag2, Weight.across)
+            each(number - lag3, Weight.done)
+            if 0 <= number - lag3 < len(steps_of):
+                gather_done |= {i for i, _, _ in steps_of[number - lag3]}
+        else:
+            for _ in range(number):
+                needs, run = next(runs)
+                assert gather_done.issuperset(needs)
+                run()
+    assert next(runs, None) is None
+    here.finish()
+
+
+def fetch(hash_ids, table, shards, extra, steps_of, dp_count):
+    width = table.shape[1]
+    tokens, gram_count = hash_ids.shape
+    count = len(shards)
+    hbm = pl.BlockSpec(memory_space=pl.ANY)
+    vmem = pl.BlockSpec(memory_space=pltpu.VMEM)
+    n, half = dp_count, width // 2
+    low = jnp.bfloat16
+    dma = pltpu.SemaphoreType.DMA
+    used_lines = tokens * gram_count // 128
+    lines = -(-used_lines // 8) * 8
+    ids = hash_ids.reshape(used_lines, 128)
+    ids = jnp.concatenate([ids, jnp.full((lines - used_lines, 128), -1, jnp.int32)])
+    gathers = 2 * len(steps_of)
+    ff = shards[4].shape[1]
+    extra_out = list(kept_shapes(tokens, width, ff, extra[3].shape[0]))
+    results = pl.pallas_call(
+        functools.partial(fetch_kernel, n, count, steps_of, tokens, gram_count, used_lines),
+        out_shape=[jax.ShapeDtypeStruct((n * w.shape[0], w.shape[1]), w.dtype) for w in shards]
+        + [
+            jax.ShapeDtypeStruct((tokens, width), jnp.float32),
+            jax.ShapeDtypeStruct((n * 8, SLOTS, 1), jnp.int32),
+        ]
+        + extra_out,
+        in_specs=[hbm] * count + [vmem, vmem] + [vmem] * len(extra),
+        out_specs=[hbm] * count + [vmem, vmem] + [vmem] * len(extra_out),
+        scratch_shapes=[
+            pltpu.VMEM((n, 2, 2, 2, lines, 128), jnp.int32),
+            pltpu.VMEM((2, 2, 2, tokens, width), low),
+            pltpu.VMEM((n, 2, 2, tokens, width), low),
+            pltpu.VMEM((n, 2, tokens, half), low),
+            pltpu.VMEM((n, 2, tokens, half), low),
+            pltpu.VMEM((n, tokens, half), low),
+            pltpu.VMEM((n, tokens, half), low),
+            pltpu.VMEM((n - 1, tokens, width), low),
+            pltpu.VMEM((4 * SLOTS, width), low),
+            dma((n, 2)),
+            dma((n, 4, 2)),
+            dma((n - 1, 2)),
+            dma((gathers, 2)),
+            dma((gathers, 4, n - 1)),
+            dma((gathers, 4, n - 1)),
+            dma((2 + n, 2)),
+            pltpu.VMEM((n * 8 * lines, 128), jnp.int32),
+            pltpu.VMEM((n * 8 * lines, 128), jnp.int32),
+            pltpu.VMEM((n * shards[4].shape[0], ff), low),
+            pltpu.VMEM((n * shards[5].shape[0], ff), low),
+            dma((count, max(n, ff // 256))),
+            dma((2, 2)),
+        ],
+        compiler_params=pltpu.CompilerParams(
+            collective_id=0, has_side_effects=True, vmem_limit_bytes=VMEM_CAP
+        ),
+        name="fetch",
+    )(*shards, ids, table, *extra)
+    return results[:count], results[count], results[count + 1], Kept(*results[count + 2 :])
+
+
+LAGS = (2, 3, 5)
+
+
+class GradSums:
+    def __init__(self, here, units, lefts_in, rights_in, outs, take, pool_count):
+        count = len(units)
+        self.here, self.units = here, units
+        self.lefts_in, self.rights_in, self.outs = lefts_in, rights_in, outs
+        self.lefts, self.rights = take(len(lefts_in)), take(len(rights_in))
+        self.pools = take(pool_count)
+        self.r1a, self.r1b, self.r2a, self.r2b, self.r3 = (take(count) for _ in range(5))
+        self.left_sems, self.right_sems, self.stage_sems, self.z_sems = take(4)
+        self.left_copies, self.right_copies = {}, {}
+        self.sums = [None] * count
+        self.using = {}
+        self.mine_of = [None] * count
+        self.sent_of = [None] * count
+
+    def bring(self, source, target, sems, i, split):
+        here = self.here
+        copies = []
+        theirs = target.at[0]
+        if source is not None:
+            theirs = source.at[1 - here.c] if split else source
+            mine = source.at[here.c] if split else source
+            local = pltpu.make_async_copy(mine, target.at[0], sems.at[i, 0])
+            local.start()
+            copies.append(local.wait)
+        remote = here.send(theirs, target.at[1], sems.at[i, 1], sems.at[i, 2], here.at(dc=1))
+        copies.append(remote.wait_recv)
+        return copies
+
+    def left(self, i):
+        if i not in self.left_copies:
+            self.left_copies[i] = self.bring(
+                self.lefts_in[i], self.lefts[i], self.left_sems, i, True
+            )
+
+    def right(self, i):
+        if i not in self.right_copies:
+            self.right_copies[i] = self.bring(
+                self.rights_in[i], self.rights[i], self.right_sems, i, False
+            )
+
+    def need(self, i):
+        self.left(self.units[i][0])
+        self.right(self.units[i][1])
+
+    def product(self, i):
+        here, n = self.here, self.here.n
+        left, right, pool, slot = self.units[i]
+        self.need(i)
+        for copies in (self.left_copies[left], self.right_copies[right]):
+            for wait in copies:
+                wait()
+            copies.clear()
+        for copy in self.using.get((pool, slot), []):
+            here.sent(copy)
+        p0 = self.pools[pool].at[slot]
+        xt, g = self.lefts[left], self.rights[right]
+        k, depth = xt.shape[2], xt.shape[3]
+        cols = g.shape[2]
+        chunks = 1 if k <= 32 else n
+        planes = n // chunks
+        tile = 256
+
+        def columns(t, carry):
+            span = pl.ds(pl.multiple_of(t * tile, tile), tile)
+            for chunk in range(chunks):
+                total = None
+                for who in range(2):
+                    rows = xt[who, chunk * planes * 4 : (chunk + 1) * planes * 4]
+                    part = matmul(rows.reshape(planes * 4 * k, depth), g[who, :, span])
+                    total = part if total is None else total + part
+                p0[chunk * planes : (chunk + 1) * planes, :, :, :, span] = total.astype(
+                    jnp.bfloat16
+                ).reshape(planes, 2, 2, k, tile)
+            return carry
+
+        lax.fori_loop(0, cols // tile, columns, 0)
+        unit = Reduction(
+            here, p0, self.r1a[i], self.r1b[i], self.r2a[i], self.r2b[i], self.stage_sems, i
+        )
+        unit.first()
+        self.sums[i] = unit
+        self.using[(pool, slot)] = [unit.s1a, unit.s1b]
+
+    def second(self, i):
+        self.sums[i].second()
+        self.using[self.units[i][2:]] += [self.sums[i].s2a, self.sums[i].s2b]
+
+    def third(self, i):
+        here, n = self.here, self.here.n
+        mine = self.sums[i].third()
+        self.sent_of[i] = []
+        for j in range(1, n):
+            self.sent_of[i].append(
+                here.send(
+                    mine.at[lax.rem(here.z + j, n)],
+                    self.r3[i].at[j - 1],
+                    self.z_sems.at[i, j - 1, 0],
+                    self.z_sems.at[i, j - 1, 1],
+                    here.at(dz=j),
+                )
+            )
+        self.using[self.units[i][2:]] += self.sent_of[i]
+        self.mine_of[i] = mine
+
+    def final(self, i):
+        total = self.mine_of[i][self.here.z].astype(jnp.float32)
+        for j in range(1, self.here.n):
+            self.sent_of[i][j - 1].wait_recv()
+            total = total + self.r3[i][j - 1].astype(jnp.float32)
+        self.outs[i][...] = total
+
+    def move(self, t, lags):
+        lag2, lag3, lag4 = lags
+        count = len(self.units)
+        if 0 <= t - lag2 < count:
+            self.second(t - lag2)
+        if 0 <= t - lag3 < count:
+            self.third(t - lag3)
+        if 0 <= t - lag4 < count:
+            self.final(t - lag4)
+
+
+def plan_sums(pairs, left_shapes, right_shapes, n, most):
+    low = jnp.bfloat16
+    dma = pltpu.SemaphoreType.DMA
+    shapes, units, seen = [], [], {}
+    for left, right in pairs:
+        shape = (left_shapes[left][2], right_shapes[right][1])
+        seen[shape] = seen.get(shape, 0) + 1
+        shapes.append(shape)
+    classes = list(seen)
+    slots = [min(seen[s], most) for s in classes]
+    used = {s: 0 for s in classes}
+    for (left, right), shape in zip(pairs, shapes):
+        pool = classes.index(shape)
+        units.append((left, right, pool, used[shape] % slots[pool]))
+        used[shape] += 1
+    count = len(pairs)
+    scratch = [pltpu.VMEM(shape, low) for shape in left_shapes]
+    scratch += [pltpu.VMEM((2, *shape), low) for shape in right_shapes]
+    scratch += [pltpu.VMEM((s, n, 2, 2, *shape), low) for s, shape in zip(slots, classes)]
+    halves = [(k, cols // 2) for k, cols in shapes]
+    for _ in range(2):
+        scratch += [pltpu.VMEM((n, 2, *half), low) for half in halves]
+    for _ in range(2):
+        scratch += [pltpu.VMEM((n, *half), low) for half in halves]
+    scratch += [pltpu.VMEM((n - 1, *shape), low) for shape in shapes]
+    scratch += [
+        dma((len(left_shapes), 3)),
+        dma((len(right_shapes), 3)),
+        dma((count, 4, 2)),
+        dma((count, n - 1, 2)),
+    ]
+    return units, shapes, scratch, len(classes)
+
+
+def taker(refs):
+    refs = list(refs)
+
+    def take(number):
+        taken = refs[:number]
+        del refs[:number]
+        return taken
+
+    return take
+
+
+def last_kernel(dp_count, units, left_count, right_count, pool_count, *refs):
+    n = dp_count
+    count = len(units)
+    take = taker(refs)
+    lefts_in, rights_in = take(left_count), take(right_count)
+    embed_in, gains_in = take(2)
+    outs = take(count)
+    gathered, gains_out = take(2)
+    here = Place(n)
+    sums = GradSums(here, units, lefts_in, rights_in, outs, take, pool_count)
+    gain_send, gain_recv, gain_sems, own_sem, near_sems, plane_sems = take(6)
+    z, x, y, c = here.z, here.x, here.y, here.c
+
+    here.greet()
+
+    own = pltpu.make_async_copy(embed_in, gathered.at[z, x, y, c], own_sem)
+    own.start()
+    for j in range(1, n):
+        here.send(
+            embed_in,
+            gathered.at[z, x, y, c],
+            plane_sems.at[j - 1, 0],
+            plane_sems.at[j - 1, 1],
+            here.at(dz=j),
+        )
+    width = embed_in.shape[1]
+    left_half, right_half = pl.ds(0, width // 2), pl.ds(width // 2, width // 2)
+
+    def embed_near(j):
+        plane = lax.rem(z + n - j, n)
+        if j:
+            here.expect(gathered.at[plane, x, y, c], plane_sems.at[j - 1, 1])
+        else:
+            own.wait()
+        a = gathered.at[plane, x, y, c, :, left_half]
+        b = gathered.at[plane, x, y, c, :, right_half]
+        here.send(a, a, near_sems.at[j, 0, 0], near_sems.at[j, 0, 1], here.at(dx=1))
+        here.send(b, b, near_sems.at[j, 1, 0], near_sems.at[j, 1, 1], here.at(dy=1))
+
+    def embed_far(j):
+        plane = lax.rem(z + n - j, n)
+        here.expect(gathered.at[plane, 1 - x, y, c, :, left_half], near_sems.at[j, 0, 1])
+        here.expect(gathered.at[plane, x, 1 - y, c, :, right_half], near_sems.at[j, 1, 1])
+        a = gathered.at[plane, :, y, c, :, left_half]
+        b = gathered.at[plane, x, :, c, :, right_half]
+        here.send(a, a, near_sems.at[j, 2, 0], near_sems.at[j, 2, 1], here.at(dy=1))
+        here.send(b, b, near_sems.at[j, 3, 0], near_sems.at[j, 3, 1], here.at(dx=1))
+
+    def embed_across(j):
+        plane = lax.rem(z + n - j, n)
+        here.expect(gathered.at[plane, :, 1 - y, c, :, left_half], near_sems.at[j, 2, 1])
+        here.expect(gathered.at[plane, 1 - x, :, c, :, right_half], near_sems.at[j, 3, 1])
+        a = gathered.at[plane, :, :, c]
+        here.send(a, a, near_sems.at[j, 4, 0], near_sems.at[j, 4, 1], here.at(dc=1))
+
+    def embed_done(j):
+        plane = lax.rem(z + n - j, n)
+        here.expect(gathered.at[plane, :, :, 1 - c], near_sems.at[j, 4, 1])
+
+    def gains(stage):
+        if stage == 0:
+            gain_send[0] = gains_in[...]
+        elif stage <= 3:
+            here.expect(gain_recv.at[stage - 1], gain_sems.at[stage - 1, 1])
+            gain_send[stage] = gain_send[stage - 1] + gain_recv[stage - 1]
+        if stage < 3:
+            peer = (here.at(dc=1), here.at(dx=1), here.at(dy=1))[stage]
+            here.send(
+                gain_send.at[stage],
+                gain_recv.at[stage],
+                gain_sems.at[stage, 0],
+                gain_sems.at[stage, 1],
+                peer,
+            )
+        elif stage == 3:
+            for j in range(1, n):
+                here.send(
+                    gain_send.at[3],
+                    gain_recv.at[2 + j],
+                    gain_sems.at[2 + j, 0],
+                    gain_sems.at[2 + j, 1],
+                    here.at(dz=j),
+                )
+        else:
+            total = gain_send[3]
+            for j in range(1, n):
+                here.expect(gain_recv.at[2 + j], gain_sems.at[2 + j, 1])
+                total = total + gain_recv[2 + j]
+            gains_out[...] = total
+
+    for i in range(count):
+        sums.need(i)
+    for t in range(max(count + LAGS[2], n + 5)):
+        if t < count:
+            sums.product(t)
+        if t == 0:
+            embed_near(0)
+        if 0 <= t - 1 < 5:
+            gains(t - 1)
+        if 1 <= t - 2 < n:
+            embed_near(t - 2)
+        sums.move(t, LAGS)
+        if 0 <= t - 3 < n:
+            embed_far(t - 3)
+        if 0 <= t - 4 < n:
+            embed_across(t - 4)
+        if 0 <= t - 5 < n:
+            embed_done(t - 5)
+    here.finish()
+
+
+def last_sums(pairs, lefts, rights, embed_low, gains, dp_count):
+    n = dp_count
+    low = jnp.bfloat16
+    dma = pltpu.SemaphoreType.DMA
+    hbm = pl.BlockSpec(memory_space=pl.ANY)
+    vmem = pl.BlockSpec(memory_space=pltpu.VMEM)
+    units, shapes, scratch, pool_count = plan_sums(
+        pairs, [a.shape for a in lefts], [a.shape for a in rights], n, 6
+    )
+    count = len(pairs)
+    tokens, width = embed_low.shape
+    scratch += [
+        pltpu.VMEM((4, 8, width), jnp.float32),
+        pltpu.VMEM((2 + n, 8, width), jnp.float32),
+        dma((2 + n, 2)),
+        dma,
+        dma((n, 5, 2)),
+        dma((n - 1, 2)),
+    ]
+    results = pl.pallas_call(
+        functools.partial(last_kernel, n, units, len(lefts), len(rights), pool_count),
+        out_shape=[jax.ShapeDtypeStruct(shape, jnp.float32) for shape in shapes]
+        + [
+            jax.ShapeDtypeStruct((n, 2, 2, 2, tokens, width), low),
+            jax.ShapeDtypeStruct((8, width), jnp.float32),
+        ],
+        in_specs=[hbm] * (len(lefts) + len(rights)) + [vmem, vmem],
+        out_specs=[vmem] * count + [hbm, vmem],
+        scratch_shapes=scratch,
+        compiler_params=pltpu.CompilerParams(
+            collective_id=2, has_side_effects=True, vmem_limit_bytes=VMEM_CAP
+        ),
+        name="last_sums",
+    )(*lefts, *rights, embed_low, gains)
+    return results[:count], results[count], results[count + 1]
+
+
+BACK_PAIRS = ((4, 8), (3, 6), (3, 7), (2, 5), (1, 4), (0, 0), (0, 1), (0, 2), (0, 3))
+
+
+class Streamed(typing.NamedTuple):
+    gate_pre: typing.Any
+    up_pre: typing.Any
+    h_out: typing.Any
+    h_mid: typing.Any
+    embedded: typing.Any
+    key_values: typing.Any
+    w_query: typing.Any
+    w_key: typing.Any
+    w_value: typing.Any
+    w_out: typing.Any
+    w_gate: typing.Any
+    w_up: typing.Any
+    w_down: typing.Any
+    c_query: typing.Any
+    c_key: typing.Any
+    c_value: typing.Any
+    c_out: typing.Any
+    cot_patches: typing.Any
+
+
+def back_kernel(dp_count, units, pool_count, *refs):
+    n = dp_count
+    take = taker(refs)
+    lefts_in = take(5)
+    hbm = Streamed(*take(len(Streamed._fields)))
+    (cot_bytes, p_query, p_key, p_value, cross_lse, gains, starts, ends, queries, lse) = take(10)
+    outs = take(len(units))
+    grad_gains, g_attn, g_query, g_key, g_value, g_embed = take(6)
+    here = Place(n)
+    sums = GradSums(here, units, lefts_in, [None] * 8 + [hbm.cot_patches], outs, take, pool_count)
+    w, tile_pre, grad_out, grad_ffn, grad_mid, kv, halo = take(7)
+    w_sems, tile_sems, pre_sems, kv_sems, halo_sems = take(5)
+    g_gate = [sums.rights[0].at[0], sums.rights[2].at[0]]
+    g_up = [sums.rights[1].at[0], sums.rights[3].at[0]]
+    g_branch, g_pquery, g_pkey, g_pvalue, cot_patches = [ref.at[0] for ref in sums.rights[4:]]
+    tokens, width = cot_bytes.shape
+    patches = p_query.shape[0]
+    tile = 256
+    first_tiles = g_gate[0].shape[1] // tile
+    tiles = first_tiles + g_gate[1].shape[1] // tile
+    rank = (here.x * 2 + here.y) * 2 + here.c
+    lane = lax.broadcasted_iota(jnp.int32, (1, 128), 1)
+    sides = [jnp.where(lane < HD, 1.0, 0.0).astype(LOW), jnp.where(lane < HD, 0.0, 1.0).astype(LOW)]
+    byte_pos = lax.broadcasted_iota(jnp.int32, (patches, tokens), 1)
+
+    here.greet()
+
+    def load_w(slot, source):
+        copy = pltpu.make_async_copy(source, w.at[slot], w_sems.at[slot])
+        copy.start()
+        return copy
+
+    def load_pre(source):
+        copies = []
+        for b in range(width // tile):
+            copy = pltpu.make_async_copy(
+                source.at[:, pl.ds(b * tile, tile)],
+                tile_pre.at[b // 2, b % 2],
+                pre_sems.at[b],
+            )
+            copy.start()
+            copies.append(copy)
+        return copies
+
+    def pre_rows(copies):
+        for copy in copies:
+            copy.wait()
+        return jnp.concatenate([tile_pre[b // 2, b % 2] for b in range(width // tile)], axis=1)
+
+    for i in (4, 3, 2, 1, 0):
+        sums.left(i)
+    sums.right(8)
+    cross = [load_w(i, a) for i, a in enumerate((hbm.c_out, hbm.c_query, hbm.c_key, hbm.c_value))]
+    h_out_copies = load_pre(hbm.h_out)
+
+    def tile_copies(t):
+        slot = lax.rem(t, 2)
+        span = pl.ds(pl.multiple_of(t * tile, tile), tile)
+        return [
+            pltpu.make_async_copy(source, target, tile_sems.at[slot, k])
+            for k, (source, target) in enumerate(
+                (
+                    (hbm.w_gate.at[:, span], w.at[slot, :, pl.ds(0, tile)]),
+                    (hbm.w_up.at[:, span], w.at[slot, :, pl.ds(tile, tile)]),
+                    (hbm.w_down.at[span], w.at[2, pl.ds(pl.multiple_of(slot * tile, tile), tile)]),
+                    (hbm.gate_pre.at[:, span], tile_pre.at[slot, 0]),
+                    (hbm.up_pre.at[:, span], tile_pre.at[slot, 1]),
+                )
+            )
+        ]
+
+    def member():
+        return (byte_pos >= starts[...]) & (byte_pos < ends[...])
+
+    def head_lse(ref, head):
+        return jnp.sum(jnp.where(lane == head, ref[...], 0.0), axis=1, keepdims=True)
+
+    def cross_heads():
+        cross[0].wait()
+        allowed = member()
+        grad_ffn[:patches] = times_t(cot_patches[...], w[0]).astype(LOW).astype(F32)
+
+        def heads_pair(pair, carry):
+            span = pl.ds(pl.multiple_of(pair * 128, 128), 128)
+            q2, k2, v2 = p_query[:, span], p_key[:, span], p_value[:, span]
+            gp2 = grad_ffn[:patches, span].astype(LOW)
+            parts = []
+            for side in range(2):
+                total = head_lse(cross_lse, pair * 2 + side)
+                scores = times_t(q2 * sides[side], k2) * SCORE_SCALE
+                probs = jnp.where(allowed, jnp.exp(jnp.where(allowed, scores, total) - total), 0.0)
+                grad_score = soft_back(probs, times_t(gp2 * sides[side], v2))
+                parts.append(
+                    (
+                        matmul(grad_score, k2),
+                        t_times(grad_score, q2),
+                        t_times(probs.astype(LOW), gp2),
+                    )
+                )
+            mine = lane < HD
+            g_pquery[:, span] = (jnp.where(mine, parts[0][0], parts[1][0]) * SCORE_SCALE).astype(LOW)
+            g_pkey[:, span] = (jnp.where(mine, parts[0][1], parts[1][1]) * SCORE_SCALE).astype(LOW)
+            g_pvalue[:, span] = jnp.where(mine, parts[0][2], parts[1][2]).astype(LOW)
+            return carry
+
+        lax.fori_loop(0, width // 128, heads_pair, 0)
+        for i in (5, 6, 7):
+            sums.right(i)
+
+    def split(v):
+        high = v.astype(LOW)
+        return high, (v - high.astype(F32)).astype(LOW)
+
+    def unit_of(v):
+        inv_rms = lax.rsqrt(jnp.mean(v * v, axis=-1, keepdims=True) + EPSILON)
+        return v * inv_rms, inv_rms
+
+    def through_norm(grad, rows, number):
+        normed, inv_rms = unit_of(rows)
+        grad_in, grad_gain = norm_back(
+            grad.astype(LOW).astype(F32), normed, inv_rms, gains[number : number + 1]
+        )
+        grad_gains[number : number + 1] = grad_gain[None]
+        return grad_in
+
+    loaded = {}
+
+    def cross_in():
+        for copy in cross[1:]:
+            copy.wait()
+        length = (ends[...] - starts[...]).astype(F32)
+        grad_pooled = cot_patches[...].astype(F32) + times_t(g_pquery[...], w[1]).astype(
+            LOW
+        ).astype(F32)
+        high, rest = split(grad_pooled / length)
+        inside = jnp.where(member(), 1.0, 0.0).astype(LOW)
+        grad_x = t_times(inside, high) + t_times(inside, rest)
+        grad_x = grad_x + times_t(g_pkey[...], w[2]) + times_t(g_pvalue[...], w[3])
+        grad_gains[...] = jnp.zeros_like(grad_gains)
+        total = cot_bytes[...].astype(F32) + through_norm(grad_x, pre_rows(h_out_copies), 2)
+        grad_out[...] = total
+        g_branch[...] = total.astype(LOW)
+        grad_ffn[...] = jnp.zeros_like(grad_ffn)
+        sums.right(4)
+        loaded[3] = load_w(3, hbm.w_out)
+
+    def feed(part):
+        first, last = ((0, first_tiles), (first_tiles, tiles))[part]
+        for copy in tile_copies(first):
+            copy.start()
+
+        def one(t, carry):
+            slot = lax.rem(t, 2)
+            for copy in tile_copies(t):
+                copy.wait()
+
+            @pl.when(t + 1 < last)
+            def _():
+                for copy in tile_copies(t + 1):
+                    copy.start()
+
+            span = pl.ds(pl.multiple_of((t - first) * tile, tile), tile)
+            down_rows = w[2, pl.ds(pl.multiple_of(slot * tile, tile), tile)]
+            grad_hidden = times_t(g_branch[...], down_rows).astype(LOW).astype(F32)
+            gate, up = tile_pre[slot, 0], tile_pre[slot, 1]
+            sig = jax.nn.sigmoid(gate)
+            gg = (grad_hidden * up * sig * (1.0 + gate * (1.0 - sig))).astype(LOW)
+            gu = (grad_hidden * (gate * sig)).astype(LOW)
+            g_gate[part][:, span] = gg
+            g_up[part][:, span] = gu
+            grad_ffn[...] += times_t(gg, w[slot, :, :tile]) + times_t(
+                gu, w[slot, :, tile : 2 * tile]
+            )
+            return carry
+
+        lax.fori_loop(first, last, one, 0)
+        sums.right(2 * part)
+        sums.right(2 * part + 1)
+
+    def feed_in():
+        copies = load_pre(hbm.h_mid)
+        loaded[3].wait()
+        grad_mid[...] = grad_out[...] + through_norm(grad_ffn[...], pre_rows(copies), 1)
+        g_attn[...] = grad_mid[...].astype(LOW)
+        g_query[...] = times_t(g_attn[...], w[3]).astype(LOW)
+        loaded[1] = load_w(1, hbm.w_query)
+        loaded[2] = load_w(2, hbm.w_key)
+        loaded[3] = load_w(3, hbm.w_value)
+        loaded[0] = load_pre(hbm.embedded)
+
+    own_key, own_value = grad_ffn, grad_out
+    sent = w.at[0]
+
+    def kv_copy(pair):
+        slot = lax.rem(pair, 2)
+        span = pl.ds(pl.multiple_of(pair * 128, 128), 128)
+        return pltpu.make_async_copy(hbm.key_values.at[:, :, span], kv.at[slot], kv_sems.at[slot])
+
+    def attend(first, last):
+        row = lax.broadcasted_iota(jnp.int32, (tokens, tokens), 0)
+        col = lax.broadcasted_iota(jnp.int32, (tokens, tokens), 1)
+        mine = col <= row
+        far_bias = jnp.where(rank >= 2, 0.0, NEG_BIG)
+        near_bias = jnp.where(rank >= 1, 0.0, NEG_BIG)
+        kv_copy(first).start()
+
+        def three(edge, middle):
+            return jnp.concatenate(
+                [
+                    jnp.where(mine, 0.0, edge).astype(LOW),
+                    middle.astype(LOW),
+                    jnp.where(mine, edge, 0.0).astype(LOW),
+                ],
+                axis=1,
+            )
+
+        def heads_pair(pair, carry):
+            kv_copy(pair).wait()
+
+            @pl.when(pair + 1 < last)
+            def _():
+                kv_copy(pair + 1).start()
+
+            slot = lax.rem(pair, 2)
+            span = pl.ds(pl.multiple_of(pair * 128, 128), 128)
+            q2, ga2 = queries[:, span], g_query[:, span]
+            k2, v2 = kv[slot, 0], kv[slot, 1]
+            parts = []
+            for side in range(2):
+                total = head_lse(lse, pair * 2 + side)
+                scores = times_t(q2 * sides[side], k2) * SCORE_SCALE
+                edge = jnp.where(mine, scores[:, 2 * tokens :], scores[:, :tokens] + far_bias)
+                edge = jnp.exp(edge - total)
+                middle = jnp.exp(scores[:, tokens : 2 * tokens] + near_bias - total)
+                grad_prob = times_t(ga2 * sides[side], v2)
+                grad_edge = jnp.where(mine, grad_prob[:, 2 * tokens :], grad_prob[:, :tokens])
+                grad_middle = grad_prob[:, tokens : 2 * tokens]
+                row_total = jnp.sum(edge * grad_edge, axis=1, keepdims=True) + jnp.sum(
+                    middle * grad_middle, axis=1, keepdims=True
+                )
+                grad_score = three(edge * (grad_edge - row_total), middle * (grad_middle - row_total))
+                parts.append(
+                    (
+                        matmul(grad_score, k2),
+                        t_times(grad_score, q2),
+                        t_times(three(edge, middle), ga2),
+                    )
+                )
+            left = lane < HD
+            g_query[:, span] = (jnp.where(left, parts[0][0], parts[1][0]) * SCORE_SCALE).astype(LOW)
+            for number, own, scale in ((1, own_key, SCORE_SCALE), (2, own_value, 1.0)):
+                grad = jnp.where(left, parts[0][number], parts[1][number]) * scale
+                own[:, span] = grad[2 * tokens :]
+                start = (number - 1) * 2 * tokens
+                sent[start : start + 2 * tokens, span] = grad[: 2 * tokens].astype(LOW)
+            return carry
+
+        lax.fori_loop(first, last, heads_pair, 0)
+
+    def halo_send():
+        for back in (1, 2):
+            target = rank - back
+            for number in range(2):
+                here.send_if(
+                    target >= 0,
+                    sent.at[pl.ds((2 * number + 2 - back) * tokens, tokens)],
+                    halo.at[back - 1, number],
+                    halo_sems.at[back - 1, number, 0],
+                    halo_sems.at[back - 1, number, 1],
+                    (here.z, jnp.maximum(target, 0) // 4, lax.rem(jnp.maximum(target, 0), 4)),
+                )
+
+    def halo_add():
+        for back in (1, 2):
+
+            @pl.when(rank + back < 8)
+            def _():
+                for number, own in ((0, own_key), (1, own_value)):
+                    here.expect(halo.at[back - 1, number], halo_sems.at[back - 1, number, 1])
+                    own[...] += halo[back - 1, number].astype(F32)
+
+        g_key[...] = own_key[...].astype(LOW)
+        g_value[...] = own_value[...].astype(LOW)
+
+    def embed_in():
+        for slot in (1, 2, 3):
+            loaded[slot].wait()
+        grad = times_t(g_query[...], w[1]) + times_t(g_key[...], w[2]) + times_t(g_value[...], w[3])
+        total = grad_mid[...] + through_norm(grad, pre_rows(loaded[0]), 0)
+        g_embed[...] = total.astype(LOW)
+
+    sums.product(0)
+    cross_heads()
+    sums.product(1)
+    sums.product(2)
+    sums.product(3)
+    cross_in()
+    sums.second(0)
+    sums.product(4)
+    sums.second(1)
+    feed(0)
+    sums.product(5)
+    sums.product(6)
+    sums.second(2)
+    sums.third(0)
+    feed(1)
+    sums.product(7)
+    sums.product(8)
+    sums.second(3)
+    sums.third(1)
+    feed_in()
+    sums.second(4)
+    sums.third(2)
+    pairs = width // 128
+    attend(0, pairs // 2)
+    sums.second(5)
+    sums.third(3)
+    attend(pairs // 2, pairs)
+    halo_send()
+    sums.second(6)
+    sums.third(4)
+    for i in range(4):
+        sums.final(i)
+    halo_add()
+    sums.second(7)
+    sums.third(5)
+    embed_in()
+    sums.second(8)
+    sums.third(6)
+    sums.third(7)
+    sums.third(8)
+    for i in range(4, 9):
+        sums.final(i)
+    here.finish()
+
+
+def back_sums(lefts, streamed, kept, dp_count):
+    n = dp_count
+    low = jnp.bfloat16
+    dma = pltpu.SemaphoreType.DMA
+    hbm = pl.BlockSpec(memory_space=pl.ANY)
+    vmem = pl.BlockSpec(memory_space=pltpu.VMEM)
+    tokens, ff = streamed.gate_pre.shape
+    patches, width = streamed.cot_patches.shape
+    tile = 256
+    first = (ff // tile + 1) // 2 * tile
+    one = jax.ShapeDtypeStruct
+    right_shapes = [(tokens, first)] * 2 + [(tokens, ff - first)] * 2
+    right_shapes += [(tokens, width), (patches, width)]
+    right_shapes += [(tokens, width)] * 2 + [(patches, width)]
+    units, shapes, scratch, pool_count = plan_sums(
+        BACK_PAIRS, [a.shape for a in lefts], right_shapes, n, 4
+    )
+    count = len(units)
+    scratch += [
+        pltpu.VMEM((4, width, width), low),
+        pltpu.VMEM((2, 2, tokens, tile), F32),
+        pltpu.VMEM((tokens, width), F32),
+        pltpu.VMEM((tokens, width), F32),
+        pltpu.VMEM((tokens, width), F32),
+        pltpu.VMEM((2, 2, 3 * tokens, 128), low),
+        pltpu.VMEM((2, 2, tokens, width), low),
+        dma((4,)),
+        dma((2, 5)),
+        dma((width // tile,)),
+        dma((2,)),
+        dma((2, 2, 2)),
+    ]
+    results = pl.pallas_call(
+        functools.partial(back_kernel, n, units, pool_count),
+        out_shape=[one(shape, F32) for shape in shapes]
+        + [one((8, width), F32)]
+        + [one((tokens, width), low)] * 5,
+        in_specs=[hbm] * (len(lefts) + len(streamed)) + [vmem] * len(kept),
+        out_specs=[vmem] * (count + 6),
+        scratch_shapes=scratch,
+        compiler_params=pltpu.CompilerParams(
+            collective_id=1, has_side_effects=True, vmem_limit_bytes=63 * 1024 * 1024
+        ),
+        name="back_sums",
+    )(*lefts, *streamed, *kept)
+    return results[:count], results[count:]
+
+
+def spread_kernel(lists, rows_of, grads, out, counts, stacked):
+    step = pl.program_id(0)
+    group, tokens = grads.shape[0], grads.shape[1]
+
+    @pl.when(step == 0)
+    def _():
+        out[...] = jnp.zeros_like(out)
+        counts[...] = jnp.zeros_like(counts)
+
+    byte_iota = lax.broadcasted_iota(jnp.int32, (SLOTS, tokens), 1)
+    for s in range(group):
+        pick = (jnp.bitwise_and(lists[s], 255) == byte_iota).astype(jnp.bfloat16)
+        stacked[s * SLOTS : (s + 1) * SLOTS, :] = matmul(pick, grads[s]).astype(jnp.bfloat16)
+    row_iota = lax.broadcasted_iota(jnp.int32, (out.shape[0], group * SLOTS), 0)
+    onto = (rows_of[0] == row_iota).astype(jnp.float32)
+    counts[...] += jnp.sum(onto, axis=1, keepdims=True)
+    out[...] += matmul(onto.astype(jnp.bfloat16), stacked[...])
+
+
+def spread(entries, gathered, rows_dev):
+    sources, tokens, width = gathered.shape
+    group = 8
+    steps = sources // group
+    rows_of = jnp.right_shift(entries, 8).reshape(steps, 1, group * SLOTS)
+    out, counts = pl.pallas_call(
+        spread_kernel,
+        grid=(steps,),
+        out_shape=[
+            jax.ShapeDtypeStruct((rows_dev, width), jnp.float32),
+            jax.ShapeDtypeStruct((rows_dev, 1), jnp.float32),
+        ],
+        in_specs=[
+            pl.BlockSpec((group, SLOTS, 1), lambda i: (i, 0, 0)),
+            pl.BlockSpec((1, 1, group * SLOTS), lambda i: (i, 0, 0)),
+            pl.BlockSpec((group, tokens, width), lambda i: (i, 0, 0)),
+        ],
+        out_specs=[
+            pl.BlockSpec((rows_dev, width), lambda i: (0, 0)),
+            pl.BlockSpec((rows_dev, 1), lambda i: (0, 0)),
+        ],
+        scratch_shapes=[pltpu.VMEM((group * SLOTS, width), jnp.bfloat16)],
+        compiler_params=pltpu.CompilerParams(vmem_limit_bytes=VMEM_CAP),
+        name="spread",
+    )(entries, rows_of, gathered)
+    return out, counts[:, 0].astype(jnp.int32)
+
+
+WEIGHT_STEPS = tuple(((i, 0, 2), (i, 1, 2)) for i in (0, 1, 2, 3, 4, 5, 6, 8, 9, 7, 10))
+
+
+def by_rows(a, dp_count):
+    depth, total = a.shape
+    pairs = dp_count * 4
+    both = total // pairs
+    a = a.T.reshape(pairs, both, depth)
+    rows = -(-(both // 2) // 16) * 16
+    return jnp.stack([a[:, :rows], a[:, both - rows :]])
+
+
+def own_rows(block, rows):
+    core = lax.axis_index(SUB) % 2
+    return jnp.where(core == 0, block[:rows], block[block.shape[0] - rows :])
 
 
 def body(
@@ -102,11 +1758,11 @@
     cot_bytes,
     cot_patches,
 ):
-    dp_count = lax.axis_size("dp")
-    rs_count = lax.axis_size(("rep", "sub"))
+    dp_count = lax.axis_size(DP)
+    rs_count = lax.axis_size(SEQ)
     all_count = dp_count * rs_count
-    rank_seq = lax.axis_index(("rep", "sub"))
-    rank_table = lax.axis_index("dp") * rs_count + rank_seq
+    rank_seq = lax.axis_index(SEQ)
+    rank_table = lax.axis_index(DP) * rs_count + rank_seq
     tokens, gram_count = hash_ids.shape
     rows_dev, model_width = hash_table.shape
     head_count = model_width // HD
@@ -130,8 +1786,8 @@
     requests = jnp.full((all_count * slot_count,), -1, jnp.int32).at[placement].set(flat_ids)
     requests = requests.reshape(dp_count, rs_count, slot_count)
     incoming = lax.all_to_all(
-        lax.all_to_all(requests, "dp", split_axis=0, concat_axis=0, tiled=True),
-        ("rep", "sub"),
+        lax.all_to_all(requests, DP, split_axis=0, concat_axis=0, tiled=True),
+        SEQ,
         split_axis=1,
         concat_axis=1,
         tiled=True,
@@ -140,8 +1796,8 @@
     safe_rows = jnp.where(present, incoming - rank_table * rows_dev, 0)
     served = jnp.where(present[..., None], hash_table[safe_rows], jnp.zeros((), jnp.bfloat16))
     returned = lax.all_to_all(
-        lax.all_to_all(served, "dp", split_axis=0, concat_axis=0, tiled=True),
-        ("rep", "sub"),
+        lax.all_to_all(served, DP, split_axis=0, concat_axis=0, tiled=True),
+        SEQ,
         split_axis=1,
         concat_axis=1,
         tiled=True,
@@ -169,17 +1825,17 @@
         c_out,
     )
     gathered = (
-        lax.all_gather(weight_list[0], "dp", axis=0, tiled=True),
-        lax.all_gather(weight_list[1], "dp", axis=0, tiled=True),
-        lax.all_gather(weight_list[2], "dp", axis=0, tiled=True),
-        lax.all_gather(weight_list[3], "dp", axis=0, tiled=True),
-        lax.all_gather(weight_list[4], "dp", axis=0, tiled=True),
-        lax.all_gather(weight_list[5], "dp", axis=0, tiled=True),
-        lax.all_gather(weight_list[6], "dp", axis=0, tiled=True),
-        lax.all_gather(weight_list[7], "dp", axis=0, tiled=True),
-        lax.all_gather(weight_list[8], "dp", axis=0, tiled=True),
-        lax.all_gather(weight_list[9], "dp", axis=0, tiled=True),
-        lax.all_gather(weight_list[10], "dp", axis=0, tiled=True),
+        lax.all_gather(weight_list[0], DP, axis=0, tiled=True),
+        lax.all_gather(weight_list[1], DP, axis=0, tiled=True),
+        lax.all_gather(weight_list[2], DP, axis=0, tiled=True),
+        lax.all_gather(weight_list[3], DP, axis=0, tiled=True),
+        lax.all_gather(weight_list[4], DP, axis=0, tiled=True),
+        lax.all_gather(weight_list[5], DP, axis=0, tiled=True),
+        lax.all_gather(weight_list[6], DP, axis=0, tiled=True),
+        lax.all_gather(weight_list[7], DP, axis=0, tiled=True),
+        lax.all_gather(weight_list[8], DP, axis=0, tiled=True),
+        lax.all_gather(weight_list[9], DP, axis=0, tiled=True),
+        lax.all_gather(weight_list[10], DP, axis=0, tiled=True),
     )
     (
         full_query,
@@ -202,7 +1858,7 @@
     key_parts = []
     value_parts = []
     for offset_back in range(behind, 0, -1):
-        far_keys, far_values = passed_along((key_rows, value_rows), ("rep", "sub"), offset_back)
+        far_keys, far_values = passed_along((key_rows, value_rows), SEQ, offset_back)
         key_parts.append(far_keys)
         value_parts.append(far_values)
     all_keys = jnp.concatenate(key_parts + [key_rows], axis=0)
@@ -379,14 +2035,14 @@
         far_grad_k, far_grad_v = (
             passed_along(
                 grad_keys_all[part_index * tokens : (part_index + 1) * tokens].astype(jnp.bfloat16),
-                ("rep", "sub"),
+                SEQ,
                 -offset_back,
             ).astype(jnp.float32),
             passed_along(
                 grad_values_all[part_index * tokens : (part_index + 1) * tokens].astype(
                     jnp.bfloat16
                 ),
-                ("rep", "sub"),
+                SEQ,
                 -offset_back,
             ).astype(jnp.float32),
         )
@@ -420,9 +2076,9 @@
     outgoing = outgoing.reshape(dp_count, rs_count, slot_count, model_width)
     arrived = lax.all_to_all(
         lax.all_to_all(
-            outgoing.astype(jnp.bfloat16), "dp", split_axis=0, concat_axis=0, tiled=True
+            outgoing.astype(jnp.bfloat16), DP, split_axis=0, concat_axis=0, tiled=True
         ),
-        ("rep", "sub"),
+        SEQ,
         split_axis=1,
         concat_axis=1,
         tiled=True,
@@ -433,21 +2089,21 @@
         .add(jnp.where(present[..., None], arrived, 0.0).reshape(-1, model_width))
     )
     summed_all = (
-        lax.psum_scatter(grad_norm_attn, ("dp", "rep", "sub"), scatter_dimension=0, tiled=True),
-        lax.psum_scatter(grad_norm_ffn, ("dp", "rep", "sub"), scatter_dimension=0, tiled=True),
-        lax.psum_scatter(grad_norm_cross, ("dp", "rep", "sub"), scatter_dimension=0, tiled=True),
-        lax.psum_scatter(grad_w_query, ("dp", "rep", "sub"), scatter_dimension=0, tiled=True),
-        lax.psum_scatter(grad_w_key, ("dp", "rep", "sub"), scatter_dimension=0, tiled=True),
-        lax.psum_scatter(grad_w_value, ("dp", "rep", "sub"), scatter_dimension=0, tiled=True),
-        lax.psum_scatter(grad_w_out, ("dp", "rep", "sub"), scatter_dimension=0, tiled=True),
-        lax.psum_scatter(grad_w_gate, ("dp", "rep", "sub"), scatter_dimension=0, tiled=True),
-        lax.psum_scatter(grad_w_up, ("dp", "rep", "sub"), scatter_dimension=0, tiled=True),
-        lax.psum_scatter(grad_w_down, ("dp", "rep", "sub"), scatter_dimension=0, tiled=True),
-        lax.psum_scatter(grad_c_query, ("dp", "rep", "sub"), scatter_dimension=0, tiled=True),
-        lax.psum_scatter(grad_c_key, ("dp", "rep", "sub"), scatter_dimension=0, tiled=True),
-        lax.psum_scatter(grad_c_value, ("dp", "rep", "sub"), scatter_dimension=0, tiled=True),
-        lax.psum_scatter(grad_c_out, ("dp", "rep", "sub"), scatter_dimension=0, tiled=True),
-        lax.psum_scatter(grad_byte_table, ("dp", "rep", "sub"), scatter_dimension=0, tiled=True),
+        lax.psum_scatter(grad_norm_attn, ALL, scatter_dimension=0, tiled=True),
+        lax.psum_scatter(grad_norm_ffn, ALL, scatter_dimension=0, tiled=True),
+        lax.psum_scatter(grad_norm_cross, ALL, scatter_dimension=0, tiled=True),
+        lax.psum_scatter(grad_w_query, ALL, scatter_dimension=0, tiled=True),
+        lax.psum_scatter(grad_w_key, ALL, scatter_dimension=0, tiled=True),
+        lax.psum_scatter(grad_w_value, ALL, scatter_dimension=0, tiled=True),
+        lax.psum_scatter(grad_w_out, ALL, scatter_dimension=0, tiled=True),
+        lax.psum_scatter(grad_w_gate, ALL, scatter_dimension=0, tiled=True),
+        lax.psum_scatter(grad_w_up, ALL, scatter_dimension=0, tiled=True),
+        lax.psum_scatter(grad_w_down, ALL, scatter_dimension=0, tiled=True),
+        lax.psum_scatter(grad_c_query, ALL, scatter_dimension=0, tiled=True),
+        lax.psum_scatter(grad_c_key, ALL, scatter_dimension=0, tiled=True),
+        lax.psum_scatter(grad_c_value, ALL, scatter_dimension=0, tiled=True),
+        lax.psum_scatter(grad_c_out, ALL, scatter_dimension=0, tiled=True),
+        lax.psum_scatter(grad_byte_table, ALL, scatter_dimension=0, tiled=True),
     )
     (
         out_norm_attn,
@@ -490,54 +2146,190 @@
     )
 
 
+def fast_body(
+    byte_ids,
+    hash_ids,
+    lengths,
+    byte_table,
+    hash_table,
+    norm_attn,
+    norm_ffn,
+    norm_cross,
+    w_query,
+    w_key,
+    w_value,
+    w_out,
+    w_gate,
+    w_up,
+    w_down,
+    c_query,
+    c_key,
+    c_value,
+    c_out,
+    cot_bytes,
+    cot_patches,
+):
+    dp_count = lax.axis_size(DP)
+    rs_count = lax.axis_size(SEQ)
+    all_count = dp_count * rs_count
+    rank_table = lax.axis_index(ALL)
+    tokens = hash_ids.shape[0]
+    rows_dev, model_width = hash_table.shape
+    patch_len = lengths[0]
+    patch_end = jnp.cumsum(patch_len)[:, None]
+    patch_start = patch_end - patch_len[:, None]
+    gains = jnp.concatenate(
+        [norm_attn[None], norm_ffn[None], norm_cross[None], jnp.zeros((5, model_width), jnp.float32)]
+    )
+    full, embedded, entries, kept = fetch(
+        hash_ids,
+        hash_table,
+        (
+            w_query,
+            w_key,
+            w_value,
+            w_out,
+            w_gate,
+            w_up,
+            w_down,
+            c_query,
+            c_key,
+            c_value,
+            c_out,
+        ),
+        (byte_ids[:, None], byte_table, gains, patch_start, patch_end),
+        WEIGHT_STEPS,
+        dp_count,
+    )
+    lefts = [
+        by_rows(a, dp_count)
+        for a in (kept.x_ffn, kept.hidden, kept.pooled, kept.x_cross, kept.p_attended)
+    ]
+    sums, results = back_sums(
+        lefts,
+        Streamed(
+            kept.gate_pre,
+            kept.up_pre,
+            kept.h_out,
+            kept.h_mid,
+            embedded,
+            kept.key_values,
+            *full,
+            cot_patches,
+        ),
+        (
+            cot_bytes,
+            kept.p_query,
+            kept.p_key,
+            kept.p_value,
+            kept.cross_lse,
+            gains,
+            patch_start,
+            patch_end,
+            kept.queries,
+            kept.lse,
+        ),
+        dp_count,
+    )
+    out_cout, out_ckey, out_cvalue, out_cquery, down_rows = sums[:5]
+    out_gate = jnp.concatenate([sums[5], sums[7]], axis=1)
+    out_up = jnp.concatenate([sums[6], sums[8]], axis=1)
+    gain_rows, grad_branch_a, grad_queries, grad_keys, grad_values, embed_grad = results
+    one_hot = byte_ids[:, None] == jnp.arange(BYTE_VALUES, dtype=jnp.int32)[None, :]
+    lefts = [
+        by_rows(a, dp_count) for a in (kept.x_attn, kept.attended, one_hot.astype(jnp.bfloat16))
+    ]
+    rights = [grad_queries, grad_keys, grad_values, grad_branch_a, embed_grad]
+    sums, all_embed, gain_sums = last_sums(
+        [(1, 3), (0, 0), (0, 1), (0, 2), (2, 4)],
+        lefts,
+        rights,
+        embed_grad,
+        gain_rows,
+        dp_count,
+    )
+    out_proj, out_query, out_key, out_value, byte_rows = sums
+    out_down = own_rows(down_rows, kept.hidden.shape[1] // all_count)
+    out_bytes = own_rows(byte_rows, BYTE_VALUES // all_count)
+    hash_table_grad, row_counts = spread(
+        entries, all_embed.reshape(all_count, tokens, model_width), rows_dev
+    )
+    own_gains = lax.dynamic_slice_in_dim(
+        gain_sums, rank_table * (model_width // all_count), model_width // all_count, 1
+    )
+    return (
+        kept.byte_states,
+        kept.patch_states,
+        embed_grad,
+        out_bytes,
+        hash_table_grad,
+        row_counts,
+        own_gains[0],
+        own_gains[1],
+        own_gains[2],
+        out_query,
+        out_key,
+        out_value,
+        out_proj,
+        out_gate,
+        out_up,
+        out_down,
+        out_cquery,
+        out_ckey,
+        out_cvalue,
+        out_cout,
+    )
+
+
 def solution(mesh):
+    fits = mesh.shape[REP] == 2 and mesh.shape[SUB] == 4 and mesh.shape[DP] <= 4
     return jax.shard_map(
-        body,
+        fast_body if fits else body,
         mesh=mesh,
         in_specs=(
-            P(("dp", "rep", "sub")),
-            P(("dp", "rep", "sub"), None),
-            P(("dp", "rep", "sub"), None),
+            P(ALL),
+            P(ALL, None),
+            P(ALL, None),
             P(),
-            P(("dp", "rep", "sub"), None),
+            P(ALL, None),
             P(),
             P(),
             P(),
-            P("dp", None),
-            P("dp", None),
-            P("dp", None),
-            P("dp", None),
-            P("dp", None),
-            P("dp", None),
-            P("dp", None),
-            P("dp", None),
-            P("dp", None),
-            P("dp", None),
-            P("dp", None),
-            P(("dp", "rep", "sub"), None),
-            P(("dp", "rep", "sub"), None),
+            P(DP, None),
+            P(DP, None),
+            P(DP, None),
+            P(DP, None),
+            P(DP, None),
+            P(DP, None),
+            P(DP, None),
+            P(DP, None),
+            P(DP, None),
+            P(DP, None),
+            P(DP, None),
+            P(ALL, None),
+            P(ALL, None),
         ),
         out_specs=(
-            P(("dp", "rep", "sub"), None),
-            P(("dp", "rep", "sub"), None),
-            P(("dp", "rep", "sub"), None),
-            P(("dp", "rep", "sub"), None),
-            P(("dp", "rep", "sub"), None),
-            P(("dp", "rep", "sub")),
-            P(("dp", "rep", "sub")),
-            P(("dp", "rep", "sub")),
-            P(("dp", "rep", "sub")),
-            P(("dp", "rep", "sub"), None),
-            P(("dp", "rep", "sub"), None),
-            P(("dp", "rep", "sub"), None),
-            P(("dp", "rep", "sub"), None),
-            P(("dp", "rep", "sub"), None),
-            P(("dp", "rep", "sub"), None),
-            P(("dp", "rep", "sub"), None),
-            P(("dp", "rep", "sub"), None),
-            P(("dp", "rep", "sub"), None),
-            P(("dp", "rep", "sub"), None),
-            P(("dp", "rep", "sub"), None),
+            P(ALL, None),
+            P(ALL, None),
+            P(ALL, None),
+            P(ALL, None),
+            P(ALL, None),
+            P(ALL),
+            P(ALL),
+            P(ALL),
+            P(ALL),
+            P(ALL, None),
+            P(ALL, None),
+            P(ALL, None),
+            P(ALL, None),
+            P(ALL, None),
+            P(ALL, None),
+            P(ALL, None),
+            P(ALL, None),
+            P(ALL, None),
+            P(ALL, None),
+            P(ALL, None),
         ),
         check_vma=False,
     )

time: 2670 us -> 670 us (0.25)
  waiting for transfers between devices: 1940 us -> 0 us
  Pallas kernels: 0 us -> 626 us
  blocking collectives: 273 us -> 0 us
  matrix products: 136 us -> 0 us
  local copies, waits for them, and re-layouts: 130 us -> 17.7 us
  other arithmetic: 122 us -> 14.9 us
  starting transfers between devices: 38.2 us -> 0 us
    reduce_scatter x12 -> x0, waiting for transfers between devices: 1340 us -> none  [the longest x1 156 us: body(): lax.psum_scatter(grad_w_gate, ('dp', 'rep', 'sub'), scatter_dimension=0,...]
    pallas_call x0 -> x4, Pallas kernels: none -> 626 us  [the longest x1 303 us: fetch(): pl.pallas_call(functools.partial(fetch_kernel, n, count, steps_of, tokens...]
    all_gather x11 -> x0, waiting for transfers between devices: 294 us -> none  [the longest x1 99.4 us: body(): lax.all_gather(weight_list[6], 'dp', axis=0, tiled=True)]
    all_to_all x4 -> x0, waiting for transfers between devices: 291 us -> none  [the longest x1 222 us: body(): lax.all_to_all(served, 'dp', split_axis=0, concat_axis=0, tiled=True)]
    all_to_all x2 -> x0, blocking collectives: 170 us -> none  [the longest x1 158 us: body(): lax.all_to_all(outgoing.astype(jnp.bfloat16), 'dp', split_axis=0, concat_...]
    dot_general x49 -> x0, matrix products: 136 us -> none  [the longest x11 40.8 us: t_times(): lax.dot_general(matrix_a, matrix_b, (((0,), (0,)), ((), ())), preferred_e...]
    unnamed x1 -> x0, blocking collectives: 103 us -> none
    scatter-add x2 -> x0, other arithmetic: 48.7 us -> none  [the longest x1 31.4 us: body(): hash_table_grad = jnp.zeros((rows_dev, model_width), jnp.float32).at[safe...]
  transfers between devices with their start and end apart: 35 -> 0, of which waited for: 20 -> 0; matrix products, arithmetic and copies ran while one was open for 12% -> 0% of each run, Pallas kernels for 0% -> 0%
where the time goes in v2:
time: 670 us; the launch traced here: 660 us
  Pallas kernels  626 us (93%)
  local copies, waits for them, and re-layouts  17.7 us (3%)
  other arithmetic  14.9 us (2%)
    pallas_call x1, Pallas kernels, fetch(): pl.pallas_call(functools.partial(fetch_kernel, n, count, steps_of, tokens...  303 us
    pallas_call x1, Pallas kernels, back_sums(): pl.pallas_call(functools.partial(back_kernel, n, units, pool_count), out_...  172 us
    pallas_call x1, Pallas kernels, last_sums(): pl.pallas_call(functools.partial(last_kernel, n, units, len(lefts), len(r...  127 us
    pallas_call x1, Pallas kernels, spread(): pl.pallas_call(spread_kernel, grid=(steps,), out_shape=[jax.ShapeDtypeStr...  23.7 us

profile of v2, /device:TPU:0, one launch (start us, length us, event | category | flops | bytes accessed | tf_op | source)
XLA Modules:
  0.0 660.0 jit_solution(17600359952018602668)
XLA Ops:
  0.7 0.7 copy.52
  2.2 1.4 maximum_maximum_fusion.refs_15_.refs_28_
  3.6 0.8 copy.51
  5.2 1.5 copy.54.refs_13_
  6.7 303.1 %fetch.1 = (bf16[1024,1024]{1,0:T(8,128)(2,1)}, bf16[1024,1024]{1,0:T(8,128)(2,1)}, bf16[1024,1024]{1,0:T(8,128)(2,1)}, bf16[1024,1024]{1,0:T(8,128)(2,1)}, bf16...) custom-call(bf16[256,1024]{1,0:T(8,128)(2,1)} %refs_0_.1, ...), custom_call_target="tpu_custom_call" | custom-call | tf_op jit(solution)/shard_map/fetch/pallas_call | solution.py:905
  309.7 1.1 copy.59
  310.8 0.8 pad_maximum_fusion.8.refs_4_
  311.6 1.4 copy.58
  313.0 0.8 pad_maximum_fusion.2.refs_3_
  314.1 0.8 pad_maximum_fusion.7.refs_2_
  314.8 0.7 copy.56
  315.7 1.3 pad_maximum_fusion.refs_1_
  317.3 0.8 pad_maximum_fusion.1.refs_0_
  318.1 172.4 %back_sums.1 = (f32[32,1024]{1,0:T(8,128)}, f32[32,1024]{1,0:T(8,128)}, f32[32,1024]{1,0:T(8,128)}, f32[32,1024]{1,0:T(8,128)}, f32[96,1024]{1,0:T(8,128)}, /*in...) custom-call(bf16[2,16,32,256]{3,2,1,0:T(8,128)(2,1)} %pad_maximum_fu, ...), custom_call_target="tpu_custom_call" | custom-call | tf_op jit(solution)/shard_map/back_sums/pallas_call | solution.py:1658
  490.5 2.1 pad_maximum_fusion.5
  493.2 1.1 pad_maximum_fusion.3
  494.3 0.7 add_convert_fusion.refs_2_
  495.1 127.1 %last_sums.1 = (f32[32,1024]{1,0:T(8,128)}, f32[32,1024]{1,0:T(8,128)}, f32[32,1024]{1,0:T(8,128)}, f32[32,1024]{1,0:T(8,128)}, f32[16,1024]{1,0:T(8,128)}, /*in...) custom-call(bf16[2,16,32,256]{3,2,1,0:T(8,128)(2,1)} %get-tuple-element.153.refs_0_, ...), custom_call_target="tpu_custom_call" | custom-call | tf_op jit(solution)/shard_map/last_sums/pallas_call | solution.py:1248
  622.8 0.7 reshape.127.rows_of
  623.5 23.7 %spread.1 = (f32[1954,1024]{1,0:T(8,128)}, f32[1954,1]{1,0:T(8,128)}) custom-call(s32[32,96,1]{2,1,0:T(8,128)} %get-tuple-element.116.lists, s32[4,1,768]{2,1,0:T(1,128)} %reshape.127.rows_of, bf16[32,256,1024]{2,1,0:T(8,128)(2,1)} %bitcast.54), custom_call_target="tpu_custom_call" | custom-call | tf_op jit(solution)/shard_map/spread/pallas_call | solution.py:1698
  647.1 2.3 convert_reduce_fusion
  650.0 0.8 constant_dynamic-slice_fusion
  651.3 0.8 slice_select_fusion
  652.1 0.8 copy.74
  652.9 0.7 copy.75
  653.5 0.8 copy.76
  654.3 0.7 copy.77
  655.0 0.7 copy.78
  655.7 0.7 copy.79
  656.3 0.7 copy.80
  657.0 0.7 copy.81
  657.6 0.7 copy.82
  (66 shorter events, 5.9 us)
Async XLA Ops:
  1.5 5.2 copy-start.4
  310.8 3.0 copy-start.9
  311.6 3.2 copy-start.2
  315.7 1.3 copy-start.8
  318.1 174.5 %copy-start.7 = (bf16[256,1024]{1,0:T(8,128)(2,1)S(1)}, bf16[256,1024]{1,0:T(8,128)(2,1)}, u32[]{:S(2)}) copy-start(bf16[256,1024]{1,0:T(8,128)(2,1)} %get-tuple-element.109) | copy-start | bytes 1572868
  490.5 2.4 copy-start.6
  492.9 1.3 copy-start.20
  495.1 127.1 %copy-start = (s32[32,96,1]{2,1,0:T(8,128)S(1)}, s32[32,96,1]{2,1,0:T(8,128)}, u32[]{:S(2)}) copy-start(s32[32,96,1]{2,1,0:T(8,128)} %get-tuple-element.116.lists) | copy-start | bytes 36868
  623.5 25.9 %copy-start.19 = (f32[16,1024]{1,0:T(8,128)S(1)}, f32[16,1024]{1,0:T(8,128)}, u32[]{:S(2)}) copy-start(f32[16,1024]{1,0:T(8,128)} %get-tuple-element.115) | copy-start | bytes 196612
  623.5 27.8 %copy-start.3 = (f32[96,1024]{1,0:T(8,128)S(1)}, f32[96,1024]{1,0:T(8,128)}, u32[]{:S(2)}) copy-start(f32[96,1024]{1,0:T(8,128)} %get-tuple-element.129) | copy-start | bytes 1179652
  647.1 5.0 copy-start.5
  647.1 5.8 copy-start.10
  647.1 6.4 copy-start.1
  647.1 7.2 %copy-start.18 = (f32[32,1024]{1,0:T(8,128)S(1)}, f32[32,1024]{1,0:T(8,128)}, u32[]{:S(2)}) copy-start(f32[32,1024]{1,0:T(8,128)} %get-tuple-element.184) | copy-start | bytes 393220
  649.4 5.6 copy-start.17
  649.4 6.3 copy-start.16
  651.3 5.0 copy-start.15
  651.3 5.7 copy-start.14
  652.1 5.6 copy-start.13
  652.1 6.2 copy-start.12
  652.1 6.9 %copy-start.11 = (f32[32,1024]{1,0:T(8,128)S(1)}, f32[32,1024]{1,0:T(8,128)}, u32[]{:S(2)}) copy-start(f32[32,1024]{1,0:T(8,128)} %get-tuple-element.194) | copy-start | bytes 393220

commit v3 on v2

--- a/solution.py
+++ b/solution.py
@@ -96,10 +96,10 @@
 
 
 SCHEDULE = (
+    (GATHER, 0),
     (HASH, 0),
-    (GATHER, 0),
+    (GATHER, 1),
     (HASH, 1),
-    (GATHER, 1),
     (HASH, 2),
     (GATHER, 2),
     (HASH, 3),
@@ -111,20 +111,21 @@
     (HASH, 6),
     (GATHER, 6),
     (HASH, 7),
+    (FORWARD, 2),
     (GATHER, 7),
-    (FORWARD, 1),
+    (FORWARD, 2),
     (GATHER, 8),
     (FORWARD, 1),
     (GATHER, 9),
-    (FORWARD, 1),
+    (FORWARD, 2),
     (GATHER, 10),
     (FORWARD, 1),
     (GATHER, 11),
-    (FORWARD, 1),
+    (FORWARD, 2),
     (GATHER, 12),
-    (FORWARD, 1),
+    (FORWARD, 2),
     (GATHER, 13),
-    (FORWARD, 5),
+    (FORWARD, 3),
 )
 VMEM_CAP = 60 * 1024 * 1024
 
@@ -334,7 +335,7 @@
 def forward_steps(here, fulls, embedded, extra_in, extra_out, slots, scratch):
     byte_ids, byte_table, gains, starts, ends = extra_in
     out = Kept(*extra_out)
-    gate_w, up_w, load_sems, halo_sems = scratch
+    gate_w, up_w, x_halo, load_sems, halo_sems = scratch
     tokens, width = embedded.shape
     heads = width // HD
     n = here.n
@@ -370,13 +371,7 @@
                 copy.wait()
 
     def through(a, slot):
-        total = None
-        for b in range(4):
-            part = matmul(
-                a[:, b * (width // 4) : (b + 1) * (width // 4)], slots[slot][b // 2, b % 2]
-            )
-            total = part if total is None else total + part
-        return total
+        return matmul(a, slots[slot][...].reshape(width, width))
 
     def embed():
         load_slot(0, 0)
@@ -386,33 +381,60 @@
         pick = jnp.where(byte_ids[...] == ids, 1.0, 0.0).astype(LOW)
         embedded[...] = embedded[...] + matmul(pick, byte_table[...])
         out.x_attn[...] = normalize(embedded[...], gains[0:1])[0]
+        halo_send()
+
+    def halo_send():
+        target = jnp.minimum(rank + 2, 7)
+        here.send_if(
+            rank + 2 < 8,
+            out.x_attn,
+            x_halo.at[0],
+            halo_sems.at[0, 0],
+            halo_sems.at[0, 1],
+            (z, target // 4, lax.rem(target, 4)),
+        )
+        here.send_if(
+            c == 0, out.x_attn, x_halo.at[1], halo_sems.at[1, 0], halo_sems.at[1, 1], here.at(dc=1)
+        )
 
     def project():
         wait(0, 1, 2)
         a = out.x_attn[...]
+        out.queries[...] = through(a, 0).astype(LOW)
         kv[0, 2 * tokens :] = through(a, 1).astype(LOW)
         kv[1, 2 * tokens :] = through(a, 2).astype(LOW)
-        for back in (1, 2):
-            target = rank + back
-            here.send_if(
-                target < 8,
-                kv.at[:, pl.ds(2 * tokens, tokens)],
-                kv.at[:, pl.ds((2 - back) * tokens, tokens)],
-                halo_sems.at[back - 1, 0],
-                halo_sems.at[back - 1, 1],
-                (z, target // 4, lax.rem(target, 4)),
-            )
-        out.queries[...] = through(a, 0).astype(LOW)
-        for back in (1, 2):
-            part = kv.at[:, pl.ds((2 - back) * tokens, tokens)]
-
-            @pl.when(rank >= back)
-            def _():
-                here.expect(part, halo_sems.at[back - 1, 1])
-
-            @pl.when(rank < back)
-            def _():
-                part[...] = jnp.zeros_like(part)
+
+    def halo():
+        there = rank >= 2
+
+        @pl.when(there)
+        def _():
+            here.expect(x_halo.at[0], halo_sems.at[0, 1])
+
+        here.send_if(
+            there & (c == 1),
+            x_halo.at[0],
+            x_halo.at[1],
+            halo_sems.at[1, 0],
+            halo_sems.at[1, 1],
+            here.at(dc=1),
+        )
+
+        @pl.when(there | (c == 1))
+        def _():
+            here.expect(x_halo.at[1], halo_sems.at[1, 1])
+
+        @pl.when(jnp.logical_not(there))
+        def _():
+            x_halo[0] = jnp.zeros_like(x_halo[0])
+
+        @pl.when(rank == 0)
+        def _():
+            x_halo[1] = jnp.zeros_like(x_halo[1])
+
+        a = x_halo[...].reshape(2 * tokens, width)
+        kv[0, : 2 * tokens] = through(a, 1).astype(LOW)
+        kv[1, : 2 * tokens] = through(a, 2).astype(LOW)
 
     lane = lax.broadcasted_iota(jnp.int32, (1, 128), 1)
     sides = [jnp.where(lane < HD, 1.0, 0.0).astype(LOW), jnp.where(lane < HD, 0.0, 1.0).astype(LOW)]
@@ -514,8 +536,6 @@
     pooled_f = []
 
     def cross_keys():
-        load_slot(8, 4)
-        load_slot(9, 5)
         inside = jnp.where(member(), 1.0, 0.0).astype(LOW)
         length = (ends[...] - starts[...]).astype(F32)
         pooled = matmul(inside, out.x_cross[...]) / length
@@ -527,8 +547,6 @@
         out.p_value[...] = through(a, 5).astype(LOW)
 
     def cross_query():
-        load_slot(7, 3)
-        load_slot(10, 0)
         wait(7)
         out.p_query[...] = through(out.pooled[...], 3).astype(LOW)
         allowed = member()
@@ -563,14 +581,18 @@
     return [
         ((0, 1, 2), embed),
         ((), project),
+        ((), halo),
         ((), lambda: attend(0)),
         ((3,), lambda: attend(1)),
         ((), attention_out),
         ((4, 5), lambda: (load(4, gate_w), load(5, up_w))),
         ((6,), feed_forward),
+        ((8, 9), lambda: (load_slot(8, 4), load_slot(9, 5))),
         ((), feed_out),
-        ((8, 9), cross_keys),
-        ((7, 10), cross_query),
+        ((7,), lambda: load_slot(7, 3)),
+        ((), cross_keys),
+        ((10,), lambda: load_slot(10, 0)),
+        ((), cross_query),
         ((), cross_out),
     ]
 
@@ -840,8 +862,6 @@
                 here.sent(copy)
 
     here.greet()
-    for t in range(len(weights)):
-        each(t, Weight.local)
     lead, lag1, lag2, lag3 = GATHER_LAGS
     for t in range(lead):
         each(t, Weight.along_z)
@@ -873,6 +893,7 @@
             each(number + lead, Weight.along_z)
             each(number, Weight.near)
             each(number - lag1, Weight.far)
+            each(number - lag1, Weight.local)
             each(number - lag2, Weight.across)
             each(number - lag3, Weight.done)
             if 0 <= number - lag3 < len(steps_of):
@@ -933,6 +954,7 @@
             pltpu.VMEM((n * 8 * lines, 128), jnp.int32),
             pltpu.VMEM((n * shards[4].shape[0], ff), low),
             pltpu.VMEM((n * shards[5].shape[0], ff), low),
+            pltpu.VMEM((2, tokens, width), low),
             dma((count, max(n, ff // 256))),
             dma((2, 2)),
         ],
@@ -1120,11 +1142,12 @@
     count = len(units)
     take = taker(refs)
     lefts_in, rights_in = take(left_count), take(right_count)
-    embed_in, gains_in = take(2)
+    embed_in, gains_in, lists, rows_of = take(4)
     outs = take(count)
-    gathered, gains_out = take(2)
+    gains_out, table_grad, counts = take(3)
     here = Place(n)
     sums = GradSums(here, units, lefts_in, rights_in, outs, take, pool_count)
+    gathered, stacked = take(2)
     gain_send, gain_recv, gain_sems, own_sem, near_sems, plane_sems = take(6)
     z, x, y, c = here.z, here.x, here.y, here.c
 
@@ -1170,9 +1193,25 @@
         a = gathered.at[plane, :, :, c]
         here.send(a, a, near_sems.at[j, 4, 0], near_sems.at[j, 4, 1], here.at(dc=1))
 
-    def embed_done(j):
+    def spread(j):
         plane = lax.rem(z + n - j, n)
         here.expect(gathered.at[plane, :, :, 1 - c], near_sems.at[j, 4, 1])
+        byte_iota = lax.broadcasted_iota(jnp.int32, (SLOTS, embed_in.shape[0]), 1)
+        for s in range(8):
+            asked = jnp.bitwise_and(lists[plane * 8 + s], 255)
+            pick = (asked == byte_iota).astype(jnp.bfloat16)
+            grads = gathered[plane, s // 4, s // 2 % 2, s % 2]
+            stacked[s * SLOTS : (s + 1) * SLOTS, :] = matmul(pick, grads).astype(jnp.bfloat16)
+        row_iota = lax.broadcasted_iota(jnp.int32, (table_grad.shape[0], 8 * SLOTS), 0)
+        onto = (rows_of[plane] == row_iota).astype(jnp.float32)
+        uses = jnp.sum(onto, axis=1, keepdims=True)
+        added = matmul(onto.astype(jnp.bfloat16), stacked[...])
+        if j == 0:
+            counts[...] = uses
+            table_grad[...] = added
+        else:
+            counts[...] += uses
+            table_grad[...] += added
 
     def gains(stage):
         if stage == 0:
@@ -1222,11 +1261,11 @@
         if 0 <= t - 4 < n:
             embed_across(t - 4)
         if 0 <= t - 5 < n:
-            embed_done(t - 5)
+            spread(t - 5)
     here.finish()
 
 
-def last_sums(pairs, lefts, rights, embed_low, gains, dp_count):
+def last_sums(pairs, lefts, rights, embed_low, gains, entries, rows_dev, dp_count):
     n = dp_count
     low = jnp.bfloat16
     dma = pltpu.SemaphoreType.DMA
@@ -1237,7 +1276,10 @@
     )
     count = len(pairs)
     tokens, width = embed_low.shape
+    rows_of = jnp.right_shift(entries, 8).reshape(n, 1, 8 * SLOTS)
     scratch += [
+        pltpu.VMEM((n, 2, 2, 2, tokens, width), low),
+        pltpu.VMEM((8 * SLOTS, width), low),
         pltpu.VMEM((4, 8, width), jnp.float32),
         pltpu.VMEM((2 + n, 8, width), jnp.float32),
         dma((2 + n, 2)),
@@ -1249,18 +1291,19 @@
         functools.partial(last_kernel, n, units, len(lefts), len(rights), pool_count),
         out_shape=[jax.ShapeDtypeStruct(shape, jnp.float32) for shape in shapes]
         + [
-            jax.ShapeDtypeStruct((n, 2, 2, 2, tokens, width), low),
             jax.ShapeDtypeStruct((8, width), jnp.float32),
+            jax.ShapeDtypeStruct((rows_dev, width), jnp.float32),
+            jax.ShapeDtypeStruct((rows_dev, 1), jnp.float32),
         ],
-        in_specs=[hbm] * (len(lefts) + len(rights)) + [vmem, vmem],
-        out_specs=[vmem] * count + [hbm, vmem],
+        in_specs=[hbm] * (len(lefts) + len(rights)) + [vmem] * 4,
+        out_specs=[vmem] * (count + 3),
         scratch_shapes=scratch,
         compiler_params=pltpu.CompilerParams(
             collective_id=2, has_side_effects=True, vmem_limit_bytes=VMEM_CAP
         ),
         name="last_sums",
-    )(*lefts, *rights, embed_low, gains)
-    return results[:count], results[count], results[count + 1]
+    )(*lefts, *rights, embed_low, gains, entries, rows_of)
+    return results[:count], *results[count:]
 
 
 BACK_PAIRS = ((4, 8), (3, 6), (3, 7), (2, 5), (1, 4), (0, 0), (0, 1), (0, 2), (0, 3))
@@ -1546,30 +1589,58 @@
 
         lax.fori_loop(first, last, heads_pair, 0)
 
+    there = rank >= 2
+
+    def part_of(number, back):
+        return sent.at[pl.ds((2 * number + 2 - back) * tokens, tokens)]
+
+    def halo_pair():
+        for number in range(2):
+            here.send_if(
+                there | (here.c == 1),
+                part_of(number, 1),
+                halo.at[1, number],
+                halo_sems.at[1, number, 0],
+                halo_sems.at[1, number, 1],
+                here.at(dc=1),
+            )
+
     def halo_send():
-        for back in (1, 2):
-            target = rank - back
-            for number in range(2):
-                here.send_if(
-                    target >= 0,
-                    sent.at[pl.ds((2 * number + 2 - back) * tokens, tokens)],
-                    halo.at[back - 1, number],
-                    halo_sems.at[back - 1, number, 0],
-                    halo_sems.at[back - 1, number, 1],
-                    (here.z, jnp.maximum(target, 0) // 4, lax.rem(jnp.maximum(target, 0), 4)),
-                )
+        for number in range(2):
+
+            @pl.when(there | (here.c == 0))
+            def _():
+                here.expect(halo.at[1, number], halo_sems.at[1, number, 1])
+
+            part = part_of(number, 2)
+
+            @pl.when(there & (here.c == 1))
+            def _():
+                part[...] = (part[...].astype(F32) + halo[1, number].astype(F32)).astype(LOW)
+
+            target = jnp.maximum(rank - 2, 0)
+            here.send_if(
+                there,
+                part,
+                halo.at[0, number],
+                halo_sems.at[0, number, 0],
+                halo_sems.at[0, number, 1],
+                (here.z, target // 4, lax.rem(target, 4)),
+            )
 
     def halo_add():
-        for back in (1, 2):
-
-            @pl.when(rank + back < 8)
+        for number, own, grad in ((0, own_key, g_key), (1, own_value, g_value)):
+
+            @pl.when(here.c == 0)
             def _():
-                for number, own in ((0, own_key), (1, own_value)):
-                    here.expect(halo.at[back - 1, number], halo_sems.at[back - 1, number, 1])
-                    own[...] += halo[back - 1, number].astype(F32)
-
-        g_key[...] = own_key[...].astype(LOW)
-        g_value[...] = own_value[...].astype(LOW)
+                own[...] += halo[1, number].astype(F32)
+
+            @pl.when(rank + 2 < 8)
+            def _():
+                here.expect(halo.at[0, number], halo_sems.at[0, number, 1])
+                own[...] += halo[0, number].astype(F32)
+
+            grad[...] = own[...].astype(LOW)
 
     def embed_in():
         for slot in (1, 2, 3):
@@ -1605,6 +1676,7 @@
     sums.second(5)
     sums.third(3)
     attend(pairs // 2, pairs)
+    halo_pair()
     halo_send()
     sums.second(6)
     sums.third(4)
@@ -1669,53 +1741,6 @@
         name="back_sums",
     )(*lefts, *streamed, *kept)
     return results[:count], results[count:]
-
-
-def spread_kernel(lists, rows_of, grads, out, counts, stacked):
-    step = pl.program_id(0)
-    group, tokens = grads.shape[0], grads.shape[1]
-
-    @pl.when(step == 0)
-    def _():
-        out[...] = jnp.zeros_like(out)
-        counts[...] = jnp.zeros_like(counts)
-
-    byte_iota = lax.broadcasted_iota(jnp.int32, (SLOTS, tokens), 1)
-    for s in range(group):
-        pick = (jnp.bitwise_and(lists[s], 255) == byte_iota).astype(jnp.bfloat16)
-        stacked[s * SLOTS : (s + 1) * SLOTS, :] = matmul(pick, grads[s]).astype(jnp.bfloat16)
-    row_iota = lax.broadcasted_iota(jnp.int32, (out.shape[0], group * SLOTS), 0)
-    onto = (rows_of[0] == row_iota).astype(jnp.float32)
-    counts[...] += jnp.sum(onto, axis=1, keepdims=True)
-    out[...] += matmul(onto.astype(jnp.bfloat16), stacked[...])
-
-
-def spread(entries, gathered, rows_dev):
-    sources, tokens, width = gathered.shape
-    group = 8
-    steps = sources // group
-    rows_of = jnp.right_shift(entries, 8).reshape(steps, 1, group * SLOTS)
-    out, counts = pl.pallas_call(
-        spread_kernel,
-        grid=(steps,),
-        out_shape=[
-            jax.ShapeDtypeStruct((rows_dev, width), jnp.float32),
-            jax.ShapeDtypeStruct((rows_dev, 1), jnp.float32),
-        ],
-        in_specs=[
-            pl.BlockSpec((group, SLOTS, 1), lambda i: (i, 0, 0)),
-            pl.BlockSpec((1, 1, group * SLOTS), lambda i: (i, 0, 0)),
-            pl.BlockSpec((group, tokens, width), lambda i: (i, 0, 0)),
-        ],
-        out_specs=[
-            pl.BlockSpec((rows_dev, width), lambda i: (0, 0)),
-            pl.BlockSpec((rows_dev, 1), lambda i: (0, 0)),
-        ],
-        scratch_shapes=[pltpu.VMEM((group * SLOTS, width), jnp.bfloat16)],
-        compiler_params=pltpu.CompilerParams(vmem_limit_bytes=VMEM_CAP),
-        name="spread",
-    )(entries, rows_of, gathered)
-    return out, counts[:, 0].astype(jnp.int32)
 
 
 WEIGHT_STEPS = tuple(((i, 0, 2), (i, 1, 2)) for i in (0, 1, 2, 3, 4, 5, 6, 8, 9, 7, 10))
@@ -2173,7 +2198,6 @@
     rs_count = lax.axis_size(SEQ)
     all_count = dp_count * rs_count
     rank_table = lax.axis_index(ALL)
-    tokens = hash_ids.shape[0]
     rows_dev, model_width = hash_table.shape
     patch_len = lengths[0]
     patch_end = jnp.cumsum(patch_len)[:, None]
@@ -2240,20 +2264,20 @@
         by_rows(a, dp_count) for a in (kept.x_attn, kept.attended, one_hot.astype(jnp.bfloat16))
     ]
     rights = [grad_queries, grad_keys, grad_values, grad_branch_a, embed_grad]
-    sums, all_embed, gain_sums = last_sums(
+    sums, gain_sums, hash_table_grad, counts = last_sums(
         [(1, 3), (0, 0), (0, 1), (0, 2), (2, 4)],
         lefts,
         rights,
         embed_grad,
         gain_rows,
+        entries,
+        rows_dev,
         dp_count,
     )
     out_proj, out_query, out_key, out_value, byte_rows = sums
     out_down = own_rows(down_rows, kept.hidden.shape[1] // all_count)
     out_bytes = own_rows(byte_rows, BYTE_VALUES // all_count)
-    hash_table_grad, row_counts = spread(
-        entries, all_embed.reshape(all_count, tokens, model_width), rows_dev
-    )
+    row_counts = counts[:, 0].astype(jnp.int32)
     own_gains = lax.dynamic_slice_in_dim(
         gain_sums, rank_table * (model_width // all_count), model_width // all_count, 1
     )

time: 670 us -> 614 us (0.916)
  Pallas kernels: 626 us -> 560 us
  local copies, waits for them, and re-layouts: 17.7 us -> 26.1 us
    pallas_call x1, Pallas kernels: 303 us -> 260 us  [fetch(): pl.pallas_call(functools.partial(fetch_kernel, n, count, steps_of, tokens...]
    pallas_call x1 -> x0, Pallas kernels: 23.7 us -> none  [spread(): pl.pallas_call(spread_kernel, grid=(steps,), out_shape=[jax.ShapeDtypeStr...]
    unnamed x54 -> x53, local copies, waits for them, and re-layouts: 8.39 us -> 16.9 us
where the time goes in v3:
time: 614 us; the launch traced here: 603 us
  Pallas kernels  560 us (91%)
  local copies, waits for them, and re-layouts  26.1 us (4%)
  other arithmetic  15.6 us (3%)
    pallas_call x1, Pallas kernels, fetch(): pl.pallas_call(functools.partial(fetch_kernel, n, count, steps_of, tokens...  260 us
    pallas_call x1, Pallas kernels, back_sums(): pl.pallas_call(functools.partial(back_kernel, n, units, pool_count), out_...  171 us
    pallas_call x1, Pallas kernels, last_sums(): pl.pallas_call(functools.partial(last_kernel, n, units, len(lefts), len(r...  130 us
    unnamed x53, local copies, waits for them, and re-layouts  16.9 us

profile of v3, /device:TPU:0, one launch (start us, length us, event | category | flops | bytes accessed | tf_op | source)
XLA Modules:
  0.0 603.4 jit_solution(17874388082247623311)
XLA Ops:
  0.7 0.7 copy.52
  2.2 1.4 maximum_maximum_fusion.refs_15_.refs_28_
  3.6 0.8 copy.51
  5.2 1.5 copy.54.refs_13_
  6.7 260.1 %fetch.1 = (bf16[1024,1024]{1,0:T(8,128)(2,1)}, bf16[1024,1024]{1,0:T(8,128)(2,1)}, bf16[1024,1024]{1,0:T(8,128)(2,1)}, bf16[1024,1024]{1,0:T(8,128)(2,1)}, bf16...) custom-call(bf16[256,1024]{1,0:T(8,128)(2,1)} %refs_0_.1, ...), custom_call_target="tpu_custom_call" | custom-call | tf_op jit(solution)/shard_map/fetch/pallas_call | solution.py:926
  266.7 1.1 copy.59
  267.8 0.8 pad_maximum_fusion.8.refs_4_
  268.6 1.4 copy.58
  270.0 0.8 pad_maximum_fusion.2.refs_3_
  271.1 0.8 pad_maximum_fusion.7.refs_2_
  271.8 0.7 copy.56
  272.7 1.3 pad_maximum_fusion.refs_1_
  274.2 0.8 pad_maximum_fusion.1.refs_0_
  275.1 170.5 %back_sums.1 = (f32[32,1024]{1,0:T(8,128)}, f32[32,1024]{1,0:T(8,128)}, f32[32,1024]{1,0:T(8,128)}, f32[32,1024]{1,0:T(8,128)}, f32[96,1024]{1,0:T(8,128)}, /*in...) custom-call(bf16[2,16,32,256]{3,2,1,0:T(8,128)(2,1)} %pad_maximum_fu, ...), custom_call_target="tpu_custom_call" | custom-call | tf_op jit(solution)/shard_map/back_sums/pallas_call | solution.py:1730
  445.6 2.1 pad_maximum_fusion.5
  448.3 1.1 pad_maximum_fusion.3
  450.3 0.7 reshape.123.refs_11_
  451.1 0.7 add_convert_fusion.refs_2_
  451.8 129.9 %last_sums.1 = (f32[32,1024]{1,0:T(8,128)}, f32[32,1024]{1,0:T(8,128)}, f32[32,1024]{1,0:T(8,128)}, f32[32,1024]{1,0:T(8,128)}, f32[16,1024]{1,0:T(8,128)}, /*in...) custom-call(bf16[2,16,32,256]{3,2,1,0:T(8,128)(2,1)} %get-tuple-element.151.refs_0_, ...), custom_call_target="tpu_custom_call" | custom-call | tf_op jit(solution)/shard_map/last_sums/pallas_call | solution.py:1290
  581.8 1.5 slice_select_fusion.1
  583.2 0.7 constant_dynamic-slice_fusion
  584.5 2.2 convert_reduce_fusion
  586.7 0.8 slice_select_fusion
  587.4 0.8 copy.75
  588.2 0.7 copy.76
  588.9 0.8 copy.77
  589.7 8.2 %copy.78 = f32[1954,1024]{1,0:T(8,128)} copy(f32[1954,1024]{1,0:T(8,128)} %get-tuple-element.177) | data formatting | bytes 16007168
  597.9 0.7 copy.79
  598.6 0.7 copy.80
  599.3 0.7 copy.81
  599.9 0.7 copy.82
  600.6 0.7 copy.83
  (64 shorter events, 6.3 us)
Async XLA Ops:
  1.5 5.2 copy-start.4
  267.8 3.0 copy-start.9
  268.6 3.2 copy-start.2
  272.7 1.3 copy-start.8
  275.1 172.7 %copy-start.7 = (bf16[256,1024]{1,0:T(8,128)(2,1)S(1)}, bf16[256,1024]{1,0:T(8,128)(2,1)}, u32[]{:S(2)}) copy-start(bf16[256,1024]{1,0:T(8,128)(2,1)} %get-tuple-element.108) | copy-start | bytes 1572868
  445.6 2.4 copy-start.6
  448.0 1.6 copy-start
  448.3 2.7 copy-start.19
  451.8 134.8 %copy-start.3 = (f32[96,1024]{1,0:T(8,128)S(1)}, f32[96,1024]{1,0:T(8,128)}, u32[]{:S(2)}) copy-start(f32[96,1024]{1,0:T(8,128)} %get-tuple-element.127) | copy-start | bytes 1179652
  581.7 5.7 copy-start.5
  581.7 6.5 %copy-start.10 = (bf16[64,1024]{1,0:T(8,128)(2,1)S(1)}, bf16[64,1024]{1,0:T(8,128)(2,1)}, u32[]{:S(2)}) copy-start(bf16[64,1024]{1,0:T(8,128)(2,1)} %get-tuple-element.174) | copy-start | bytes 393220
  581.7 7.2 %copy-start.1 = (bf16[256,1024]{1,0:T(8,128)(2,1)S(1)}, bf16[256,1024]{1,0:T(8,128)(2,1)}, u32[]{:S(2)}) copy-start(bf16[256,1024]{1,0:T(8,128)(2,1)} %get-tuple-element.175.refs_7_.refs_8_) | copy-start | bytes 1572868
  589.7 8.3 %copy-start.18 = (f32[32,1024]{1,0:T(8,128)S(1)}, f32[32,1024]{1,0:T(8,128)}, u32[]{:S(2)}) copy-start(f32[32,1024]{1,0:T(8,128)} %get-tuple-element.182) | copy-start | bytes 393220
  589.7 8.9 %copy-start.17 = (f32[32,1024]{1,0:T(8,128)S(1)}, f32[32,1024]{1,0:T(8,128)}, u32[]{:S(2)}) copy-start(f32[32,1024]{1,0:T(8,128)} %get-tuple-element.183) | copy-start | bytes 393220
  589.7 9.6 %copy-start.16 = (f32[32,1024]{1,0:T(8,128)S(1)}, f32[32,1024]{1,0:T(8,128)}, u32[]{:S(2)}) copy-start(f32[32,1024]{1,0:T(8,128)} %get-tuple-element.184) | copy-start | bytes 393220
  589.7 10.2 %copy-start.15 = (f32[32,1024]{1,0:T(8,128)S(1)}, f32[32,1024]{1,0:T(8,128)}, u32[]{:S(2)}) copy-start(f32[32,1024]{1,0:T(8,128)} %get-tuple-element.185) | copy-start | bytes 393220
  589.7 10.9 %copy-start.14 = (f32[32,1024]{1,0:T(8,128)S(1)}, f32[32,1024]{1,0:T(8,128)}, u32[]{:S(2)}) copy-start(f32[32,1024]{1,0:T(8,128)} %get-tuple-element.189) | copy-start | bytes 393220
  589.7 11.5 %copy-start.13 = (f32[32,1024]{1,0:T(8,128)S(1)}, f32[32,1024]{1,0:T(8,128)}, u32[]{:S(2)}) copy-start(f32[32,1024]{1,0:T(8,128)} %get-tuple-element.190) | copy-start | bytes 393220
  589.7 12.2 %copy-start.12 = (f32[32,1024]{1,0:T(8,128)S(1)}, f32[32,1024]{1,0:T(8,128)}, u32[]{:S(2)}) copy-start(f32[32,1024]{1,0:T(8,128)} %get-tuple-element.191) | copy-start | bytes 393220
  589.7 12.8 %copy-start.11 = (f32[32,1024]{1,0:T(8,128)S(1)}, f32[32,1024]{1,0:T(8,128)}, u32[]{:S(2)}) copy-start(f32[32,1024]{1,0:T(8,128)} %get-tuple-element.192) | copy-start | bytes 393220

commit v4 on v3

--- a/solution.py
+++ b/solution.py
@@ -89,7 +89,7 @@
 
 MESH_ID = pl.DeviceIdType.MESH
 SLOTS = 96
-GATHER_LAGS = (1, 1, 2, 3)
+GATHER_LAGS = (1, 2, 3)
 
 
 HASH, GATHER, FORWARD = range(3)
@@ -627,6 +627,7 @@
         local_sems,
         w_send,
         w_recv,
+        z_send,
         id_sems,
         places,
         entries,
@@ -684,13 +685,41 @@
             )
             return plane
 
+        def hop(self, there, up, k, plane, src_ref):
+            peer = jnp.clip(z + 1 if up else z - 1, 0, n - 1)
+            here.send_if(
+                there,
+                self.cut(src_ref, self.q, 1),
+                self.cut(self.on(plane), self.q, 1),
+                z_send.at[self.i, 0 if up else 1, k],
+                w_recv.at[self.i, 0, (k + 1 if up else n - k - 1) - 1],
+                (peer, x, y * 2 + c),
+            )
+
         def along_z(self):
-            for j in range(1, n):
-                self.stage(0, j, self.q, 1, self.shard, z, here.at(dz=j))
+            self.hop(z + 1 < n, True, 0, z, self.shard)
+            self.hop(z >= 1, False, 0, z, self.shard)
+
+        def onward(self, k):
+            for up in (True, False):
+                there = (z >= k) & (z + 1 < n) if up else (z + k < n) & (z >= 1)
+                plane = jnp.clip(z - k if up else z + k, 0, n - 1)
+                j = k if up else n - k
+
+                @pl.when(there)
+                def _():
+                    self.came(0, j, self.q, 1)
+
+                self.hop(there, up, k, plane, self.on(plane))
 
         def near(self):
             for j in range(1, n):
-                plane = self.came(0, j, self.q, 1)
+                plane = lax.rem(z + n - j, n)
+
+                @pl.when((z == 0) | (z == n - 1))
+                def _():
+                    self.came(0, j, self.q, 1)
+
                 peer = here.at(dx=1) if self.kind == 0 else here.at(dy=1)
                 self.stage(1, j, self.q, 1, self.on(plane), plane, peer)
 
@@ -777,17 +806,14 @@
 
         lax.fori_loop(0, sources, source, 0)
 
-    row_iota = lax.broadcasted_iota(jnp.int32, (SLOTS, table.shape[0]), 1)
+    row_iota = lax.broadcasted_iota(jnp.int32, (4 * SLOTS, table.shape[0]), 1)
     byte_iota = lax.broadcasted_iota(jnp.int32, (SLOTS, tokens), 1)
 
     def partial_sums(plane, core, write):
-        for place in range(4):
-            source = plane * 8 + place * 2 + core
-            entry = lists[source]
-            pick = (jnp.right_shift(entry, 8) == row_iota).astype(jnp.bfloat16)
-            g_rows[place * SLOTS : (place + 1) * SLOTS, :] = matmul(pick, table[...]).astype(
-                jnp.bfloat16
-            )
+        asked = [lists[plane * 8 + place * 2 + core] for place in range(4)]
+        rows = jnp.right_shift(jnp.concatenate(asked, axis=0), 8)
+        pick = (rows == row_iota).astype(jnp.bfloat16)
+        g_rows[...] = matmul(pick, table[...]).astype(jnp.bfloat16)
         for place in range(4):
             source = plane * 8 + place * 2 + core
             entry = lists[source]
@@ -862,9 +888,12 @@
                 here.sent(copy)
 
     here.greet()
-    lead, lag1, lag2, lag3 = GATHER_LAGS
-    for t in range(lead):
+    lag1, lag2, lag3 = GATHER_LAGS
+    for t in range(n - 1):
         each(t, Weight.along_z)
+        for k in range(1, n - 1):
+            if k <= t:
+                each(t - k, lambda w, k=k: w.onward(k))
     gather_ids()
     list_rows()
     hash_steps = []
@@ -890,7 +919,9 @@
             for run in hash_steps[number]:
                 run()
         elif what == GATHER:
-            each(number + lead, Weight.along_z)
+            each(number + n - 1, Weight.along_z)
+            for k in range(1, n - 1):
+                each(number + n - 1 - k, lambda w, k=k: w.onward(k))
             each(number, Weight.near)
             each(number - lag1, Weight.far)
             each(number - lag1, Weight.local)
@@ -949,6 +980,7 @@
             dma((gathers, 2)),
             dma((gathers, 4, n - 1)),
             dma((gathers, 4, n - 1)),
+            dma((gathers, 2, n - 1)),
             dma((2 + n, 2)),
             pltpu.VMEM((n * 8 * lines, 128), jnp.int32),
             pltpu.VMEM((n * 8 * lines, 128), jnp.int32),
@@ -1144,7 +1176,7 @@
     lefts_in, rights_in = take(left_count), take(right_count)
     embed_in, gains_in, lists, rows_of = take(4)
     outs = take(count)
-    gains_out, table_grad, counts = take(3)
+    gains_out, table_grad, counts, stacked_last, rows_last = take(5)
     here = Place(n)
     sums = GradSums(here, units, lefts_in, rights_in, outs, take, pool_count)
     gathered, stacked = take(2)
@@ -1201,7 +1233,11 @@
             asked = jnp.bitwise_and(lists[plane * 8 + s], 255)
             pick = (asked == byte_iota).astype(jnp.bfloat16)
             grads = gathered[plane, s // 4, s // 2 % 2, s % 2]
-            stacked[s * SLOTS : (s + 1) * SLOTS, :] = matmul(pick, grads).astype(jnp.bfloat16)
+            target = stacked_last if j == n - 1 else stacked
+            target[s * SLOTS : (s + 1) * SLOTS, :] = matmul(pick, grads).astype(jnp.bfloat16)
+        if j == n - 1:
+            rows_last[...] = rows_of[plane]
+            return
         row_iota = lax.broadcasted_iota(jnp.int32, (table_grad.shape[0], 8 * SLOTS), 0)
         onto = (rows_of[plane] == row_iota).astype(jnp.float32)
         uses = jnp.sum(onto, axis=1, keepdims=True)
@@ -1294,9 +1330,11 @@
             jax.ShapeDtypeStruct((8, width), jnp.float32),
             jax.ShapeDtypeStruct((rows_dev, width), jnp.float32),
             jax.ShapeDtypeStruct((rows_dev, 1), jnp.float32),
+            jax.ShapeDtypeStruct((8 * SLOTS, width), low),
+            jax.ShapeDtypeStruct((1, 8 * SLOTS), jnp.int32),
         ],
         in_specs=[hbm] * (len(lefts) + len(rights)) + [vmem] * 4,
-        out_specs=[vmem] * (count + 3),
+        out_specs=[vmem] * (count + 5),
         scratch_shapes=scratch,
         compiler_params=pltpu.CompilerParams(
             collective_id=2, has_side_effects=True, vmem_limit_bytes=VMEM_CAP
@@ -1591,40 +1629,45 @@
 
     there = rank >= 2
 
-    def part_of(number, back):
-        return sent.at[pl.ds((2 * number + 2 - back) * tokens, tokens)]
-
-    def halo_pair():
-        for number in range(2):
+    def part_of(number, back, span):
+        return sent.at[pl.ds((2 * number + 2 - back) * tokens, tokens), span]
+
+    def halo_parts(half):
+        span = pl.ds(half * (width // 2), width // 2)
+        return [(number, span, 2 * number + half) for number in range(2)]
+
+    def halo_pair(half):
+        for number, span, sem in halo_parts(half):
             here.send_if(
                 there | (here.c == 1),
-                part_of(number, 1),
-                halo.at[1, number],
-                halo_sems.at[1, number, 0],
-                halo_sems.at[1, number, 1],
+                part_of(number, 1, span),
+                halo.at[1, number, :, span],
+                halo_sems.at[1, sem, 0],
+                halo_sems.at[1, sem, 1],
                 here.at(dc=1),
             )
 
-    def halo_send():
-        for number in range(2):
+    def halo_send(half):
+        for number, span, sem in halo_parts(half):
 
             @pl.when(there | (here.c == 0))
             def _():
-                here.expect(halo.at[1, number], halo_sems.at[1, number, 1])
-
-            part = part_of(number, 2)
+                here.expect(halo.at[1, number, :, span], halo_sems.at[1, sem, 1])
+
+            part = part_of(number, 2, span)
 
             @pl.when(there & (here.c == 1))
             def _():
-                part[...] = (part[...].astype(F32) + halo[1, number].astype(F32)).astype(LOW)
+                added = part[...].astype(F32) + halo[1, number, :, span].astype(F32)
+                part[...] = added.astype(LOW)
 
             target = jnp.maximum(rank - 2, 0)
             here.send_if(
                 there,
                 part,
-                halo.at[0, number],
-                halo_sems.at[0, number, 0],
-                halo_sems.at[0, number, 1],
+                halo.at[0, number, :, span],
+                halo_sems.at[0, sem, 0],
+                halo_sems.at[0, sem, 1],
                 (here.z, target // 4, lax.rem(target, 4)),
             )
 
@@ -1637,7 +1680,9 @@
 
             @pl.when(rank + 2 < 8)
             def _():
-                here.expect(halo.at[0, number], halo_sems.at[0, number, 1])
+                for half in range(2):
+                    _, span, sem = halo_parts(half)[number]
+                    here.expect(halo.at[0, number, :, span], halo_sems.at[0, sem, 1])
                 own[...] += halo[0, number].astype(F32)
 
             grad[...] = own[...].astype(LOW)
@@ -1672,24 +1717,29 @@
     sums.second(4)
     sums.third(2)
     pairs = width // 128
-    attend(0, pairs // 2)
+    quarter = pairs // 4
+    attend(0, quarter)
     sums.second(5)
     sums.third(3)
-    attend(pairs // 2, pairs)
-    halo_pair()
-    halo_send()
+    sums.third(4)
+    attend(quarter, 2 * quarter)
+    halo_pair(0)
+    halo_send(0)
     sums.second(6)
-    sums.third(4)
+    sums.third(5)
+    attend(2 * quarter, 3 * quarter)
+    sums.second(7)
+    sums.third(6)
+    attend(3 * quarter, pairs)
+    halo_pair(1)
+    halo_send(1)
+    sums.second(8)
+    sums.third(7)
     for i in range(4):
         sums.final(i)
     halo_add()
-    sums.second(7)
-    sums.third(5)
+    sums.third(8)
     embed_in()
-    sums.second(8)
-    sums.third(6)
-    sums.third(7)
-    sums.third(8)
     for i in range(4, 9):
         sums.final(i)
     here.finish()
@@ -1725,7 +1775,7 @@
         dma((2, 5)),
         dma((width // tile,)),
         dma((2,)),
-        dma((2, 2, 2)),
+        dma((2, 4, 2)),
     ]
     results = pl.pallas_call(
         functools.partial(back_kernel, n, units, pool_count),
@@ -1743,6 +1793,56 @@
     return results[:count], results[count:]
 
 
+def finish_kernel(cuts, rows, stacked, table_in, counts_in, *refs):
+    wholes, refs = refs[: len(cuts)], list(refs[len(cuts) :])
+    halves = [refs.pop(0) for _ in range(4)]
+    table, counts = refs.pop(0), refs.pop(0)
+    row = lax.broadcasted_iota(jnp.int32, (table.shape[0], rows.shape[1]), 0)
+    onto = (rows[...] == row + pl.program_id(0) * table.shape[0]).astype(jnp.float32)
+    counts[...] = (counts_in[...] + jnp.sum(onto, axis=1, keepdims=True)).astype(jnp.int32)
+    table[...] = table_in[...] + matmul(onto.astype(jnp.bfloat16), stacked[...])
+
+    @pl.when(pl.program_id(0) == 0)
+    def _():
+        core = lax.axis_index(SUB) % 2
+        for cut, source, target in zip(cuts, wholes, refs):
+            if cut == source.shape[0]:
+                target[...] = source[...]
+            else:
+                target[...] = jnp.where(core == 0, source[:cut], source[source.shape[0] - cut :])
+        for k in range(2):
+            left, right = halves[k], halves[2 + k]
+            target = refs[len(cuts) + k]
+            target[:, : left.shape[1]] = left[...]
+            target[:, left.shape[1] :] = right[...]
+
+
+def finish(table_grad, counts, stacked, rows, wholes, cuts, halves):
+    rows_dev, width = table_grad.shape
+    block = 256
+    one = jax.ShapeDtypeStruct
+
+    def whole(shape):
+        return pl.BlockSpec(shape, lambda i: (0, 0))
+
+    def blocks(cols):
+        return pl.BlockSpec((block, cols), lambda i: (i, 0))
+
+    shapes = [(cut, a.shape[1]) for a, cut in zip(wholes, cuts)]
+    shapes += [(a.shape[0], a.shape[1] + b.shape[1]) for a, b in zip(halves[:2], halves[2:])]
+    return pl.pallas_call(
+        functools.partial(finish_kernel, cuts),
+        grid=(-(-rows_dev // block),),
+        out_shape=[one((rows_dev, width), F32), one((rows_dev, 1), jnp.int32)]
+        + [one(shape, F32) for shape in shapes],
+        in_specs=[whole(rows.shape), whole(stacked.shape), blocks(width), blocks(1)]
+        + [whole(a.shape) for a in (*wholes, *halves)],
+        out_specs=[blocks(width), blocks(1)] + [whole(shape) for shape in shapes],
+        compiler_params=pltpu.CompilerParams(vmem_limit_bytes=VMEM_CAP),
+        name="finish",
+    )(rows, stacked, table_grad, counts, *wholes, *halves)
+
+
 WEIGHT_STEPS = tuple(((i, 0, 2), (i, 1, 2)) for i in (0, 1, 2, 3, 4, 5, 6, 8, 9, 7, 10))
 
 
@@ -1753,11 +1853,6 @@
     a = a.T.reshape(pairs, both, depth)
     rows = -(-(both // 2) // 16) * 16
     return jnp.stack([a[:, :rows], a[:, both - rows :]])
-
-
-def own_rows(block, rows):
-    core = lax.axis_index(SUB) % 2
-    return jnp.where(core == 0, block[:rows], block[block.shape[0] - rows :])
 
 
 def body(
@@ -2255,16 +2350,14 @@
         ),
         dp_count,
     )
-    out_cout, out_ckey, out_cvalue, out_cquery, down_rows = sums[:5]
-    out_gate = jnp.concatenate([sums[5], sums[7]], axis=1)
-    out_up = jnp.concatenate([sums[6], sums[8]], axis=1)
+    first_sums = sums
     gain_rows, grad_branch_a, grad_queries, grad_keys, grad_values, embed_grad = results
     one_hot = byte_ids[:, None] == jnp.arange(BYTE_VALUES, dtype=jnp.int32)[None, :]
     lefts = [
         by_rows(a, dp_count) for a in (kept.x_attn, kept.attended, one_hot.astype(jnp.bfloat16))
     ]
     rights = [grad_queries, grad_keys, grad_values, grad_branch_a, embed_grad]
-    sums, gain_sums, hash_table_grad, counts = last_sums(
+    sums, gain_sums, *table_parts = last_sums(
         [(1, 3), (0, 0), (0, 1), (0, 2), (2, 4)],
         lefts,
         rights,
@@ -2274,10 +2367,27 @@
         rows_dev,
         dp_count,
     )
-    out_proj, out_query, out_key, out_value, byte_rows = sums
-    out_down = own_rows(down_rows, kept.hidden.shape[1] // all_count)
-    out_bytes = own_rows(byte_rows, BYTE_VALUES // all_count)
-    row_counts = counts[:, 0].astype(jnp.int32)
+    wholes = (*sums, *first_sums[:5])
+    cuts = [a.shape[0] for a in wholes]
+    cuts[4] = BYTE_VALUES // all_count
+    cuts[9] = kept.hidden.shape[1] // all_count
+    (
+        hash_table_grad,
+        counts,
+        out_proj,
+        out_query,
+        out_key,
+        out_value,
+        out_bytes,
+        out_cout,
+        out_ckey,
+        out_cvalue,
+        out_cquery,
+        out_down,
+        out_gate,
+        out_up,
+    ) = finish(*table_parts, wholes, tuple(cuts), first_sums[5:])
+    row_counts = counts[:, 0]
     own_gains = lax.dynamic_slice_in_dim(
         gain_sums, rank_table * (model_width // all_count), model_width // all_count, 1
     )

time: 614 us -> 582 us (0.948)
  local copies, waits for them, and re-layouts: 26.1 us -> 13.5 us
  Pallas kernels: 560 us -> 548 us
    pallas_call x1, Pallas kernels: 260 us -> 245 us  [fetch(): pl.pallas_call(functools.partial(fetch_kernel, n, count, steps_of, tokens...]
    pallas_call x0 -> x1, Pallas kernels: none -> 12.8 us  [finish(): pl.pallas_call(functools.partial(finish_kernel, cuts), grid=(-(-rows_dev...]
    unnamed x53 -> x26, local copies, waits for them, and re-layouts: 16.9 us -> 4.38 us
    pallas_call x1, Pallas kernels: 171 us -> 164 us  [back_sums(): pl.pallas_call(functools.partial(back_kernel, n, units, pool_count), out_...]
where the time goes in v4:
time: 582 us; the launch traced here: 572 us
  Pallas kernels  548 us (94%)
  local copies, waits for them, and re-layouts  13.5 us (2%)
  other arithmetic  10.1 us (2%)
    pallas_call x1, Pallas kernels, fetch(): pl.pallas_call(functools.partial(fetch_kernel, n, count, steps_of, tokens...  245 us
    pallas_call x1, Pallas kernels, back_sums(): pl.pallas_call(functools.partial(back_kernel, n, units, pool_count), out_...  164 us
    pallas_call x1, Pallas kernels, last_sums(): pl.pallas_call(functools.partial(last_kernel, n, units, len(lefts), len(r...  126 us
    pallas_call x1, Pallas kernels, finish(): pl.pallas_call(functools.partial(finish_kernel, cuts), grid=(-(-rows_dev...  12.8 us

profile of v4, /device:TPU:0, one launch (start us, length us, event | category | flops | bytes accessed | tf_op | source)
XLA Modules:
  0.0 572.5 jit_solution(14149681363880756568)
XLA Ops:
  0.7 0.7 copy.52
  1.5 0.6 sub.3.refs_16_.refs_29_
  2.2 1.4 maximum_maximum_fusion.refs_15_.refs_28_
  3.6 0.8 copy.51
  4.6 0.6 concatenate.6.refs_11_
  5.2 1.5 copy.54.refs_13_
  6.7 244.5 %fetch.1 = (bf16[1024,1024]{1,0:T(8,128)(2,1)}, bf16[1024,1024]{1,0:T(8,128)(2,1)}, bf16[1024,1024]{1,0:T(8,128)(2,1)}, bf16[1024,1024]{1,0:T(8,128)(2,1)}, bf16...) custom-call(bf16[256,1024]{1,0:T(8,128)(2,1)} %refs_0_.1, ...), custom_call_target="tpu_custom_call" | custom-call | tf_op jit(solution)/shard_map/fetch/pallas_call | solution.py:957
  251.2 1.1 copy.59
  252.4 1.1 copy.57
  253.6 0.9 pad_maximum_fusion.5
  254.5 0.2 copy.58
  254.7 0.2 copy.55
  255.0 1.1 pad_maximum_fusion.1
  256.2 0.7 copy.56
  257.1 1.3 pad_maximum_fusion.refs_1_
  258.4 163.9 %back_sums.1 = (f32[32,1024]{1,0:T(8,128)}, f32[32,1024]{1,0:T(8,128)}, f32[32,1024]{1,0:T(8,128)}, f32[32,1024]{1,0:T(8,128)}, f32[96,1024]{1,0:T(8,128)}, /*in...) custom-call(bf16[2,16,32,256]{3,2,1,0:T(8,128)(2,1)} %get-tuple-elem, ...), custom_call_target="tpu_custom_call" | custom-call | tf_op jit(solution)/shard_map/back_sums/pallas_call | solution.py:1780
  422.3 0.2 copy.61
  422.6 0.8 copy-done.5
  423.4 0.2 copy.60
  423.6 1.1 pad_maximum_fusion.3
  424.7 0.3 copy-done
  425.0 0.6 shift-right-arithmetic_reduce_fusion
  425.6 0.7 reshape.122.refs_11_
  426.4 0.7 add_convert_fusion.refs_2_
  427.1 126.3 %last_sums.1 = (f32[32,1024]{1,0:T(8,128)}, f32[32,1024]{1,0:T(8,128)}, f32[32,1024]{1,0:T(8,128)}, f32[32,1024]{1,0:T(8,128)}, f32[16,1024]{1,0:T(8,128)}, /*in...) custom-call(bf16[2,16,32,256]{3,2,1,0:T(8,128)(2,1)} %get-tuple-elem, ...), custom_call_target="tpu_custom_call" | custom-call | tf_op jit(solution)/shard_map/last_sums/pallas_call | solution.py:1326
  553.5 12.8 %finish.1 = (f32[1954,1024]{1,0:T(8,128)}, s32[1954,1]{1,0:T(8,128)}, f32[32,1024]{1,0:T(8,128)}, f32[32,1024]{1,0:T(8,128)}, f32[32,1024]{1,0:T(8,128)}, /*inde...) custom-call(s32[1,768]{1,0:T(1,128)} %get-tuple-element.131.rows, ...), custom_call_target="tpu_custom_call" | custom-call | tf_op jit(solution)/shard_map/finish/pallas_call | solution.py:1833
  566.3 2.2 reduce.1
  568.5 0.8 constant_dynamic-slice_fusion
  569.3 0.5 slice_bitcast_fusion.14
  569.8 0.8 copy.66
  570.6 0.7 copy.67
  571.2 0.8 copy.68
  (33 shorter events, 1.0 us)
Async XLA Ops:
  1.5 5.2 copy-start.3
  251.2 3.2 copy-start.8
  252.4 2.3 copy-start.7
  254.7 1.5 copy-start.2
  258.4 163.9 %copy-start.6 = (bf16[256,1024]{1,0:T(8,128)(2,1)S(1)}, bf16[256,1024]{1,0:T(8,128)(2,1)}, u32[]{:S(2)}) copy-start(bf16[256,1024]{1,0:T(8,128)(2,1)} %get-tuple-element.124) | copy-start | bytes 1572868
  422.3 1.0 copy-start.5
  423.4 1.6 copy-start
  423.6 2.7 copy-start.10
  553.5 16.3 %copy-start.4 = (bf16[256,1024]{1,0:T(8,128)(2,1)S(1)}, bf16[256,1024]{1,0:T(8,128)(2,1)}, u32[]{:S(2)}) copy-start(bf16[256,1024]{1,0:T(8,128)(2,1)} %get-tuple-element.207) | copy-start | bytes 1572868
  566.3 4.3 copy-start.9
  566.3 5.0 copy-start.1

commit v5 on v4

--- a/solution.py
+++ b/solution.py
@@ -115,11 +115,10 @@
     (GATHER, 7),
     (FORWARD, 2),
     (GATHER, 8),
-    (FORWARD, 1),
+    (FORWARD, 2),
     (GATHER, 9),
     (FORWARD, 2),
     (GATHER, 10),
-    (FORWARD, 1),
     (GATHER, 11),
     (FORWARD, 2),
     (GATHER, 12),
@@ -334,8 +333,17 @@
 
 def forward_steps(here, fulls, embedded, extra_in, extra_out, slots, scratch):
     byte_ids, byte_table, gains, starts, ends = extra_in
+    gate_w, up_w, x_halo, load_sems, halo_sems, *buffers, flush_sems = scratch
     out = Kept(*extra_out)
-    gate_w, up_w, x_halo, load_sems, halo_sems = scratch
+    flushed = (out.gate_pre, out.up_pre, out.key_values)
+    out = out._replace(gate_pre=buffers[0], up_pre=buffers[1], key_values=buffers[2])
+    flushes = []
+
+    def flush(i):
+        copy = pltpu.make_async_copy(buffers[i], flushed[i], flush_sems.at[i])
+        copy.start()
+        flushes.append(copy)
+
     tokens, width = embedded.shape
     heads = width // HD
     n = here.n
@@ -435,6 +443,7 @@
         a = x_halo[...].reshape(2 * tokens, width)
         kv[0, : 2 * tokens] = through(a, 1).astype(LOW)
         kv[1, : 2 * tokens] = through(a, 2).astype(LOW)
+        flush(2)
 
     lane = lax.broadcasted_iota(jnp.int32, (1, 128), 1)
     sides = [jnp.where(lane < HD, 1.0, 0.0).astype(LOW), jnp.where(lane < HD, 0.0, 1.0).astype(LOW)]
@@ -516,6 +525,8 @@
             return carry
 
         lax.fori_loop(0, tiles, columns, 0)
+        flush(0)
+        flush(1)
 
     def feed_out():
         wait(6)
@@ -576,6 +587,8 @@
         wait(10)
         states = pooled_f[0] + through(out.p_attended[...], 0)
         out.patch_states[...] = states.astype(LOW)
+        for copy in flushes:
+            copy.wait()
 
     down_sems = load_sems.at[6]
     return [
@@ -583,9 +596,9 @@
         ((), project),
         ((), halo),
         ((), lambda: attend(0)),
+        ((4, 5), lambda: (load(4, gate_w), load(5, up_w))),
         ((3,), lambda: attend(1)),
         ((), attention_out),
-        ((4, 5), lambda: (load(4, gate_w), load(5, up_w))),
         ((6,), feed_forward),
         ((8, 9), lambda: (load_slot(8, 4), load_slot(9, 5))),
         ((), feed_out),
@@ -954,6 +967,8 @@
     gathers = 2 * len(steps_of)
     ff = shards[4].shape[1]
     extra_out = list(kept_shapes(tokens, width, ff, extra[3].shape[0]))
+    out_places = Kept(*[vmem] * len(extra_out))
+    out_places = list(out_places._replace(gate_pre=hbm, up_pre=hbm, key_values=hbm))
     results = pl.pallas_call(
         functools.partial(fetch_kernel, n, count, steps_of, tokens, gram_count, used_lines),
         out_shape=[jax.ShapeDtypeStruct((n * w.shape[0], w.shape[1]), w.dtype) for w in shards]
@@ -963,7 +978,7 @@
         ]
         + extra_out,
         in_specs=[hbm] * count + [vmem, vmem] + [vmem] * len(extra),
-        out_specs=[hbm] * count + [vmem, vmem] + [vmem] * len(extra_out),
+        out_specs=[hbm] * count + [vmem, vmem] + out_places,
         scratch_shapes=[
             pltpu.VMEM((n, 2, 2, 2, lines, 128), jnp.int32),
             pltpu.VMEM((2, 2, 2, tokens, width), low),
@@ -989,6 +1004,10 @@
             pltpu.VMEM((2, tokens, width), low),
             dma((count, max(n, ff // 256))),
             dma((2, 2)),
+            pltpu.VMEM((tokens, ff), F32),
+            pltpu.VMEM((tokens, ff), F32),
+            pltpu.VMEM((2, 3 * tokens, width), low),
+            dma((3,)),
         ],
         compiler_params=pltpu.CompilerParams(
             collective_id=0, has_side_effects=True, vmem_limit_bytes=VMEM_CAP
@@ -1021,8 +1040,12 @@
         copies = []
         theirs = target.at[0]
         if source is not None:
-            theirs = source.at[1 - here.c] if split else source
-            mine = source.at[here.c] if split else source
+            mine = theirs = source
+            if split:
+                rows = target.shape[2]
+                apart = source.shape[1] - rows
+                mine = source.at[:, pl.ds(pl.multiple_of(here.c * apart, 16), rows)]
+                theirs = source.at[:, pl.ds(pl.multiple_of((1 - here.c) * apart, 16), rows)]
             local = pltpu.make_async_copy(mine, target.at[0], sems.at[i, 0])
             local.start()
             copies.append(local.wait)
@@ -1122,6 +1145,11 @@
             self.third(t - lag3)
         if 0 <= t - lag4 < count:
             self.final(t - lag4)
+
+
+def left_shape(a):
+    pairs, both, depth = a.shape
+    return (2, pairs, -(-(both // 2) // 16) * 16, depth)
 
 
 def plan_sums(pairs, left_shapes, right_shapes, n, most):
@@ -1308,7 +1336,7 @@
     hbm = pl.BlockSpec(memory_space=pl.ANY)
     vmem = pl.BlockSpec(memory_space=pltpu.VMEM)
     units, shapes, scratch, pool_count = plan_sums(
-        pairs, [a.shape for a in lefts], [a.shape for a in rights], n, 6
+        pairs, [left_shape(a) for a in lefts], [a.shape for a in rights], n, 6
     )
     count = len(pairs)
     tokens, width = embed_low.shape
@@ -1760,7 +1788,7 @@
     right_shapes += [(tokens, width), (patches, width)]
     right_shapes += [(tokens, width)] * 2 + [(patches, width)]
     units, shapes, scratch, pool_count = plan_sums(
-        BACK_PAIRS, [a.shape for a in lefts], right_shapes, n, 4
+        BACK_PAIRS, [left_shape(a) for a in lefts], right_shapes, n, 4
     )
     count = len(units)
     scratch += [
@@ -1848,11 +1876,7 @@
 
 def by_rows(a, dp_count):
     depth, total = a.shape
-    pairs = dp_count * 4
-    both = total // pairs
-    a = a.T.reshape(pairs, both, depth)
-    rows = -(-(both // 2) // 16) * 16
-    return jnp.stack([a[:, :rows], a[:, both - rows :]])
+    return a.T.reshape(dp_count * 4, total // (dp_count * 4), depth)
 
 
 def body(

time: 582 us -> 577 us (level)
  no operation moved by 1% of the time
where the time goes in v5:
time: 577 us; the launch traced here: 568 us
  Pallas kernels  543 us (94%)
  local copies, waits for them, and re-layouts  16.4 us (3%)
  other arithmetic  7.18 us (1%)
    pallas_call x1, Pallas kernels, fetch(): pl.pallas_call(functools.partial(fetch_kernel, n, count, steps_of, tokens...  241 us
    pallas_call x1, Pallas kernels, back_sums(): pl.pallas_call(functools.partial(back_kernel, n, units, pool_count), out_...  165 us
    pallas_call x1, Pallas kernels, last_sums(): pl.pallas_call(functools.partial(last_kernel, n, units, len(lefts), len(r...  125 us
    pallas_call x1, Pallas kernels, finish(): pl.pallas_call(functools.partial(finish_kernel, cuts), grid=(-(-rows_dev...  12.8 us

profile of v5, /device:TPU:0, one launch (start us, length us, event | category | flops | bytes accessed | tf_op | source)
XLA Modules:
  0.0 568.3 jit_solution(351925280268899607)
XLA Ops:
  0.7 0.7 copy.52
  1.4 0.1 broadcast_in_dim.28.refs_17_.refs_30_
  1.5 0.6 sub.3.refs_16_.refs_29_
  2.1 0.1 pad.4.clone
  2.2 1.4 maximum_maximum_fusion.refs_15_.refs_28_
  3.6 0.8 copy.51
  4.4 0.1 reshape.105
  4.6 0.6 concatenate.6.refs_11_
  5.2 1.5 copy.54.refs_13_
  6.7 240.8 %fetch.1 = (bf16[1024,1024]{1,0:T(8,128)(2,1)}, bf16[1024,1024]{1,0:T(8,128)(2,1)}, bf16[1024,1024]{1,0:T(8,128)(2,1)}, bf16[1024,1024]{1,0:T(8,128)(2,1)}, bf16...) custom-call(bf16[256,1024]{1,0:T(8,128)(2,1)} %refs_0_.1, ...), custom_call_target="tpu_custom_call" | custom-call | tf_op jit(solution)/shard_map/fetch/pallas_call | solution.py:972
  247.5 2.6 copy.56
  250.1 1.0 copy.58
  251.1 1.0 copy.55
  252.1 0.0 copy-done.8
  252.1 0.8 copy.57
  253.0 0.8 copy.59
  253.8 164.9 %back_sums.1 = (f32[32,1024]{1,0:T(8,128)}, f32[32,1024]{1,0:T(8,128)}, f32[32,1024]{1,0:T(8,128)}, f32[32,1024]{1,0:T(8,128)}, f32[96,1024]{1,0:T(8,128)}, /*in...) custom-call(bf16[16,64,256]{2,1,0:T(8,128)(2,1)} %bitcast.27, ...), custom_call_target="tpu_custom_call" | custom-call | tf_op jit(solution)/shard_map/back_sums/pallas_call | solution.py:1808
  418.7 0.0 copy-start.3
  418.7 0.0 copy-start.10
  418.7 2.1 shift-right-arithmetic_reduce_fusion
  420.8 0.7 reshape.115.refs_11_
  421.5 1.0 copy.60
  422.5 1.0 copy.61
  423.5 0.8 compare_convert_fusion.refs_2_
  424.2 125.1 %last_sums.1 = (f32[32,1024]{1,0:T(8,128)}, f32[32,1024]{1,0:T(8,128)}, f32[32,1024]{1,0:T(8,128)}, f32[32,1024]{1,0:T(8,128)}, f32[16,1024]{1,0:T(8,128)}, /*in...) custom-call(bf16[16,64,256]{2,1,0:T(8,128)(2,1)} %bitcast.28, ...), custom_call_target="tpu_custom_call" | custom-call | tf_op jit(solution)/shard_map/last_sums/pallas_call | solution.py:1354
  549.3 12.8 %finish.1 = (f32[1954,1024]{1,0:T(8,128)}, s32[1954,1]{1,0:T(8,128)}, f32[32,1024]{1,0:T(8,128)}, f32[32,1024]{1,0:T(8,128)}, f32[32,1024]{1,0:T(8,128)}, /*inde...) custom-call(s32[1,768]{1,0:T(1,128)} %get-tuple-element.131.rows, ...), custom_call_target="tpu_custom_call" | custom-call | tf_op jit(solution)/shard_map/finish/pallas_call | solution.py:1861
  562.1 2.2 reduce.1
  564.3 0.7 constant_dynamic-slice_fusion
  565.1 0.5 slice_bitcast_fusion
  565.6 0.8 copy.66
  566.4 0.7 copy.67
  567.1 0.8 copy.68
  (21 shorter events, 0.0 us)
Async XLA Ops:
  1.5 5.2 copy-start.1
  247.4 2.7 copy-start.6
  247.4 3.7 copy-start.5
  247.5 4.7 copy-start.8
  247.5 5.5 copy-start.7
  253.8 167.7 %copy-start.4 = (bf16[256,1024]{1,0:T(8,128)(2,1)S(1)}, bf16[256,1024]{1,0:T(8,128)(2,1)}, u32[]{:S(2)}) copy-start(bf16[256,1024]{1,0:T(8,128)(2,1)} %get-tuple-element.123) | copy-start | bytes 1572868
  418.7 3.8 copy-start.3
  418.7 4.8 copy-start.10
  549.3 16.3 %copy-start.2 = (bf16[256,1024]{1,0:T(8,128)(2,1)S(1)}, bf16[256,1024]{1,0:T(8,128)(2,1)}, u32[]{:S(2)}) copy-start(bf16[256,1024]{1,0:T(8,128)(2,1)} %get-tuple-element.187) | copy-start | bytes 1572868
  562.1 4.3 copy-start.9
  562.1 5.0 copy-start

commit v6 on v5

--- a/solution.py
+++ b/solution.py
@@ -1017,7 +1017,7 @@
     return results[:count], results[count], results[count + 1], Kept(*results[count + 2 :])
 
 
-LAGS = (2, 3, 5)
+LAGS = (1, 2, 4)
 
 
 class GradSums:
@@ -1847,7 +1847,7 @@
 
 def finish(table_grad, counts, stacked, rows, wholes, cuts, halves):
     rows_dev, width = table_grad.shape
-    block = 256
+    block = 512
     one = jax.ShapeDtypeStruct
 
     def whole(shape):

time: 577 us -> 576 us (level)
  no operation moved by 1% of the time
where the time goes in v6:
time: 576 us; the launch traced here: 567 us
  Pallas kernels  542 us (94%)
  local copies, waits for them, and re-layouts  16.4 us (3%)
  other arithmetic  7.18 us (1%)
    pallas_call x1, Pallas kernels, fetch(): pl.pallas_call(functools.partial(fetch_kernel, n, count, steps_of, tokens...  241 us
    pallas_call x1, Pallas kernels, back_sums(): pl.pallas_call(functools.partial(back_kernel, n, units, pool_count), out_...  165 us
    pallas_call x1, Pallas kernels, last_sums(): pl.pallas_call(functools.partial(last_kernel, n, units, len(lefts), len(r...  125 us

profile of v6, /device:TPU:0, one launch (start us, length us, event | category | flops | bytes accessed | tf_op | source)
XLA Modules:
  0.0 566.9 jit_solution(8773096569748208727)
XLA Ops:
  0.7 0.7 copy.52
  1.4 0.1 broadcast_in_dim.28.refs_17_.refs_30_
  1.5 0.6 sub.3.refs_16_.refs_29_
  2.1 0.1 pad.4.clone
  2.2 1.4 maximum_maximum_fusion.refs_15_.refs_28_
  3.6 0.8 copy.51
  4.4 0.1 reshape.105
  4.6 0.6 concatenate.6.refs_11_
  5.2 1.5 copy.54.refs_13_
  6.7 0.0 copy-done.1
  6.7 240.8 %fetch.1 = (bf16[1024,1024]{1,0:T(8,128)(2,1)}, bf16[1024,1024]{1,0:T(8,128)(2,1)}, bf16[1024,1024]{1,0:T(8,128)(2,1)}, bf16[1024,1024]{1,0:T(8,128)(2,1)}, bf16...) custom-call(bf16[256,1024]{1,0:T(8,128)(2,1)} %refs_0_.1, ...), custom_call_target="tpu_custom_call" | custom-call | tf_op jit(solution)/shard_map/fetch/pallas_call | solution.py:972
  247.5 2.6 copy.56
  250.1 0.0 copy-done.6
  250.1 1.0 copy.58
  251.1 1.0 copy.55
  252.1 0.8 copy.57
  253.0 0.8 copy.59
  253.8 164.9 %back_sums.1 = (f32[32,1024]{1,0:T(8,128)}, f32[32,1024]{1,0:T(8,128)}, f32[32,1024]{1,0:T(8,128)}, f32[32,1024]{1,0:T(8,128)}, f32[96,1024]{1,0:T(8,128)}, /*in...) custom-call(bf16[16,64,256]{2,1,0:T(8,128)(2,1)} %bitcast.27, ...), custom_call_target="tpu_custom_call" | custom-call | tf_op jit(solution)/shard_map/back_sums/pallas_call | solution.py:1808
  418.7 0.0 copy-start.10
  418.7 2.1 shift-right-arithmetic_reduce_fusion
  420.8 0.7 reshape.115.refs_11_
  421.5 1.0 copy.60
  422.5 1.0 copy.61
  423.5 0.8 compare_convert_fusion.refs_2_
  424.2 125.1 %last_sums.1 = (f32[32,1024]{1,0:T(8,128)}, f32[32,1024]{1,0:T(8,128)}, f32[32,1024]{1,0:T(8,128)}, f32[32,1024]{1,0:T(8,128)}, f32[16,1024]{1,0:T(8,128)}, /*in...) custom-call(bf16[16,64,256]{2,1,0:T(8,128)(2,1)} %bitcast.28, ...), custom_call_target="tpu_custom_call" | custom-call | tf_op jit(solution)/shard_map/last_sums/pallas_call | solution.py:1354
  549.3 11.3 %finish.1 = (f32[1954,1024]{1,0:T(8,128)}, s32[1954,1]{1,0:T(8,128)}, f32[32,1024]{1,0:T(8,128)}, f32[32,1024]{1,0:T(8,128)}, f32[32,1024]{1,0:T(8,128)}, /*inde...) custom-call(s32[1,768]{1,0:T(1,128)} %get-tuple-element.131.rows, ...), custom_call_target="tpu_custom_call" | custom-call | tf_op jit(solution)/shard_map/finish/pallas_call | solution.py:1861
  560.7 2.2 reduce.1
  562.9 0.7 constant_dynamic-slice_fusion
  563.6 0.5 slice_bitcast_fusion
  564.2 0.8 copy.66
  565.0 0.7 copy.67
  565.6 0.8 copy.68
  (21 shorter events, 0.0 us)
Async XLA Ops:
  1.5 5.2 copy-start.1
  247.4 2.7 copy-start.6
  247.4 3.7 copy-start.5
  247.5 4.7 copy-start.8
  247.5 5.5 copy-start.7
  253.8 167.7 %copy-start.4 = (bf16[256,1024]{1,0:T(8,128)(2,1)S(1)}, bf16[256,1024]{1,0:T(8,128)(2,1)}, u32[]{:S(2)}) copy-start(bf16[256,1024]{1,0:T(8,128)(2,1)} %get-tuple-element.123) | copy-start | bytes 1572868
  418.7 3.8 copy-start.3
  418.7 4.8 copy-start.10
  549.3 14.9 %copy-start.2 = (bf16[256,1024]{1,0:T(8,128)(2,1)S(1)}, bf16[256,1024]{1,0:T(8,128)(2,1)}, u32[]{:S(2)}) copy-start(bf16[256,1024]{1,0:T(8,128)(2,1)} %get-tuple-element.187) | copy-start | bytes 1572868
  560.7 4.3 copy-start.9
  560.7 5.0 copy-start
